TPU v7x, 32 devices: a whole 2x2x4 slice. The times are simulated.
32 devices in a mesh: dp: 32 (over z, y, x, core).
Axes of the slice: x: 2, y: 2, z: 4, core: 2. Of those that a mesh axis runs over, the one named last changes fastest.
Arguments:
- visible: bfloat16 [16384, 768], P('dp'), may hold values from -6 to 6
- embed_weight: bfloat16 [768, 512], replicated, may hold values from -0.21875 to 0.21875
- embed_bias: float32 [512], replicated, may hold values from -3 to 3
- mask_token: float32 [512], replicated, may hold values from -5 to 5
- pos_embed: float32 [512, 512], replicated, may hold values from -1 to 1
- norm1_gain: float32 [512], replicated, may hold values from 0.5 to 1.5
- qkv_weight: bfloat16 [512, 1536], replicated, may hold values from -0.25 to 0.25
- rel_table: float32 [16, 49], replicated, may hold values from -4 to 4
- out_weight: bfloat16 [512, 512], replicated, may hold values from -0.75 to 0.75
- out_bias: float32 [512], replicated, may hold values from -3 to 3
- norm2_gain: float32 [512], replicated, may hold values from 0.5 to 1.5
- up_weight: bfloat16 [512, 2048], replicated, may hold values from -0.25 to 0.25
- up_bias: float32 [2048], replicated, may hold values from -3 to 3
- down_weight: bfloat16 [2048, 512], replicated, may hold values from -0.125 to 0.125
- down_bias: float32 [512], replicated, may hold values from -3 to 3
- cotangent: bfloat16 [65536, 512], P('dp'), may hold values from -6 to 6
- visible_index: int32 [32, 32, 16], P('dp'), may hold values from 0 to 2047, as said below
- slot_counts: int32 [32, 32], P('dp'), may hold values from 8 to 16, as said below
- segment_ids: int32 [8192], replicated, may hold values from 1 to 96, as said below
Outputs:
- out: bfloat16 [65536, 512], P('dp')
- grad_visible: bfloat16 [16384, 768], P('dp')
- grad_embed_weight: float32 [768, 512], replicated
- grad_embed_bias: float32 [512], replicated
- grad_mask_token: float32 [512], replicated
- grad_norm1_gain: float32 [512], replicated
- grad_qkv_weight: float32 [512, 1536], replicated
- grad_rel_table: float32 [16, 49], replicated
- grad_out_weight: float32 [512, 512], replicated
- grad_out_bias: float32 [512], replicated
- grad_norm2_gain: float32 [512], replicated
- grad_up_weight: float32 [512, 2048], replicated
- grad_up_bias: float32 [2048], replicated
- grad_down_weight: float32 [2048, 512], replicated
- grad_down_bias: float32 [512], replicated
Inputs may be any that keep to these rules, and one draw needn't show every extreme that they name: For each slab d the 512 entries visible_index[d] are distinct token positions of that slab; entry [d, s, k] is used only where k < slot_counts[d, s]. slot_counts[d, s] rows go from device s to slab d; every slab receives 16 rows from its own device. `segment_ids`: frames with equal ids form one clip of one or more whole position grids; clips start only at multiples of 64 frames that are not multiples of 256; the time axis is a cycle, so the last clip continues into frame 0.
All inputs are finite; a program needn't handle non-finite values.
Results may differ from a plain program's by a relative error of at most 0.013.
Values may be sent and summed in bfloat16 or wider, within the bound.
No kernel may reach another device: no remote copies, remote signals or barrier semaphores. Data moves between devices by JAX's collectives and lax.ppermute only.
A program may use at most 256 MiB of HBM per device.

v0:
```python
from functools import partial

import jax
import jax.numpy as jnp
from jax import lax
from jax.sharding import PartitionSpec as P

HEADS = 16
BANDS = 8
GRID_FR = 64
WIN = 4
SHIFT = 2


EPSILON = 1e-06
MASKED = -1e30
PRECISE = lax.Precision.HIGHEST


def shifted_2(x, axis, by):
    devices = lax.axis_size(axis)
    return lax.ppermute(x, axis, [(i, (i + by) % devices) for i in range(devices)])


def layer_norm(inputs, norm_gain):
    row_mean = jnp.mean(inputs, axis=-1, keepdims=True)
    centred = inputs - row_mean
    row_var = jnp.mean(centred * centred, axis=-1, keepdims=True)
    return centred * lax.rsqrt(row_var + EPSILON) * norm_gain


def relative_onehot():
    spots = jnp.arange(WIN * WIN)
    frame_off = spots // WIN
    band_off = spots % WIN
    rel_index = (frame_off[:, None] - frame_off[None, :] + WIN - 1) * (2 * WIN - 1) + (
        band_off[:, None] - band_off[None, :] + WIN - 1
    )
    return (rel_index[:, :, None] == jnp.arange((2 * WIN - 1) ** 2)[None, None, :]).astype(
        jnp.float32
    )


def split_windows(tape_rows, frames, head_count):
    model_width = tape_rows.shape[-1]
    blocks = tape_rows.reshape(
        frames // WIN, WIN, BANDS // WIN, WIN, head_count, model_width // head_count
    )
    return blocks.transpose(0, 2, 4, 1, 3, 5).reshape(
        frames // WIN, BANDS // WIN, head_count, WIN * WIN, model_width // head_count
    )


def join_windows(windows, frames):
    head_count = windows.shape[2]
    head_size = windows.shape[4]
    blocks = windows.reshape(frames // WIN, BANDS // WIN, head_count, WIN, WIN, head_size)
    return blocks.transpose(0, 3, 1, 4, 2, 5).reshape(frames * BANDS, head_count * head_size)


def clip_mask(seg_tape, frames):
    per_frame = seg_tape.reshape(frames // WIN, WIN)
    per_token = jnp.repeat(per_frame, WIN, axis=1)
    return per_token[:, :, None] == per_token[:, None, :]


def window_scores(queries, keys_win, pos_bias, same_clip, score_scale):
    raw_scores = (
        jnp.einsum("abhid,abhjd->abhij", queries, keys_win, preferred_element_type=jnp.float32)
        * score_scale
    )
    return jnp.where(same_clip[:, None, None], raw_scores + pos_bias, MASKED)


def per_device(
    visible,
    embed_weight,
    embed_bias,
    mask_token,
    pos_embed,
    norm1_gain,
    qkv_weight,
    rel_table,
    out_weight,
    out_bias,
    norm2_gain,
    up_weight,
    up_bias,
    down_weight,
    down_bias,
    cotangent,
    visible_index,
    slot_counts,
    segment_ids,
):
    device_count = lax.axis_size("dp")
    device_rank = lax.axis_index("dp")
    tok_rows = cotangent.shape[0]
    frames = tok_rows // BANDS
    model_width = qkv_weight.shape[0]
    slot_rows = visible_index.shape[2]
    recv_rows = device_count * slot_rows
    rim_rows = SHIFT * BANDS
    score_scale = (model_width // HEADS) ** (-0.5)
    arrived = lax.all_to_all(visible, "dp", split_axis=0, concat_axis=0, tiled=True)
    embedded = (
        jnp.dot(arrived, embed_weight, preferred_element_type=jnp.float32) + embed_bias
    ).astype(jnp.bfloat16)
    places = visible_index.reshape(recv_rows)
    live_slot = (jnp.arange(slot_rows)[None, :] < slot_counts.reshape(device_count, 1)).reshape(
        recv_rows
    )
    onehot = ((jnp.arange(tok_rows)[:, None] == places[None, :]) & live_slot[None, :]).astype(
        jnp.bfloat16
    )
    seen_mask = jnp.sum(onehot.astype(jnp.float32), axis=1)
    hidden_share = 1.0 - seen_mask
    positions = jnp.tile(pos_embed, (frames // GRID_FR, 1))
    start = (
        jnp.dot(onehot, embedded, preferred_element_type=jnp.float32)
        + hidden_share[:, None] * mask_token
        + positions
    )
    h_one = layer_norm(start, norm1_gain).astype(jnp.bfloat16)
    qkv = jnp.dot(h_one, qkv_weight, preferred_element_type=jnp.float32).astype(jnp.bfloat16)
    incoming = shifted_2(qkv[:rim_rows], "dp", -1)
    shifted = jnp.concatenate([qkv[rim_rows:], incoming], axis=0)
    seg_cycle = jnp.concatenate([segment_ids, segment_ids[:SHIFT]])
    seg_tape = lax.dynamic_slice_in_dim(seg_cycle, device_rank * frames + SHIFT, frames)
    same_clip = clip_mask(seg_tape, frames)
    relhot = relative_onehot()
    pos_bias = jnp.einsum("hr,ijr->hij", rel_table, relhot, precision=PRECISE)
    queries = split_windows(shifted[:, :model_width], frames, HEADS)
    keys_win = split_windows(shifted[:, model_width : 2 * model_width], frames, HEADS)
    values_win = split_windows(shifted[:, 2 * model_width :], frames, HEADS)
    scores = window_scores(queries, keys_win, pos_bias, same_clip, score_scale)
    row_top = jnp.max(scores, axis=-1, keepdims=True)
    expd = jnp.exp(scores - row_top)
    totals = jnp.sum(expd, axis=-1, keepdims=True)
    probs = expd / totals
    log_total = row_top + jnp.log(totals)
    context_win = jnp.einsum(
        "abhij,abhjd->abhid",
        probs.astype(jnp.bfloat16),
        values_win,
        preferred_element_type=jnp.float32,
    ).astype(jnp.bfloat16)
    context_tape = join_windows(context_win, frames)
    sent_back = shifted_2(context_tape[tok_rows - rim_rows :], "dp", 1)
    context = jnp.concatenate([sent_back, context_tape[: tok_rows - rim_rows]], axis=0)
    middle = start + jnp.dot(context, out_weight, preferred_element_type=jnp.float32) + out_bias
    h_two = layer_norm(middle, norm2_gain).astype(jnp.bfloat16)
    up_value = jnp.dot(h_two, up_weight, preferred_element_type=jnp.float32) + up_bias
    activated = jax.nn.gelu(up_value, approximate=False).astype(jnp.bfloat16)
    result = (
        middle + jnp.dot(activated, down_weight, preferred_element_type=jnp.float32) + down_bias
    )
    grad_result = cotangent.astype(jnp.float32)
    grad_down_weight = jnp.einsum(
        "rf,rd->fd", activated, cotangent, preferred_element_type=jnp.float32
    )
    grad_down_bias = jnp.sum(grad_result, axis=0)
    grad_act = jnp.einsum("rd,fd->rf", cotangent, down_weight, preferred_element_type=jnp.float32)
    gelu_pull = jax.vjp(partial(jax.nn.gelu, approximate=False), up_value)[1]
    grad_up = gelu_pull(grad_act)[0]
    grad_up_bias = jnp.sum(grad_up, axis=0)
    grad_up_low = grad_up.astype(jnp.bfloat16)
    grad_up_weight = jnp.einsum("rd,rf->df", h_two, grad_up_low, preferred_element_type=jnp.float32)
    grad_h_two = jnp.einsum("rf,df->rd", grad_up_low, up_weight, preferred_element_type=jnp.float32)
    norm_pull_two = jax.vjp(layer_norm, middle, norm2_gain)[1]
    grad_middle_norm, grad_norm2_gain = norm_pull_two(grad_h_two)
    grad_middle = grad_result + grad_middle_norm
    grad_out_bias = jnp.sum(grad_middle, axis=0)
    grad_middle_low = grad_middle.astype(jnp.bfloat16)
    grad_out_weight = jnp.einsum(
        "rc,rd->cd", context, grad_middle_low, preferred_element_type=jnp.float32
    )
    grad_context = jnp.einsum(
        "rd,cd->rc", grad_middle_low, out_weight, preferred_element_type=jnp.float32
    ).astype(jnp.bfloat16)
    grad_incoming = shifted_2(grad_context[:rim_rows], "dp", -1)
    grad_tape = jnp.concatenate([grad_context[rim_rows:], grad_incoming], axis=0)
    grad_windows = split_windows(grad_tape, frames, HEADS)
    again = window_scores(queries, keys_win, pos_bias, same_clip, score_scale)
    probs_again = jnp.exp(again - log_total)
    grad_probs = jnp.einsum(
        "abhid,abhjd->abhij", grad_windows, values_win, preferred_element_type=jnp.float32
    )
    row_delta = jnp.sum(grad_probs * probs_again, axis=-1, keepdims=True)
    grad_scores = probs_again * (grad_probs - row_delta)
    grad_rel_table = jnp.einsum(
        "hij,ijr->hr", jnp.sum(grad_scores, axis=(0, 1)), relhot, precision=PRECISE
    )
    grad_scores_low = grad_scores.astype(jnp.bfloat16)
    grad_query = (
        jnp.einsum(
            "abhij,abhjd->abhid", grad_scores_low, keys_win, preferred_element_type=jnp.float32
        )
        * score_scale
    )
    grad_key = (
        jnp.einsum(
            "abhij,abhid->abhjd", grad_scores_low, queries, preferred_element_type=jnp.float32
        )
        * score_scale
    )
    grad_value = jnp.einsum(
        "abhij,abhid->abhjd",
        probs_again.astype(jnp.bfloat16),
        grad_windows,
        preferred_element_type=jnp.float32,
    )
    grad_qkv_tape = jnp.concatenate(
        [
            join_windows(grad_query, frames),
            join_windows(grad_key, frames),
            join_windows(grad_value, frames),
        ],
        axis=1,
    ).astype(jnp.bfloat16)
    back_rim = shifted_2(grad_qkv_tape[tok_rows - rim_rows :], "dp", 1)
    grad_qkv = jnp.concatenate([back_rim, grad_qkv_tape[: tok_rows - rim_rows]], axis=0)
    grad_qkv_weight = jnp.einsum("rd,rc->dc", h_one, grad_qkv, preferred_element_type=jnp.float32)
    grad_h_one = jnp.einsum("rc,dc->rd", grad_qkv, qkv_weight, preferred_element_type=jnp.float32)
    norm_pull_one = jax.vjp(layer_norm, start, norm1_gain)[1]
    grad_start_norm, grad_norm1_gain = norm_pull_one(grad_h_one)
    grad_start = grad_middle + grad_start_norm
    grad_mask_token = jnp.sum(hidden_share[:, None] * grad_start, axis=0)
    grad_embedded = jnp.einsum(
        "rv,rd->vd", onehot, grad_start.astype(jnp.bfloat16), preferred_element_type=jnp.float32
    ).astype(jnp.bfloat16)
    grad_embed_weight = jnp.einsum(
        "ve,vd->ed", arrived, grad_embedded, preferred_element_type=jnp.float32
    )
    grad_embed_bias = jnp.sum(grad_embedded.astype(jnp.float32), axis=0)
    grad_arrived = jnp.einsum(
        "vd,ed->ve", grad_embedded, embed_weight, preferred_element_type=jnp.float32
    ).astype(jnp.bfloat16)
    grad_visible = lax.all_to_all(grad_arrived, "dp", split_axis=0, concat_axis=0, tiled=True)
    summed = lax.psum(
        (
            grad_embed_weight,
            grad_embed_bias,
            grad_mask_token,
            grad_norm1_gain,
            grad_qkv_weight,
            grad_rel_table,
            grad_out_weight,
            grad_out_bias,
            grad_norm2_gain,
            grad_up_weight,
            grad_up_bias,
            grad_down_weight,
            grad_down_bias,
        ),
        "dp",
    )
    return (
        result.astype(jnp.bfloat16),
        grad_visible,
        summed[0],
        summed[1],
        summed[2],
        summed[3],
        summed[4],
        summed[5],
        summed[6],
        summed[7],
        summed[8],
        summed[9],
        summed[10],
        summed[11],
        summed[12],
    )


def solution(mesh):
    in_specs = (
        P("dp", None),
        P(),
        P(),
        P(),
        P(),
        P(),
        P(),
        P(),
        P(),
        P(),
        P(),
        P(),
        P(),
        P(),
        P(),
        P("dp", None),
        P("dp", None, None),
        P("dp", None),
        P(),
    )
    out_specs = (
        P("dp", None),
        P("dp", None),
        P(),
        P(),
        P(),
        P(),
        P(),
        P(),
        P(),
        P(),
        P(),
        P(),
        P(),
        P(),
        P(),
    )
    return jax.shard_map(
        per_device, mesh=mesh, in_specs=in_specs, out_specs=out_specs, check_vma=False
    )
```

profile of v0, /device:TPU:0, one launch (start us, length us, event | category | flops | bytes accessed | tf_op | source)
XLA Modules:
  0.0 760.8 jit_solution(1580427478692935342)
XLA Ops:
  24.2 11.1 %all-to-all-done = bf16[32,16,768]{2,1,0:T(8,128)(2,1)} async-done(((bf16[32,16,768]{2,1,0:T(8,128)(2,1)}), bf16[32,16,768]{2,1,0:T(8,128)(2,1)}, u32[]{:S(2)}, u32[]{:S(2)}) %all-to-all-start) | async-done | bytes 786464 | tf_op jit(solution)/shard_map/all_to_all | solution.py:105
  66.3 10.3 %reshape.294 = bf16[64,4,2,4,16,32]{5,4,3,2,1,0:T(8,128)(2,1)} reshape(bf16[2048,512]{1,0:T(8,128)(2,1)} %get-tuple-element.101) | data formatting | bytes 4194304 | tf_op jit(solution)/shard_map/reshape | solution.py:46
  84.9 10.3 %reshape.296 = bf16[64,4,2,4,16,32]{5,4,3,2,1,0:T(8,128)(2,1)} reshape(bf16[2048,512]{1,0:T(8,128)(2,1)} %get-tuple-element.100) | data formatting | bytes 4194304 | tf_op jit(solution)/shard_map/reshape | solution.py:46
  103.5 10.3 %reshape.298 = bf16[64,4,2,4,16,32]{5,4,3,2,1,0:T(8,128)(2,1)} reshape(bf16[2048,512]{1,0:T(8,128)(2,1)} %get-tuple-element.102) | data formatting | bytes 4194304 | tf_op jit(solution)/shard_map/reshape | solution.py:46
  122.0 12.1 %fusion.66 = (f32[64,2,16,16]{3,2,1,0:T(8,128)S(1)}, f32[64,2,16,16,16]{3,4,2,1,0:T(8,128)}) fusion(f32[16,16,16]{1,2,0:T(8,128)S(1)} %copy.106, bf16[64,2,16,16,32]{4,3,2,1,0:T(8,128)(2,1)} %bitcast.82, bf16[64,2,16,16,32]{4,3,2,1,0:T(8,128)(2,1)} %bitcast.86, pred[64,16,16]{1,2,0:T(8,128)(4,1)S(1)} %broadcast_compare_fusion), kind=kOutput, calls=%fused_computation.136 | convolution fusion | flops 35618816 | bytes 6455296 | tf_op jit(solution)/shard_map/abhid,abhjd->abhij/dot_general | solution.py:69
  134.1 9.9 %fusion.6 = f32[64,2,16,16]{3,2,1,0:T(8,128)} fusion(f32[64,2,16,16,16]{3,4,2,1,0:T(8,128)} %get-tuple-element.108, f32[64,2,16,16]{3,2,1,0:T(8,128)S(1)} %get-tuple-element.107), kind=kLoop, calls=%fused_computation.25 | loop fusion | flops 1015808 | bytes 2359296 | tf_op jit(solution)/shard_map/reduce_sum | solution.py:139
  144.0 14.3 %fusion.12 = bf16[64,2,16,16,32]{4,3,2,1,0:T(8,128)(2,1)} fusion(bf16[64,2,16,16,32]{4,3,2,1,0:T(8,128)(2,1)} %bitcast.90, f32[64,2,16,16,16]{3,4,2,1,0:T(8,128)} %get-tuple-element.108, f32[64,2,16,16]{3,2,1,0:T(8,128)} %fusion.6, f32[64,2,16,16]{3,2,1,0:T(8,128)S(1)} %get-tuple-element.107), kind=kOutput, calls=%fused_computation.37 | convolution fusion | flops 36175872 | bytes 6553600 | tf_op jit(solution)/shard_map/abhij,abhjd->abhid/dot_general | solution.py:142
  158.3 10.5 %copy.137 = bf16[64,2,16,4,4,32]{5,2,4,1,3,0:T(8,128)(2,1)} copy(bf16[64,2,16,4,4,32]{5,4,3,2,1,0:T(4,128)(2,1)} %bitcast.102) | data formatting | bytes 4194304 | tf_op jit(solution)/shard_map/reshape | solution.py:57
  168.8 12.0 %reshape.301 = bf16[2048,512]{1,0:T(8,128)(2,1)} reshape(bf16[64,4,2,4,16,32]{5,4,3,2,1,0:T(8,128)(2,1)} %bitcast.96) | data formatting | bytes 4194304 | tf_op jit(solution)/shard_map/reshape | solution.py:58
  191.5 43.9 %multiply_convert_fusion.2 = (bf16[2048,2048]{1,0:T(8,128)(2,1)}, f32[2048,2048]{1,0:T(8,128)}, f32[2048,2048]{1,0:T(8,128)}) fusion(f32[2048]{0:T(1024)S(1)} %copy-done.51, bf16[512,2048]{1,0:T(8,128)(2,1)S(1)} %copy-done, f32[2048,512]{0,1:T(8,128)S(1)} %get-tuple-element.110, f32[512]{0:T(512)S(1)} %copy-done.40, f32[2048]{0:T(1024)S(1)} %fusion.53, ...), kind=kOutput, calls=%fused_computation.8 | convolution fusion | flops 4575985664 | bytes 48261120 | tf_op jit(solution)/shard_map/dot_general | solution.py:153
  235.4 22.3 %fusion.68 = (f32[2048]{0:T(1024)}, bf16[2048,2048]{1,0:T(8,128)(2,1)}) fusion(f32[2048,2048]{1,0:T(8,128)} %get-tuple-element.99, bf16[2048,512]{1,0:T(8,128)(2,1)} %param.34, bf16[2048,512]{1,0:T(8,128)(2,1)} %param.32, f32[2048,2048]{1,0:T(8,128)} %get-tuple-element.111, f32[2048]{0:T(1024)S(1)} %copy-done.51), kind=kOutput, calls=%fused_computation.138 | convolution fusion | flops 4362074112 | bytes 46153728 | tf_op jit(solution)/shard_map/rd,fd->rf/dot_general | solution.py:163
  304.8 13.1 %fusion.13 = bf16[64,2,16,16,32]{4,3,2,1,0:T(8,128)(2,1)} fusion(bf16[64,2,16,16,32]{4,3,2,1,0:T(8,128)(2,1)} %bitcast.84, f32[64,2,16,16,16]{3,4,2,1,0:T(8,128)} %get-tuple-element.108, f32[64,2,16,16]{3,2,1,0:T(8,128)S(1)} %copy-done.9), kind=kOutput, calls=%fused_computation.38 | convolution fusion | flops 35651584 | bytes 6422528 | tf_op jit(solution)/shard_map/abhij,abhid->abhjd/dot_general | solution.py:207
  317.8 19.2 %multiply_reduce_fusion = (f32[64,2,16,16]{3,2,1,0:T(8,128)S(1)}, f32[64,2,16,16,16]{3,4,2,1,0:T(8,128)}) fusion(f32[64,2,16,16,16]{3,4,2,1,0:T(8,128)} %get-tuple-element.108, f32[64,2,16,16]{3,2,1,0:T(8,128)S(1)} %copy-done.9, bf16[64,2,16,16,32]{4,3,2,1,0:T(8,128)(2,1)} %bitcast.85, bf16[64,2,16,16,32]{4,3,2,1,0:T(8,128)(2,1)} %bitcast.91), kind=kOutput, calls=%fused_computation.5 | convolution fusion | flops 35094528 | bytes 8650752 | tf_op jit(solution)/shard_map/abhid,abhjd->abhij/dot_general | solution.py:186
  337.0 15.7 %fusion.62 = (f32[16,16,16]{1,2,0:T(8,128)S(1)}, bf16[64,2,16,16,16]{3,4,2,1,0:T(8,128)(2,1)}) fusion(f32[64,2,16,16,16]{3,4,2,1,0:T(8,128)} %get-tuple-element.115, f32[64,2,16,16]{3,2,1,0:T(8,128)S(1)} %get-tuple-element.114, f32[64,2,16,16,16]{3,4,2,1,0:T(8,128)} %get-tuple-element.108, f32[64,2,16,16]{3,2,1,0:T(8,128)S(1)} %copy-done.9), kind=kLoop, calls=%fused_computation.133 | loop fusion | flops 2617344 | bytes 5521408 | tf_op jit(solution)/shard_map/reduce_sum | solution.py:192
  352.8 13.5 %multiply_convert_fusion = bf16[64,2,16,16,32]{4,3,2,1,0:T(8,128)(2,1)} fusion(bf16[64,2,16,16,32]{4,3,2,1,0:T(8,128)(2,1)} %bitcast.83, bf16[64,2,16,16,16]{3,4,2,1,0:T(8,128)(2,1)} %get-tuple-element.95), kind=kOutput, calls=%fused_computation.2 | convolution fusion | flops 35651584 | bytes 5242880 | tf_op jit(solution)/shard_map/abhij,abhid->abhjd/dot_general | solution.py:202
  375.7 10.5 %copy.134 = bf16[64,2,16,4,4,32]{5,2,4,1,3,0:T(8,128)(2,1)} copy(bf16[64,2,16,4,4,32]{5,4,3,2,1,0:T(4,128)(2,1)} %bitcast.89) | data formatting | bytes 4194304 | tf_op jit(solution)/shard_map/reshape | solution.py:57
  386.3 11.1 %reshape.309 = bf16[2048,512]{1,0:T(8,128)(2,1)S(1)} reshape(bf16[64,4,2,4,16,32]{5,4,3,2,1,0:T(8,128)(2,1)} %bitcast.98) | data formatting | bytes 4194304 | tf_op jit(solution)/shard_map/reshape | solution.py:58
  397.4 10.5 %copy.135 = bf16[64,2,16,4,4,32]{5,2,4,1,3,0:T(8,128)(2,1)} copy(bf16[64,2,16,4,4,32]{5,4,3,2,1,0:T(4,128)(2,1)} %bitcast.88) | data formatting | bytes 4194304 | tf_op jit(solution)/shard_map/reshape | solution.py:57
  407.9 12.0 %reshape.307 = bf16[2048,512]{1,0:T(8,128)(2,1)} reshape(bf16[64,4,2,4,16,32]{5,4,3,2,1,0:T(8,128)(2,1)} %bitcast.99) | data formatting | bytes 4194304 | tf_op jit(solution)/shard_map/reshape | solution.py:58
  419.9 10.5 %copy.136 = bf16[64,2,16,4,4,32]{5,2,4,1,3,0:T(8,128)(2,1)} copy(bf16[64,2,16,4,4,32]{5,4,3,2,1,0:T(4,128)(2,1)} %bitcast.92) | data formatting | bytes 4194304 | tf_op jit(solution)/shard_map/reshape | solution.py:57
  430.4 12.0 %reshape.305 = bf16[2048,512]{1,0:T(8,128)(2,1)} reshape(bf16[64,4,2,4,16,32]{5,4,3,2,1,0:T(8,128)(2,1)} %bitcast.100) | data formatting | bytes 4194304 | tf_op jit(solution)/shard_map/reshape | solution.py:58
  478.3 11.3 %add_convert_fusion = bf16[2048,512]{0,1:T(8,128)(2,1)} fusion(f32[2048,512]{0,1:T(8,128)} %copy-done.2, bf16[2048,2048]{1,0:T(8,128)(2,1)} %get-tuple-element.98, bf16[2048,512]{1,0:T(8,128)(2,1)} %param.32, f32[512]{0:T(512)S(1)} %copy-done.54), kind=kOutput, calls=%fused_computation.58 | convolution fusion | flops 4298113024 | bytes 16779264 | tf_op jit(solution)/shard_map/dot_general | solution.py:156
  498.5 42.6 %all-reduce = (f32[512]{0:T(512)}, f32[512]{0:T(512)}, f32[512]{0:T(512)}, f32[16,49]{1,0:T(8,128)}, f32[512]{0:T(512)}, /*index=5*/f32[512]{0:T(512)}, f32[2048]{0:T(1024)}, f32[512]{0:T(512)}) all-reduce(f32[512]{0:T(512)S(1)} %get-tuple-element.117, f32[512]{0:T(512)S(1)} %get-tuple-element.80, ...), channel_id=1, replica_groups=mesh['dp'=32] {'dp'}, use_global_device_ids=true, to_apply=%region_14.15 | all-reduce | flops 5904 | bytes 47232 | tf_op jit(solution)/shard_map/psum | solution.py:240
  541.1 197.9 %all-reduce.4.cloned.1.call-done = (f32[768,512]{0,1:T(8,128)}, f32[512,1536]{1,0:T(8,128)}, f32[512,512]{1,0:T(8,128)}, f32[512,2048]{1,0:T(8,128)}, f32[2048,512]{1,0:T(8,128)}) async-done(((f32[768,512]{0,1:T(8,128)}, f32[512,1536]{1,0:T(8,128)}, f32[512,512]{1,0:T(8,128)}, f32[512,2048]{1,0:T(8,128)}, f32[2048,512]{1,0:T(8,128)}), (f32[768,512]{0,1:T(8,128)}, f32[512,1536]{1,0:T(8,128)}, ...) | async-done | bytes 14155792 | tf_op jit(solution)/shard_map/psum | solution.py:240
  (217 shorter events, 198.9 us)
Async XLA Ops:
  7.2 184.3 %copy-start = (bf16[512,2048]{1,0:T(8,128)(2,1)S(1)}, bf16[512,2048]{1,0:T(8,128)(2,1)}, u32[]{:S(2)}) copy-start(bf16[512,2048]{1,0:T(8,128)(2,1)} %param.30) | copy-start | bytes 6291460
  7.2 28.0 %all-to-all-start = ((bf16[32,16,768]{2,1,0:T(8,128)(2,1)}), bf16[32,16,768]{2,1,0:T(8,128)(2,1)}, u32[]{:S(2)}, u32[]{:S(2)}) async-start(bf16[32,16,768]{2,1,0:T(8,128)(2,1)} %bitcast.107), calls=%async_computation | async-start | bytes 1572864 | tf_op jit(solution)/shard_map/all_to_all | solution.py:105
  14.6 724.3 %all-reduce.4.cloned.1.call-start = ((), (), s32[]{:S(2)}) async-start(), calls=%async_computation.2 | async-start | bytes 28311552 | tf_op jit(solution)/shard_map/psum | solution.py:240
  15.5 19.7 %copy-start.42 = (s32[512]{0:T(512)}, s32[512]{0:T(512)S(1)}, u32[]{:S(2)}) copy-start(s32[512]{0:T(512)S(1)} %eq.56) | copy-start | bytes 6148
  16.4 18.9 %copy-start.47 = (pred[512]{0:T(512)(128)(4,1)}, pred[512]{0:T(512)(128)(4,1)S(1)}, u32[]{:S(2)}) copy-start(pred[512]{0:T(512)(128)(4,1)S(1)} %lt.37) | copy-start | bytes 1540
  18.7 16.6 %copy-start.49 = (bf16[768,512]{1,0:T(8,128)(2,1)S(1)}, bf16[768,512]{1,0:T(8,128)(2,1)}, u32[]{:S(2)}) copy-start(bf16[768,512]{1,0:T(8,128)(2,1)} %param.20) | copy-start | bytes 2359300
  18.7 16.6 %copy-start.52 = (f32[512]{0:T(512)S(1)}, f32[512]{0:T(512)}, u32[]{:S(2)}) copy-start(f32[512]{0:T(512)} %param.22) | copy-start | bytes 6148
  18.7 16.6 %copy-start.53 = (f32[512]{0:T(512)S(1)}, f32[512]{0:T(512)}, u32[]{:S(2)}) copy-start(f32[512]{0:T(512)} %param.21) | copy-start | bytes 6148
  23.9 32.5 %copy-start.26 = (s32[16,16]{1,0:T(8,128)}, s32[16,16]{1,0:T(8,128)S(1)}, u32[]{:S(2)}) copy-start(s32[16,16]{1,0:T(8,128)S(1)} %add_add_fusion.6) | copy-start | bytes 3076
  23.9 17.9 %copy-start.31 = (f32[2048]{0:T(1024)}, f32[2048]{0:T(1024)S(1)}, u32[]{:S(2)}) copy-start(f32[2048]{0:T(1024)S(1)} %broadcast_subtract_fusion) | copy-start | bytes 24580
  41.9 8.9 %copy-start.28 = (f32[2048]{0:T(1024)}, f32[2048]{0:T(1024)S(1)}, u32[]{:S(2)}) copy-start(f32[2048]{0:T(1024)S(1)} %broadcast_multiply_fusion.1) | copy-start | bytes 24580
  45.3 11.1 %copy-start.38 = (f32[16,49]{1,0:T(8,128)S(1)}, f32[16,49]{1,0:T(8,128)}, u32[]{:S(2)}) copy-start(f32[16,49]{1,0:T(8,128)} %param.26) | copy-start | bytes 9412
  53.4 7.5 collective-permute-start
  180.8 7.6 %copy-start.44 = (f32[512]{0:T(512)S(1)}, f32[512]{0:T(512)}, u32[]{:S(2)}) copy-start(f32[512]{0:T(512)} %param.28) | copy-start | bytes 6148
  181.7 6.8 collective-permute-start.1
  189.9 45.4 %copy-start.2 = (f32[2048,512]{0,1:T(8,128)}, f32[2048,512]{0,1:T(8,128)S(1)}, u32[]{:S(2)}) copy-start(f32[2048,512]{0,1:T(8,128)S(1)} %get-tuple-element.110) | copy-start | bytes 12582916
  257.7 9.3 %copy-start.25 = (f32[2048]{0:T(1024)S(1)}, f32[2048]{0:T(1024)}, u32[]{:S(2)}) copy-start(f32[2048]{0:T(1024)} %copy-done.24) | copy-start | bytes 24580
  257.7 9.3 %copy-start.3 = (f32[2048,512]{0,1:T(8,128)S(1)}, f32[2048,512]{0,1:T(8,128)}, u32[]{:S(2)}) copy-start(f32[2048,512]{0,1:T(8,128)} %copy-done.2) | copy-start | bytes 12582916
  267.0 9.4 %slice-start.6 = ((s8[8388608]{0:T(1024)(128)(4,1)}), s8[4194304]{0:T(1024)(128)(4,1)S(1)}, s32[]{:S(2)}) async-start(s8[8388608]{0:T(1024)(128)(4,1)} %bitcast.112), calls=%async_computation.9 | async-start | bytes 8388608
  271.6 11.2 %slice-start.4 = ((s8[8388608]{0:T(1024)(128)(4,1)}), s8[4194304]{0:T(1024)(128)(4,1)S(1)}, s32[]{:S(2)}) async-start(s8[8388608]{0:T(1024)(128)(4,1)} %bitcast.110), calls=%async_computation.7 | async-start | bytes 8388608
  273.7 15.5 %collective-permute-start.2 = (bf16[16,512]{1,0:T(8,128)(2,1)S(1)}, bf16[16,512]{1,0:T(8,128)(2,1)S(1)}, u32[]{:S(2)}, u32[]{:S(2)}) collective-permute-start(bf16[16,512]{1,0:T(8,128)(2,1)S(1)} %slice.57), channel_id=1, source_target_pairs={{0,31},{1,0},{2,1},{3,2},{4,3},{5,4},{6,5},{7,6},{8,7},{9,8},{10,9... | collective-permute-start | bytes 49160 | tf_op jit(solution)/shard_map/ppermute | solution.py:22
  296.4 8.4 %copy-start.9 = (f32[64,2,16,16]{3,2,1,0:T(8,128)S(1)}, f32[64,2,16,16]{3,2,1,0:T(8,128)}, u32[]{:S(2)}) copy-start(f32[64,2,16,16]{3,2,1,0:T(8,128)} %log_add_fusion) | copy-start | bytes 393220
  444.9 8.4 %collective-permute-start.3 = (bf16[16,1536]{1,0:T(8,128)(2,1)S(1)}, bf16[16,1536]{1,0:T(8,128)(2,1)S(1)}, u32[]{:S(2)}, u32[]{:S(2)}) collective-permute-start(bf16[16,1536]{1,0:T(8,128)(2,1)S(1)} %slice.58), channel_id=1, source_target_pairs={{0,1},{1,2},{2,3},{3,4},{4,5},{5,6},{6,7},{7,8},{8,9},{9,10},{10,1... | collective-permute-start | bytes 147464 | tf_op jit(solution)/shard_map/ppermute | solution.py:22
  474.7 66.4 %all-to-all-start.1 = ((bf16[32,16,768]{2,1,0:T(8,128)(2,1)}), bf16[32,16,768]{2,1,0:T(8,128)(2,1)S(1)}, u32[]{:S(2)}, u32[]{:S(2)}) async-start(bf16[32,16,768]{2,1,0:T(8,128)(2,1)} %bitcast.22), calls=%async_computation.1 | async-start | bytes 1572864 | tf_op jit(solution)/shard_map/all_to_all | solution.py:239
  (46 other events, 174.5 us)
Sparse Core Ops, SparseCore 0:
  472.2 266.7 all-reduce.3
where the time goes:
time: 770 us; the launch traced here: 761 us
  matrix products  216 us (28%)
  local copies, waits for them, and re-layouts  212 us (28%)
  waiting for transfers between devices  211 us (27%)
  other arithmetic  46.7 us (6%)
  blocking collectives  42.6 us (6%)
  starting transfers between devices  17.2 us (2%)
  between operations  15.2 us (2%)
    psum x1, waiting for transfers between devices, per_device(): lax.psum((grad_embed_weight, grad_embed_bias, grad_mask_token, grad_norm1...  198 us
    reshape x4, local copies, waits for them, and re-layouts, join_windows(): blocks.transpose(0, 3, 1, 4, 2, 5)  47.1 us
    dot_general x1, matrix products, per_device(): jnp.dot(h_two, up_weight, preferred_element_type=jnp.float32) + up_bias  43.9 us
    psum x1, blocking collectives, per_device(): lax.psum((grad_embed_weight, grad_embed_bias, grad_mask_token, grad_norm1...  42.6 us
    reshape x4, local copies, waits for them, and re-layouts, join_windows(): windows.reshape(frames // WIN, BANDS // WIN, head_count, WIN, WIN, head_s...  42.1 us
    unnamed x135, local copies, waits for them, and re-layouts  41.1 us
    reshape x4, local copies, waits for them, and re-layouts, split_windows(): tape_rows.reshape(frames // WIN, WIN, BANDS // WIN, WIN, head_count, mode...  37.8 us
    transpose x4, local copies, waits for them, and re-layouts, split_windows(): blocks.transpose(0, 2, 4, 1, 3, 5)  33.3 us
  transfers between devices with their start and end apart: 7, of which 3 were waited for; matrix products, arithmetic and copies ran while one was open for 8% of the time, Pallas kernels for 0%

commit v1 on v0

v1 whole, which is shorter than its diff:
```python
from functools import partial

import jax
import jax.numpy as jnp
import numpy as np
from jax import lax
from jax.experimental import pallas as pl
from jax.experimental.pallas import tpu as pltpu
from jax.sharding import Mesh, PartitionSpec as P

HEADS = 16
HD = 32
BANDS = 8
WIN = 4
SHIFT = 2
RIM = SHIFT * BANDS
SPOTS = WIN * WIN
OCT = 8
OCT_D = OCT * HD
OCT_S = OCT * SPOTS
RIM_SLOTS = 128
EPSILON = 1e-06
MASKED = -1e30
SCALE = HD ** (-0.5)
PRECISE = lax.Precision.HIGHEST
VMEM_LIMIT = 56 * 2**20
bf16 = jnp.bfloat16
f32 = jnp.float32
AXES = ("z", "p", "c")


def mm(a, b):
    return jnp.dot(a, b, preferred_element_type=f32)


def mm_nt(a, b):
    return lax.dot_general(a, b, (((1,), (1,)), ((), ())), preferred_element_type=f32)


def mm_tn(a, b):
    return lax.dot_general(a, b, (((0,), (0,)), ((), ())), preferred_element_type=f32)


def window_order(x):
    return (
        x.reshape(-1, WIN, BANDS // WIN, WIN, x.shape[-1])
        .transpose(0, 2, 1, 3, 4)
        .reshape(x.shape)
    )


def frame_order(x):
    return (
        x.reshape(-1, BANDS // WIN, WIN, WIN, x.shape[-1])
        .transpose(0, 2, 1, 3, 4)
        .reshape(x.shape)
    )


def window_row(token):
    group, rest = token // (WIN * BANDS), token % (WIN * BANDS)
    frame, band = rest // BANDS, rest % BANDS
    return group * (WIN * BANDS) + (band // WIN) * SPOTS + frame * WIN + band % WIN


def spread(x, block_ones):
    return jnp.concatenate([x] * OCT, axis=0) * block_ones


def own_heads(z):
    lane_head = lax.broadcasted_iota(jnp.int32, (SPOTS, 128), 1) // HD
    halves = []
    per = 128 // HD
    for t in range(OCT_D // 128):
        total = None
        for q in range(per):
            piece = z[(t * per + q) * SPOTS : (t * per + q + 1) * SPOTS, t * 128 : (t + 1) * 128]
            piece = jnp.where(lane_head == q, piece, 0.0)
            total = piece if total is None else total + piece
        halves.append(total)
    return jnp.concatenate(halves, axis=1)


def normalized(x):
    centred = x - jnp.mean(x, axis=-1, keepdims=True)
    inverse = lax.rsqrt(jnp.mean(centred * centred, axis=-1, keepdims=True) + EPSILON)
    return centred * inverse, inverse


def norm_back(grad, n, inverse):
    return inverse * (
        grad
        - jnp.mean(grad, axis=-1, keepdims=True)
        - n * jnp.mean(grad * n, axis=-1, keepdims=True)
    )


def slot_onehot(step, rows, places):
    row = lax.broadcasted_iota(jnp.int32, (rows, places.shape[1]), 0) + step * rows
    return jnp.where(row == places, 1.0, 0.0)


def head_slices(w, o):
    return slice(w * SPOTS, (w + 1) * SPOTS), slice(o * OCT_S, (o + 1) * OCT_S)


def forward_kernel(
    first, cut, arrived, rim, embed_w, embed_b, places, positions, mask_token, gain1, qkv_w, bias,
    across, ones, out_w, out_b, gain2, *rest
):
    start_o, h_one_o, qkv_o, probs_o, context_o, middle_o, h_two_o, slots_s, score_s, context_s = (
        rest[-10:]
    )
    rows, width = start_o.shape
    own = arrived.shape[0]
    step = pl.program_id(0)

    @pl.when(step == 0)
    def _():
        slots_s[0:own, :] = (mm(arrived[...], embed_w[...]) + embed_b[...]).astype(bf16)
        slots_s[own:, :] = (mm(rim[...], embed_w[...]) + embed_b[...]).astype(bf16)

    onehot = slot_onehot(step + first, rows, places[...])
    seen = jnp.sum(onehot, axis=1, keepdims=True)
    start = mm(onehot.astype(bf16), slots_s[...]) + (1.0 - seen) * mask_token[...] + positions[...]
    start_o[...] = start
    h_one = (normalized(start)[0] * gain1[...]).astype(bf16)
    h_one_o[...] = h_one
    qkv_o[...] = mm(h_one, qkv_w[...]).astype(bf16)
    block_ones = ones[...]
    windows = rows // SPOTS
    for w in range(windows):
        cut_w = cut[(step + first) * windows + w]
        for o in range(HEADS // OCT):
            r, s = head_slices(w, o)
            q = qkv_o[r, o * OCT_D : (o + 1) * OCT_D]
            k = qkv_o[r, width + o * OCT_D : width + (o + 1) * OCT_D]
            raw = mm_nt(k, spread(q, block_ones)) * SCALE + bias[:, s]
            score_s[r, s] = raw + cut_w * across[:, s]
    scores = score_s[...].reshape(windows, SPOTS, HEADS * SPOTS)
    expd = jnp.exp(scores - jnp.max(scores, axis=1, keepdims=True))
    probs = expd / jnp.sum(expd, axis=1, keepdims=True)
    probs_o[...] = probs.reshape(rows, HEADS * SPOTS)
    for w in range(windows):
        for o in range(HEADS // OCT):
            r, s = head_slices(w, o)
            v = qkv_o[r, 2 * width + o * OCT_D : 2 * width + (o + 1) * OCT_D]
            context_s[r, o * OCT_D : (o + 1) * OCT_D] = own_heads(mm_tn(probs_o[r, s].astype(bf16), v))
    context = context_s[...].astype(bf16)
    context_o[...] = context
    middle = start + mm(context, out_w[...]) + out_b[...]
    middle_o[...] = middle
    h_two_o[...] = (normalized(middle)[0] * gain2[...]).astype(bf16)


def feed_kernel(
    core, h_two, cotangent, up_w, up_b, down_w, after, act_o, grad_h_o, keep_o, send_o, bias_o,
    down_s, up_s
):
    del after
    step = pl.program_id(0)
    width = h_two.shape[1]
    hidden = down_w.shape[0]

    @pl.when(step == 0)
    def _():
        down_s[...] = jnp.zeros_like(down_s)
        up_s[...] = jnp.zeros_like(up_s)
        bias_o[...] = jnp.zeros_like(bias_o)

    h = h_two[...]
    cot = cotangent[...]
    up_value = mm(h, up_w[...]) + up_b[...]
    below = 0.5 * (1.0 + lax.erf(up_value * (0.5**0.5)))
    act = (up_value * below).astype(bf16)
    act_o[...] = act
    slope = below + up_value * (jnp.exp(-0.5 * up_value * up_value) * 0.3989422804014327)
    grad_up = mm_nt(cot, down_w[...]) * slope
    bias_o[...] += jnp.sum(grad_up, axis=0, keepdims=True)
    grad_low = grad_up.astype(bf16)
    down_s[...] += mm_tn(act, cot)
    up_s[...] += mm_tn(h, grad_low)
    grad_h_o[...] = mm_nt(grad_low, up_w[...])

    def give(down_o, up_o):
        down_o[...] = down_s[...].astype(bf16)
        for block in range(hidden // width):
            at = slice(block * width, (block + 1) * width)
            up_o[at, :] = up_s[:, at].astype(bf16)

    last = step == pl.num_programs(0) - 1

    @pl.when(last & (core[0] == 0))
    def _():
        give(keep_o, send_o)

    @pl.when(last & (core[0] == 1))
    def _():
        give(send_o, keep_o)


def attend_back_kernel(
    core, grad_h_a, grad_h_b, cotangent, middle, context, qkv, probs, h_one, gain2, out_w, ones,
    after, gqkv_o, grad_middle_o, keep_o, send_o, sums_o, rel_o, out_s, qkv_s, score_s,
):
    del after
    step = pl.program_id(0)
    rows, width = middle.shape
    windows = rows // SPOTS

    @pl.when(step == 0)
    def _():
        out_s[...] = jnp.zeros_like(out_s)
        qkv_s[...] = jnp.zeros_like(qkv_s)
        sums_o[...] = jnp.zeros_like(sums_o)
        rel_o[...] = jnp.zeros_like(rel_o)

    cot = cotangent[...].astype(f32)
    grad_h_two = grad_h_a[...] + grad_h_b[...]
    n2, r2 = normalized(middle[...])
    sums_o[0:1, :] += jnp.sum(grad_h_two * n2, axis=0, keepdims=True)
    grad_middle = cot + norm_back(grad_h_two * gain2[...], n2, r2)
    grad_middle_o[...] = grad_middle
    sums_o[1:2, :] += jnp.sum(grad_middle, axis=0, keepdims=True)
    sums_o[2:3, :] += jnp.sum(cot, axis=0, keepdims=True)
    grad_middle_low = grad_middle.astype(bf16)
    out_s[...] += mm_tn(context[...], grad_middle_low)
    grad_context = mm_nt(grad_middle_low, out_w[...]).astype(bf16)
    block_ones = ones[...]
    for w in range(windows):
        for o in range(HEADS // OCT):
            r, s = head_slices(w, o)
            heads = slice(o * OCT_D, (o + 1) * OCT_D)
            v_at = slice(2 * width + o * OCT_D, 2 * width + (o + 1) * OCT_D)
            wide = spread(grad_context[r, heads], block_ones)
            score_s[r, s] = mm_nt(qkv[r, v_at], wide)
            gqkv_o[r, v_at] = mm(probs[r, s].astype(bf16), wide).astype(bf16)
    pr = probs[...].reshape(windows, SPOTS, HEADS * SPOTS)
    grad_probs = score_s[...].reshape(windows, SPOTS, HEADS * SPOTS)
    delta = jnp.sum(grad_probs * pr, axis=1, keepdims=True)
    grad_scores = pr * (grad_probs - delta)
    rel_o[...] += jnp.sum(grad_scores, axis=0)
    score_s[...] = grad_scores.reshape(rows, HEADS * SPOTS)
    for w in range(windows):
        for o in range(HEADS // OCT):
            r, s = head_slices(w, o)
            q_at = slice(o * OCT_D, (o + 1) * OCT_D)
            k_at = slice(width + o * OCT_D, width + (o + 1) * OCT_D)
            low = score_s[r, s].astype(bf16)
            gqkv_o[r, q_at] = (own_heads(mm_tn(low, qkv[r, k_at])) * SCALE).astype(bf16)
            gqkv_o[r, k_at] = (mm(low, spread(qkv[r, q_at], block_ones)) * SCALE).astype(bf16)
    qkv_s[...] += mm_tn(h_one[...], gqkv_o[...])

    def give(low_o, high_o):
        low_o[0:width, :] = qkv_s[:, 0:width].astype(bf16)
        low_o[width : 2 * width, :] = qkv_s[:, width : 2 * width].astype(bf16)
        high_o[0:width, :] = qkv_s[:, 2 * width : 3 * width].astype(bf16)
        high_o[width : 2 * width, :] = out_s[...].astype(bf16)

    last = step == pl.num_programs(0) - 1

    @pl.when(last & (core[0] == 0))
    def _():
        give(keep_o, send_o)

    @pl.when(last & (core[0] == 1))
    def _():
        give(send_o, keep_o)


def scatter_back_kernel(
    core, gqkv, start, grad_middle, places, qkv_w, gain1, arrived, rim, sums, rel, up_bias_a,
    up_bias_b, after_a, after_b, slots_o, keep_o, send_o, slots_s, embed_s, sums_s,
):
    del after_a, after_b
    step = pl.program_id(0)
    rows, width = start.shape
    own, e_in = arrived.shape

    @pl.when(step == 0)
    def _():
        slots_s[...] = jnp.zeros_like(slots_s)
        sums_s[...] = jnp.zeros_like(sums_s)

    grad_h_one = mm_nt(gqkv[...], qkv_w[...])
    n1, r1 = normalized(start[...])
    sums_s[3:4, :] += jnp.sum(grad_h_one * n1, axis=0, keepdims=True)
    grad_start = grad_middle[...] + norm_back(grad_h_one * gain1[...], n1, r1)
    onehot = slot_onehot(step, rows, places[...])
    hidden = 1.0 - jnp.sum(onehot, axis=1, keepdims=True)
    sums_s[4:5, :] += jnp.sum(hidden * grad_start, axis=0, keepdims=True)
    slots_s[...] += mm_tn(onehot.astype(bf16), grad_start.astype(bf16))

    def give(low_o, high_o):
        half = low_o.shape[0]
        low_o[...] = embed_s[0:half, :].astype(bf16)
        left = e_in - half
        high_o[...] = jnp.zeros_like(high_o)
        if left > 0:
            high_o[0:left, :] = embed_s[half:e_in, :].astype(bf16)
        left = max(left, 0)
        high_o[left : left + 16, :] = sums_s[...].astype(bf16)
        high_o[left + 16 : left + 16 + SPOTS, 0 : HEADS * SPOTS] = rel[...].astype(bf16)

    last = step == pl.num_programs(0) - 1

    @pl.when(last)
    def _():
        slots = slots_s[...].astype(bf16)
        slots_o[...] = slots
        embed_s[0:e_in, :] = mm_tn(arrived[...], slots[0:own]) + mm_tn(rim[...], slots[own:])
        sums_s[0:3, :] = sums[0:3, :]
        sums_s[5:6, :] = jnp.sum(slots.astype(f32), axis=0, keepdims=True)
        at = 6
        for up_bias in (up_bias_a, up_bias_b):
            for block in range(up_bias.shape[1] // width):
                sums_s[at : at + 1, :] = up_bias[:, block * width : (block + 1) * width]
                at += 1

    @pl.when(last & (core[0] == 0))
    def _():
        give(keep_o, send_o)

    @pl.when(last & (core[0] == 1))
    def _():
        give(send_o, keep_o)


def prepare_kernel(cotangent, next_cot, pos_embed, order, cot_o, positions_o):
    block = order.shape[0]
    tokens = cotangent.shape[0]
    for at in range(0, tokens, block):
        if at + block < tokens:
            rows = cotangent[at + RIM : at + RIM + block, :]
        else:
            rows = jnp.concatenate([cotangent[at + RIM :, :], next_cot[...]], axis=0)
        cot_o[at : at + block, :] = mm(order[...].astype(bf16), rows).astype(bf16)
    grid_rows = pos_embed.shape[0]
    for at in range(0, grid_rows, block):
        if at + block < grid_rows:
            rows = pos_embed[at + RIM : at + RIM + block, :]
        else:
            rows = jnp.concatenate([pos_embed[at + RIM :, :], pos_embed[0:RIM, :]], axis=0)
        positions_o[at : at + block, :] = jnp.dot(
            order[...], rows, precision=PRECISE, preferred_element_type=f32
        )


def out_kernel(
    middle, act_a, act_b, down_a, down_b, down_bias, order, after, out_o, rim_o
):
    del after
    step = pl.program_id(0)
    last = pl.num_programs(0) - 1
    rows = middle.shape[0]
    block = order.shape[0]
    result = (
        middle[...] + mm(act_a[...], down_a[...]) + mm(act_b[...], down_b[...]) + down_bias[...]
    ).astype(bf16)
    result = jnp.concatenate(
        [mm_tn(order[...], result[b : b + block]).astype(bf16) for b in range(0, rows, block)],
        axis=0,
    )

    @pl.when(step < last)
    def _():
        out_o[pl.ds(pl.multiple_of(step * rows + RIM, RIM), rows), :] = result

    @pl.when(step == last)
    def _():
        out_o[pl.ds(pl.multiple_of(step * rows + RIM, RIM), rows - RIM), :] = result[: rows - RIM]
        rim_o[...] = result[rows - RIM :]
        out_o[0:RIM, :] = jnp.zeros((RIM, result.shape[1]), bf16)


def pair_sum_kernel(keep, got, after, sum_o):
    del after
    sum_o[...] = (keep[...].astype(f32) + got[...].astype(f32)).astype(bf16)


def cell_sum_kernel(count, *refs):
    parts, out = refs[:count], refs[-1]
    at = 0
    for part in parts:
        total = jnp.sum(part[...].astype(f32), axis=0).astype(bf16)
        chunks = out.shape[0]
        rows = total.shape[0] // chunks
        out[:, at : at + rows, :] = total.reshape(chunks, rows, total.shape[1])
        at += rows


def repeat_sum_kernel(part, after, out):
    del after
    total = jnp.sum(part[...].astype(f32), axis=0).astype(bf16)
    for copy in range(out.shape[0]):
        out[copy] = total


def repeat_kernel(part, after, out):
    del after
    for copy in range(out.shape[0]):
        out[copy] = part[...]


def feed_unpack_kernel(core, mine, other, down_o, up_o):
    parts = mine.shape[2]
    width = down_o.shape[1]

    def give(down, up):
        for f in range(parts):
            rows = down[:, :, f].reshape(-1, width).astype(f32)
            piece = rows.shape[0]
            down_o[f * piece : (f + 1) * piece, :] = rows
            rows = up[:, :, f].reshape(-1, width).astype(f32)
            for block in range(piece // width):
                up_o[:, f * piece + block * width : f * piece + (block + 1) * width] = rows[
                    block * width : (block + 1) * width
                ]

    @pl.when(core[0] == 0)
    def _():
        give(mine, other)

    @pl.when(core[0] == 1)
    def _():
        give(other, mine)


def rest_unpack_kernel(split, core, mine, other, qkv_o, out_o, embed_o, small_o):
    width = out_o.shape[1]
    e_in = embed_o.shape[0]

    def give(low, high):
        rows = low[:, :, 0:split].reshape(-1, width).astype(f32)
        qkv_o[:, 0:width] = rows[0:width]
        qkv_o[:, width : 2 * width] = rows[width:]
        rows = high[:, :, 0:split].reshape(-1, width).astype(f32)
        qkv_o[:, 2 * width :] = rows[0:width]
        out_o[...] = rows[width:]
        rows = low[:, :, split:].reshape(-1, width).astype(f32)
        half = rows.shape[0]
        embed_o[0 : min(half, e_in), :] = rows[0 : min(half, e_in)]
        rows = high[:, :, split:].reshape(-1, width).astype(f32)
        left = max(e_in - half, 0)
        if left:
            embed_o[half:e_in, :] = rows[0:left]
        small_o[...] = rows[left : left + small_o.shape[0]]

    @pl.when(core[0] == 0)
    def _():
        give(mine, other)

    @pl.when(core[0] == 1)
    def _():
        give(other, mine)


ANY = pl.BlockSpec(memory_space=pl.ANY)
SMEM = pl.BlockSpec(memory_space=pltpu.SMEM)


def whole(s):
    return pl.BlockSpec(s, lambda *i: (0,) * len(s))


def tile(rows, width, first=0):
    return pl.BlockSpec((rows, width), lambda i: (i + first, 0))


def params():
    return pltpu.CompilerParams(vmem_limit_bytes=VMEM_LIMIT)


def shape(s, d):
    return jax.ShapeDtypeStruct(s, d)


def at_once(kernel, args, outs, specs=None):
    if specs is None:
        specs = [whole(a.shape) for a in args]
    many = isinstance(outs, (list, tuple))
    out_specs = [whole(o.shape) for o in outs] if many else whole(outs.shape)
    return pl.pallas_call(
        kernel,
        grid=(1,),
        in_specs=specs,
        out_specs=out_specs,
        out_shape=outs,
        compiler_params=params(),
    )(*args)


def swap_cores(x):
    return lax.ppermute(x, "c", [(0, 1), (1, 0)])


def exchange(x, axis):
    return lax.all_to_all(x, axis, 0, 0, tiled=True)


def chip_share(keep, send, after):
    return at_once(
        pair_sum_kernel,
        (keep, swap_cores(send), after),
        shape(keep.shape, bf16),
        [whole(keep.shape)] * 2 + [ANY],
    )


def plane_exchange(share):
    cells = lax.axis_size("p")
    return exchange(share.reshape(cells, -1, share.shape[1]), "p")


def z_exchange(parts, after):
    planes = lax.axis_size("z")
    width = parts[0].shape[2]
    rows = sum(p.shape[1] for p in parts) // planes
    shares = at_once(
        partial(cell_sum_kernel, len(parts)),
        (*parts, *after),
        shape((planes, rows, width), bf16),
        [whole(p.shape) for p in parts] + [ANY] * len(after),
    )
    return shares, exchange(shares, "z")


def z_gather(part, after):
    repeated = at_once(
        repeat_sum_kernel, (part, after), shape(part.shape, bf16), [whole(part.shape), ANY]
    )
    return repeated, exchange(repeated, "z")


def plane_gather(part, after):
    cells = lax.axis_size("p")
    repeated = at_once(
        repeat_kernel, (part, after), shape((cells, *part.shape), bf16), [whole(part.shape), ANY]
    )
    return repeated, exchange(repeated, "p")


def order_matrix(block):
    token = np.arange(block)
    group, rest = token // (WIN * BANDS), token % (WIN * BANDS)
    frame, band = rest // BANDS, rest % BANDS
    row = group * (WIN * BANDS) + (band // WIN) * SPOTS + frame * WIN + band % WIN
    matrix = np.zeros((block, block), np.float32)
    matrix[row, token] = 1.0
    return matrix


def per_device(
    visible, embed_weight, embed_bias, mask_token, pos_embed, norm1_gain, qkv_weight, rel_table,
    out_weight, out_bias, norm2_gain, up_weight, up_bias, down_weight, down_bias, cotangent,
    visible_index, slot_counts, segment_ids,
):
    device_count = lax.axis_size(AXES)
    device_rank = lax.axis_index(AXES)
    core = lax.axis_index("c").reshape(1).astype(jnp.int32)
    planes, cells = lax.axis_size("z"), lax.axis_size("p")
    tokens, width = cotangent.shape
    frames = tokens // BANDS
    hidden = down_weight.shape[0]
    e_in = visible.shape[1]
    slot_rows = visible_index.shape[2]
    slots = device_count * slot_rows
    ext = slots + RIM_SLOTS
    back = [(i, (i - 1) % device_count) for i in range(device_count)]
    ahead = [(i, (i + 1) % device_count) for i in range(device_count)]
    row = lambda v: v.reshape(1, -1)

    arrived = exchange(visible, AXES)

    spot = visible_index.reshape(slots)
    live = (
        jnp.arange(slot_rows)[None, :] < slot_counts.reshape(device_count, 1)
    ).reshape(slots)
    rim_hot = ((jnp.arange(RIM)[:, None] == spot[None, :]) & live[None, :]).astype(bf16)
    rim_seen = jnp.sum(rim_hot.astype(f32), axis=1, keepdims=True).astype(bf16)
    sent_back = jnp.concatenate(
        [cotangent[:RIM], jnp.broadcast_to(rim_seen, (RIM, width))], axis=0
    )
    from_next = lax.ppermute(sent_back, AXES, back)
    next_seen = from_next[RIM:, 0].astype(f32)
    own_places = jnp.where(live & (spot >= RIM), window_row(spot - RIM), -1)
    rim_places = jnp.where(
        next_seen > 0.5, window_row(tokens - RIM + np.arange(RIM)), -1
    )
    places = jnp.concatenate(
        [own_places, rim_places, np.full((RIM_SLOTS - RIM,), -1, np.int32)]
    ).reshape(1, ext).astype(jnp.int32)

    seg_cycle = jnp.concatenate([segment_ids, segment_ids[:SHIFT]])
    seg_tape = lax.dynamic_slice_in_dim(seg_cycle, device_rank * frames + SHIFT, frames)
    seg_win = seg_tape.reshape(frames // WIN, WIN)
    cut = jnp.repeat(
        (seg_win[:, SHIFT - 1] != seg_win[:, SHIFT]).astype(f32), BANDS // WIN
    )

    spots = np.arange(SPOTS)
    frame_of, band_of = spots // WIN, spots % WIN
    rels = 2 * WIN - 1
    rel_index = (frame_of[:, None] - frame_of[None, :] + WIN - 1) * rels + (
        band_of[:, None] - band_of[None, :] + WIN - 1
    )
    rel_hot = (rel_index[:, :, None] == np.arange(rels * rels)).astype(np.float32)
    bias = jnp.einsum("hr,ijr->jhi", rel_table, rel_hot, precision=PRECISE).reshape(
        SPOTS, HEADS * SPOTS
    )
    halves = frame_of // SHIFT
    across = np.tile(
        np.where(halves[:, None] != halves[None, :], MASKED, 0.0).astype(np.float32), (1, HEADS)
    )
    ones = jnp.asarray(
        np.arange(OCT_S)[:, None] // SPOTS == np.arange(OCT_D)[None, :] // HD, bf16
    )
    order = order_matrix(256)
    cot, positions = at_once(
        prepare_kernel,
        (cotangent, from_next[:RIM], pos_embed, order),
        [shape(cotangent.shape, bf16), shape(pos_embed.shape, f32)],
    )

    tm = min(512, tokens)
    steps = tokens // tm
    grid = (steps,)
    pos_blocks = pos_embed.shape[0] // tm
    forward_outs = [
        (width, f32), (width, bf16), (3 * width, bf16), (HEADS * SPOTS, f32), (width, bf16),
        (width, f32), (width, bf16),
    ]

    def forward(first, count, rim, held):
        fixed = [
            cut, arrived, rim, embed_weight, row(embed_bias), places, positions, row(mask_token),
            row(norm1_gain), qkv_weight, bias, across, ones, out_weight, row(out_bias),
            row(norm2_gain),
        ]
        specs = [SMEM] + [whole(a.shape) for a in fixed[1:]]
        specs[6] = pl.BlockSpec((tm, width), lambda i: (lax.rem(i + first, pos_blocks), 0))
        return pl.pallas_call(
            partial(forward_kernel, first),
            grid=(count,),
            in_specs=specs + [ANY] * len(held),
            out_specs=[tile(tm, w, first) for w, _ in forward_outs],
            out_shape=[shape((tokens, w), d) for w, d in forward_outs],
            input_output_aliases={len(fixed) + i: i for i in range(len(held))},
            scratch_shapes=[
                pltpu.VMEM((ext, width), bf16),
                pltpu.VMEM((tm, HEADS * SPOTS), f32),
                pltpu.VMEM((tm, width), f32),
            ],
            compiler_params=params(),
        )(*fixed, *held)

    rim_rows = jnp.dot(rim_hot, arrived, preferred_element_type=f32).astype(bf16)
    next_rows = lax.ppermute(rim_rows, AXES, back)
    rim = jnp.pad(next_rows, ((0, RIM_SLOTS - RIM), (0, 0)))
    held = forward(0, steps - 1, jnp.zeros((RIM_SLOTS, e_in), bf16), ())
    start, h_one, qkv, probs, context, middle, h_two = forward(steps - 1, 1, rim, held)

    parts = 2
    piece = hidden // parts

    def feed(f, after):
        return pl.pallas_call(
            feed_kernel,
            grid=grid,
            in_specs=[
                SMEM,
                tile(tm, width),
                tile(tm, width),
                pl.BlockSpec((width, piece), lambda i: (0, f)),
                pl.BlockSpec((1, piece), lambda i: (0, f)),
                pl.BlockSpec((piece, width), lambda i: (f, 0)),
                ANY,
            ],
            out_specs=[
                tile(tm, piece),
                tile(tm, width),
                whole((piece, width)),
                whole((piece, width)),
                whole((1, piece)),
            ],
            out_shape=[
                shape((tokens, piece), bf16),
                shape((tokens, width), f32),
                shape((piece, width), bf16),
                shape((piece, width), bf16),
                shape((1, piece), f32),
            ],
            scratch_shapes=[pltpu.VMEM((piece, width), f32), pltpu.VMEM((width, piece), f32)],
            compiler_params=params(),
        )(core, h_two, cot, up_weight, row(up_bias), down_weight, after)

    act_a, grad_h_a, keep_a, send_a, up_bias_a = feed(0, cot)
    share_a = chip_share(keep_a, send_a, cot)
    plane_a = plane_exchange(share_a)
    act_b, grad_h_b, keep_b, send_b, up_bias_b = feed(1, share_a)
    share_b = chip_share(keep_b, send_b, cot)
    plane_b = plane_exchange(share_b)

    gqkv, grad_middle, keep_c, send_c, sums, rel_sum = pl.pallas_call(
        attend_back_kernel,
        grid=grid,
        in_specs=[
            SMEM,
            tile(tm, width),
            tile(tm, width),
            tile(tm, width),
            tile(tm, width),
            tile(tm, width),
            tile(tm, 3 * width),
            tile(tm, HEADS * SPOTS),
            tile(tm, width),
            whole((1, width)),
            whole((width, width)),
            whole((OCT_S, OCT_D)),
            ANY,
        ],
        out_specs=[
            tile(tm, 3 * width),
            tile(tm, width),
            whole((2 * width, width)),
            whole((2 * width, width)),
            whole((8, width)),
            whole((SPOTS, HEADS * SPOTS)),
        ],
        out_shape=[
            shape((tokens, 3 * width), bf16),
            shape((tokens, width), f32),
            shape((2 * width, width), bf16),
            shape((2 * width, width), bf16),
            shape((8, width), f32),
            shape((SPOTS, HEADS * SPOTS), f32),
        ],
        scratch_shapes=[
            pltpu.VMEM((width, width), f32),
            pltpu.VMEM((width, 3 * width), f32),
            pltpu.VMEM((tm, HEADS * SPOTS), f32),
        ],
        compiler_params=params(),
    )(
        core, grad_h_a, grad_h_b, cot, middle, context, qkv, probs, h_one, row(norm2_gain),
        out_weight, ones, share_b,
    )
    feed_shares, feed_z = z_exchange((plane_a, plane_b), (sums,))
    share_c = chip_share(keep_c, send_c, cot)
    plane_c = plane_exchange(share_c)

    unit = 16 * planes * cells
    half = -(-width // unit) * unit
    grad_slots, keep_d, send_d = pl.pallas_call(
        scatter_back_kernel,
        grid=grid,
        in_specs=[
            SMEM,
            tile(tm, 3 * width),
            tile(tm, width),
            tile(tm, width),
            whole((1, ext)),
            whole((width, 3 * width)),
            whole((1, width)),
            whole((slots, e_in)),
            whole((RIM_SLOTS, e_in)),
            whole((8, width)),
            whole((SPOTS, HEADS * SPOTS)),
            whole((1, piece)),
            whole((1, piece)),
            ANY,
            ANY,
        ],
        out_specs=[whole((ext, width)), whole((half, width)), whole((half, width))],
        out_shape=[shape((ext, width), bf16), shape((half, width), bf16), shape((half, width), bf16)],
        scratch_shapes=[
            pltpu.VMEM((ext, width), f32),
            pltpu.VMEM((max(e_in, half), width), f32),
            pltpu.VMEM((16, width), f32),
        ],
        compiler_params=params(),
    )(
        core, gqkv, start, grad_middle, places, qkv_weight, row(norm1_gain), arrived, rim, sums,
        rel_sum, up_bias_a, up_bias_b, feed_shares, share_c,
    )
    share_d = chip_share(keep_d, send_d, cot)
    plane_d = plane_exchange(share_d)
    rim_grad = lax.ppermute(grad_slots[slots : slots + RIM], AXES, ahead)
    feed_repeated, feed_z_all = z_gather(feed_z, share_d)

    out, rim_out = pl.pallas_call(
        out_kernel,
        grid=grid,
        in_specs=[
            tile(tm, width),
            tile(tm, piece),
            tile(tm, piece),
            pl.BlockSpec((piece, width), lambda i: (0, 0)),
            pl.BlockSpec((piece, width), lambda i: (1, 0)),
            whole((1, width)),
            whole(order.shape),
            ANY,
        ],
        out_specs=[whole((tokens, width)), whole((RIM, width))],
        out_shape=[shape((tokens, width), bf16), shape((RIM, width), bf16)],
        compiler_params=params(),
    )(
        middle, act_a, act_b, down_weight, down_weight, row(down_bias), jnp.asarray(order, bf16),
        feed_repeated,
    )
    rest_shares, rest_z = z_exchange((plane_c, plane_d), (rim_out,))
    feed_plane_repeated, feed_all = plane_gather(feed_z_all, rest_shares)

    grad_embedded = (
        grad_slots[:slots].astype(f32)
        + lax.dot_general(rim_hot, rim_grad, (((0,), (0,)), ((), ())), preferred_element_type=f32)
    ).astype(bf16)
    returned = exchange(grad_embedded, AXES)
    grad_visible = lax.dot_general(
        returned, embed_weight, (((1,), (1,)), ((), ())), preferred_element_type=f32
    ).astype(bf16)
    first_rows = lax.ppermute(rim_out, AXES, ahead)
    out = lax.dynamic_update_slice(out, first_rows, (0, 0))

    rest_repeated, rest_z_all = z_gather(rest_z, feed_plane_repeated)
    rest_plane_repeated, rest_all = plane_gather(rest_z_all, rest_repeated)

    chunk = piece // (cells * planes)
    feed_all = feed_all.reshape(cells, planes, parts, chunk, width)
    grad_down_weight, grad_up_weight = at_once(
        feed_unpack_kernel,
        (core, feed_all, swap_cores(feed_all)),
        [shape((hidden, width), f32), shape((width, hidden), f32)],
        [SMEM, whole(feed_all.shape), whole(feed_all.shape)],
    )
    split = 2 * width // (cells * planes)
    small_rows = 16 + SPOTS
    rest_all = rest_all.reshape(cells, planes, -1, width)
    grad_qkv_weight, grad_out_weight, grad_embed_weight, small = at_once(
        partial(rest_unpack_kernel, split),
        (core, rest_all, swap_cores(rest_all)),
        [
            shape((width, 3 * width), f32),
            shape((width, width), f32),
            shape((e_in, width), f32),
            shape((small_rows, width), f32),
        ],
        [SMEM, whole(rest_all.shape), whole(rest_all.shape)],
    )
    grad_rel = jnp.einsum(
        "jhi,ijr->hr",
        small[16:, : HEADS * SPOTS].reshape(SPOTS, HEADS, SPOTS),
        rel_hot,
        precision=PRECISE,
    )
    up_rows = hidden // width
    return (
        out,
        grad_visible,
        grad_embed_weight,
        small[5],
        small[4],
        small[3],
        grad_qkv_weight,
        grad_rel,
        grad_out_weight,
        small[1],
        small[0],
        grad_up_weight,
        small[6 : 6 + up_rows].reshape(hidden),
        grad_down_weight,
        small[2],
    )


def solution(mesh):
    planes = 4
    grid = Mesh(mesh.devices.reshape(planes, -1, 2), AXES)
    split = P(AXES)
    in_specs = (split,) + (P(),) * 14 + (split, split, split, P())
    out_specs = (split, split) + (P(),) * 13
    return jax.shard_map(
        per_device, mesh=grid, in_specs=in_specs, out_specs=out_specs, check_vma=False
    )
```

time: 770 us -> 354 us (0.46)
  matrix products: 216 us -> 5.76 us
  local copies, waits for them, and re-layouts: 212 us -> 17.1 us
  Pallas kernels: 0 us -> 152 us
  waiting for transfers between devices: 211 us -> 84.2 us
  other arithmetic: 46.7 us -> 2.1 us
  starting transfers between devices: 17.2 us -> 55.3 us
  between operations: 15.2 us -> 0.95 us
  blocking collectives: 42.6 us -> 33.9 us
    dot_general x24 -> x5, matrix products: 216 us -> 5.76 us  [the longest x1 1.89 us: per_device(): lax.dot_general(rim_hot, rim_grad, (((0,), (0,)), ((), ())), preferred_el...]
    psum x1 -> x0, waiting for transfers between devices: 198 us -> none  [per_device(): lax.psum((grad_embed_weight, grad_embed_bias, grad_mask_token, grad_norm1...]
    pallas_call x0 -> x20, Pallas kernels: none -> 152 us  [the longest x13 39.1 us: at_once(): pl.pallas_call(kernel, grid=(1,), in_specs=specs, out_specs=out_specs, ou...]
    reshape x14 -> x5, local copies, waits for them, and re-layouts: 127 us -> 2.16 us  [the longest x1 0.7 us: per_device(): jnp.einsum('hr,ijr->jhi', rel_table, rel_hot, precision=PRECISE)]
    all_to_all x2 -> x10, waiting for transfers between devices: 11.1 us -> 63.3 us  [exchange(): return lax.all_to_all(x, axis, 0, 0, tiled=True)]
    psum x1 -> x0, blocking collectives: 42.6 us -> none  [per_device(): lax.psum((grad_embed_weight, grad_embed_bias, grad_mask_token, grad_norm1...]
    reduce_sum x9 -> x1, other arithmetic: 39.8 us -> 0.12 us  [per_device(): rim_seen = jnp.sum(rim_hot.astype(f32), axis=1, keepdims=True).astype(bf16)]
    all_to_all x2 -> x10, starting transfers between devices: 11.1 us -> 45.9 us  [exchange(): return lax.all_to_all(x, axis, 0, 0, tiled=True)]
  transfers between devices with their start and end apart: 7 -> 20, of which waited for: 3 -> 12; matrix products, arithmetic and copies ran while one was open for 8% -> 5% of each run, Pallas kernels for 0% -> 28%
where the time goes in v1:
time: 354 us; the launch traced here: 352 us
  Pallas kernels  152 us (43%)
  waiting for transfers between devices  84.2 us (24%)
  starting transfers between devices  55.3 us (16%)
  blocking collectives  33.9 us (10%)
  local copies, waits for them, and re-layouts  17.1 us (5%)
  matrix products  5.76 us (2%)
    all_to_all x10, waiting for transfers between devices, exchange(): return lax.all_to_all(x, axis, 0, 0, tiled=True)  63.3 us
    all_to_all x10, starting transfers between devices, exchange(): return lax.all_to_all(x, axis, 0, 0, tiled=True)  45.9 us
    pallas_call x13, Pallas kernels, at_once(): pl.pallas_call(kernel, grid=(1,), in_specs=specs, out_specs=out_specs, ou...  39.1 us
    pallas_call x2, Pallas kernels, feed(): pl.pallas_call(feed_kernel, grid=grid, in_specs=[SMEM, tile(tm, width), t...  34.2 us
    all_to_all x2, blocking collectives, exchange(): return lax.all_to_all(x, axis, 0, 0, tiled=True)  33.9 us
    pallas_call x1, Pallas kernels, per_device(): pl.pallas_call(attend_back_kernel, grid=grid, in_specs=[SMEM, tile(tm, wi...  28.2 us
    pallas_call x2, Pallas kernels, forward(): pl.pallas_call(partial(forward_kernel, first), grid=(count,), in_specs=sp...  27.2 us
    ppermute x1, waiting for transfers between devices, per_device(): first_rows = lax.ppermute(rim_out, AXES, ahead)  14.6 us
  transfers between devices with their start and end apart: 20, of which 12 were waited for; matrix products, arithmetic and copies ran while one was open for 5% of the time, Pallas kernels for 28%

profile of v1, /device:TPU:0, one launch (start us, length us, event | category | flops | bytes accessed | tf_op | source)
XLA Modules:
  0.0 351.6 jit_solution(17183873015210792477)
XLA Ops:
  0.7 7.3 %all-to-all-start = ((bf16[32,16,768]{2,1,0:T(8,128)(2,1)}), bf16[32,16,768]{2,1,0:T(8,128)(2,1)S(1)}, u32[]{:S(2)}, u32[]{:S(2)}) async-start(bf16[32,16,768]{2,1,0:T(8,128)(2,1)} %bitcast.50), calls=%async_computation | async-start | bytes 1572864 | tf_op jit(solution)/shard_map/all_to_all | solution.py:498
  10.7 5.2 %collective-permute-start.1 = (bf16[32,512]{1,0:T(8,128)(2,1)S(1)}, bf16[32,512]{1,0:T(8,128)(2,1)S(1)}, u32[]{:S(2)}, u32[]{:S(2)}) collective-permute-start(bf16[32,512]{1,0:T(8,128)(2,1)S(1)} %pad_maximum_fusion), channel_id=1, source_target_pairs={{0,31},{1,0},{2,1},{3,2},{4,3},{5,4},{6,5},{7,6},{8,7},{9,8},{10,9... | collective-permute-start | bytes 98312 | tf_op jit(solution)/shard_map/ppermute | solution.py:584
  21.8 6.8 %all-to-all-done = bf16[32,16,768]{2,1,0:T(8,128)(2,1)S(1)} async-done(((bf16[32,16,768]{2,1,0:T(8,128)(2,1)}), bf16[32,16,768]{2,1,0:T(8,128)(2,1)S(1)}, u32[]{:S(2)}, u32[]{:S(2)}) %all-to-all-start) | async-done | bytes 786464 | tf_op jit(solution)/shard_map/all_to_all | solution.py:498
  33.0 4.5 %shard_map.370 = (bf16[2048,512]{1,0:T(8,128)(2,1)}, f32[512,512]{1,0:T(8,128)}) custom-call(bf16[2048,512]{1,0:T(8,128)(2,1)} %cotangent.1, bf16[16,512]{1,0:T(8,128)(2,1)} %slice.67.next_cot, f32[512,512]{1,0:T(8,128)} %pos_embed.1, f32[256,256]{1,0:T(8,128)} %constant.117.clone.order), custom_call_target="tpu_custom_call" | custom-call | tf_op jit(solution)/shard_map/pallas_call | solution.py:483
  38.2 18.8 %shard_map.371 = (f32[2048,512]{1,0:T(8,128)}, bf16[2048,512]{1,0:T(8,128)(2,1)}, bf16[2048,1536]{1,0:T(8,128)(2,1)}, f32[2048,256]{1,0:T(8,128)}, bf16[2048,512...) custom-call(f32[128]{0:T(128)} %reshape.131.cut, bf16[512,768]{1,0:T(8,128)(2,1)} %bitcast.42, ...), custom_call_target="tpu_custom_call" | custom-call | tf_op jit(solution)/shard_map/pallas_call | solution.py:642
  57.8 8.4 %shard_map.372 = (f32[2048,512]{1,0:T(8,128)}, bf16[2048,512]{1,0:T(8,128)(2,1)}, bf16[2048,1536]{1,0:T(8,128)(2,1)}, f32[2048,256]{1,0:T(8,128)}, bf16[2048,512...) custom-call(f32[128]{0:T(128)} %reshape.131.cut, ...), custom_call_target="tpu_custom_call", output_to_operand_aliasing={{0}: (16, {}), {1}: (17, {}), {2}: (18, {}), {3}: (19, {}),... | custom-call | tf_op jit(solution)/shard_map/pallas_call | solution.py:642
  66.1 17.1 %shard_map.373 = (bf16[2048,1024]{1,0:T(8,128)(2,1)}, f32[2048,512]{1,0:T(8,128)}, bf16[1024,512]{1,0:T(8,128)(2,1)}, bf16[1024,512]{1,0:T(8,128)(2,1)}, f32[1,1024]{1,0:T(1,128)}) custom-call(s32[1]{0:T(128)} %bitcast.10.core, bf16[2048,512]{1,0:T(8,128)(2,1)} %get-tuple-element.67.h_two, bf16[2048,512]{1,0:T(8,128)(2,1)} %get-tuple-element.68.cotangent.after, ...), custom_call_target="tpu_custom_call" | custom-call | tf_op jit(solution)/shard_map/pallas_call | solution.py:667
  89.9 17.1 %shard_map.375 = (bf16[2048,1024]{1,0:T(8,128)(2,1)}, f32[2048,512]{1,0:T(8,128)}, bf16[1024,512]{1,0:T(8,128)(2,1)}, bf16[1024,512]{1,0:T(8,128)(2,1)}, f32[1,1024]{1,0:T(1,128)}) custom-call(s32[1]{0:T(128)} %bitcast.10.core, bf16[2048,512]{1,0:T(8,128)(2,1)} %get-tuple-element.67.h_two, bf16[2048,512]{1,0:T(8,128)(2,1)} %get-tuple-element.68.cotangent.after, ...), custom_call_target="tpu_custom_call" | custom-call | tf_op jit(solution)/shard_map/pallas_call | solution.py:667
  114.4 10.7 %all-to-all-done.1.refs_0_ = bf16[4,256,512]{2,1,0:T(8,128)(2,1)S(1)} async-done(((bf16[4,256,512]{2,1,0:T(8,128)(2,1)}), bf16[4,256,512]{2,1,0:T(8,128)(2,1)S(1)}, u32[]{:S(2)}, u32[]{:S(2)}) %all-to-all-start.1) | async-done | bytes 1048608 | tf_op jit(solution)/shard_map/all_to_all | solution.py:498
  128.6 28.2 %shard_map.377 = (bf16[2048,1536]{1,0:T(8,128)(2,1)}, f32[2048,512]{1,0:T(8,128)}, bf16[1024,512]{1,0:T(8,128)(2,1)}, bf16[1024,512]{1,0:T(8,128)(2,1)}, f32[8,512]{1,0:T(8,128)}, /*index=5*/f32[16,256]{1,0:T(8,128)}) custom-call(s32[1]{0:T(128)} %bitcast.10.core, f32[2048,512]{1,0:T(8,128)} %get-tuple-element.75.grad_h_a, ...), custom_call_target="tpu_custom_call" | custom-call | tf_op jit(solution)/shard_map/pallas_call | solution.py:704
  167.7 11.7 %all-to-all-done.3.part = bf16[4,128,512]{2,1,0:T(8,128)(2,1)S(1)} async-done(((bf16[4,128,512]{2,1,0:T(8,128)(2,1)}), bf16[4,128,512]{2,1,0:T(8,128)(2,1)S(1)}, u32[]{:S(2)}, u32[]{:S(2)}) %all-to-all-start.3) | async-done | bytes 524320 | tf_op jit(solution)/shard_map/all_to_all | solution.py:498
  179.3 4.1 %all-to-all-start.5 = ((bf16[4,256,512]{2,1,0:T(8,128)(2,1)}), bf16[4,256,512]{2,1,0:T(8,128)(2,1)S(1)}, u32[]{:S(2)}, u32[]{:S(2)}) async-start(bf16[4,256,512]{2,1,0:T(8,128)(2,1)} %bitcast.45), calls=%async_computation.5 | async-start | bytes 2097152 | tf_op jit(solution)/shard_map/all_to_all | solution.py:498
  183.5 13.0 %shard_map.380 = (bf16[640,512]{1,0:T(8,128)(2,1)}, bf16[512,512]{1,0:T(8,128)(2,1)}, bf16[512,512]{1,0:T(8,128)(2,1)}) custom-call(s32[1]{0:T(128)} %bitcast.10.core, bf16[2048,1536]{1,0:T(8,128)(2,1)} %get-tuple-element.82.gqkv, f32[2048,512]{1,0:T(8,128)} %get-tuple-element.83.start, f32[2048,512]{1,0:T(8,128)} %get-tuple-element.84.grad_middle, ...), custom_call_target="tpu_custom_call" | custom-call | tf_op jit(solution)/shard_map/pallas_call | solution.py:754
  201.6 4.2 %all-to-all-start.6 = ((bf16[4,128,512]{2,1,0:T(8,128)(2,1)}), bf16[4,128,512]{2,1,0:T(8,128)(2,1)S(1)}, u32[]{:S(2)}, u32[]{:S(2)}) async-start(bf16[4,128,512]{2,1,0:T(8,128)(2,1)} %bitcast.49), calls=%async_computation.6 | async-start | bytes 1048576 | tf_op jit(solution)/shard_map/all_to_all | solution.py:498
  207.7 6.4 %all-to-all-done.6.refs_1_ = bf16[4,128,512]{2,1,0:T(8,128)(2,1)S(1)} async-done(((bf16[4,128,512]{2,1,0:T(8,128)(2,1)}), bf16[4,128,512]{2,1,0:T(8,128)(2,1)S(1)}, u32[]{:S(2)}, u32[]{:S(2)}) %all-to-all-start.6) | async-done | bytes 524320 | tf_op jit(solution)/shard_map/all_to_all | solution.py:498
  217.5 10.7 %shard_map.383 = (bf16[2048,512]{1,0:T(8,128)(2,1)}, bf16[16,512]{1,0:T(8,128)(2,1)}) custom-call(f32[2048,512]{1,0:T(8,128)} %get-tuple-element.66.middle, bf16[2048,1024]{1,0:T(8,128)(2,1)} %get-tuple-element.69.act_a, bf16[2048,1024]{1,0:T(8,128)(2,1)} %get-tuple-element.72.act_b, bf16[2048,512]{1,0:T(8,128)(2,1)} %down_b.1, bf16[2048,512]{1,0:T(8,128)(2,1)} %down_b.1, ...), custom_call_target="tpu_custom_call" | custom-call | tf_op jit(solution)/shard_map/pallas_call | solution.py:791
  238.1 8.1 %all-to-all-done.7.part = bf16[4,96,512]{2,1,0:T(8,128)(2,1)S(1)} async-done(((bf16[4,96,512]{2,1,0:T(8,128)(2,1)}), bf16[4,96,512]{2,1,0:T(8,128)(2,1)S(1)}, u32[]{:S(2)}, u32[]{:S(2)}) %all-to-all-start.7) | async-done | bytes 393248 | tf_op jit(solution)/shard_map/all_to_all | solution.py:498
  248.7 13.6 %all_to_all.73.part = bf16[4,96,512]{2,1,0:T(8,128)(2,1)} all-to-all(bf16[4,96,512]{2,1,0:T(8,128)(2,1)} %shard_map.386.after), channel_id=1, replica_groups=mesh['z'=4,'p'=4,'c'=2] {'z'}, dimensions={0} | all-to-all | bytes 786432 | tf_op jit(solution)/shard_map/all_to_all | solution.py:498
  264.5 20.3 %all_to_all.74.mine = bf16[4,4,96,512]{3,2,1,0:T(8,128)(2,1)} all-to-all(bf16[4,4,96,512]{3,2,1,0:T(8,128)(2,1)} %shard_map.387), channel_id=1, replica_groups=mesh['z'=4,'p'=4,'c'=2] {'p'}, dimensions={0} | all-to-all | bytes 3145728 | tf_op jit(solution)/shard_map/all_to_all | solution.py:498
  289.8 18.5 %all-to-all-done.11 = bf16[4,4,128,512]{3,2,1,0:T(8,128)(2,1)S(1)} async-done(((bf16[4,4,128,512]{3,2,1,0:T(8,128)(2,1)}), bf16[4,4,128,512]{3,2,1,0:T(8,128)(2,1)S(1)}, u32[]{:S(2)}, u32[]{:S(2)}) %all-to-all-start.11) | async-done | bytes 2097184 | tf_op jit(solution)/shard_map/all_to_all | solution.py:498
  310.2 8.4 %all-to-all-start.4 = ((bf16[32,16,512]{2,1,0:T(8,128)(2,1)}), bf16[32,16,512]{2,1,0:T(8,128)(2,1)S(1)}, u32[]{:S(2)}, u32[]{:S(2)}) async-start(bf16[32,16,512]{2,1,0:T(8,128)(2,1)} %bitcast.15), calls=%async_computation.4 | async-start | bytes 1048576 | tf_op jit(solution)/shard_map/all_to_all | solution.py:498
  319.0 14.6 %collective-permute-done.6 = bf16[16,512]{1,0:T(8,128)(2,1)S(1)} collective-permute-done((bf16[16,512]{1,0:T(8,128)(2,1)}, bf16[16,512]{1,0:T(8,128)(2,1)S(1)}, u32[]{:S(2)}, u32[]{:S(2)}) %collective-permute-start.6) | collective-permute-done | bytes 16416 | tf_op jit(solution)/shard_map/ppermute | solution.py:822
  335.9 4.8 %shard_map.388 = (f32[512,1536]{1,0:T(8,128)}, f32[512,512]{1,0:T(8,128)}, f32[768,512]{1,0:T(8,128)}, f32[32,512]{1,0:T(8,128)}) custom-call(s32[1]{0:T(128)} %bitcast.10.core, bf16[4,4,96,512]{3,2,1,0:T(8,128)(2,1)} %all_to_all.74.mine, bf16[4,4,96,512]{3,2,1,0:T(8,128)(2,1)} %collective-permute-done.8.other), custom_call_target="tpu_custom_call" | custom-call | tf_op jit(solution)/shard_map/pallas_call | solution.py:483
  345.5 6.2 %shard_map.389 = (f32[2048,512]{1,0:T(8,128)}, f32[512,2048]{1,0:T(8,128)}) custom-call(s32[1]{0:T(128)} %bitcast.10.core, bf16[4,4,2,64,512]{4,3,2,1,0:T(8,128)(2,1)} %bitcast.48, bf16[4,4,2,64,512]{4,3,2,1,0:T(8,128)(2,1)} %collective-permute-done.9.other), custom_call_target="tpu_custom_call" | custom-call | tf_op jit(solution)/shard_map/pallas_call | solution.py:483
  (112 shorter events, 82.1 us)
Async XLA Ops:
  0.7 27.9 %all-to-all-start = ((bf16[32,16,768]{2,1,0:T(8,128)(2,1)}), bf16[32,16,768]{2,1,0:T(8,128)(2,1)S(1)}, u32[]{:S(2)}, u32[]{:S(2)}) async-start(bf16[32,16,768]{2,1,0:T(8,128)(2,1)} %bitcast.50), calls=%async_computation | async-start | bytes 1572864 | tf_op jit(solution)/shard_map/all_to_all | solution.py:498
  10.7 11.1 %collective-permute-start.1 = (bf16[32,512]{1,0:T(8,128)(2,1)S(1)}, bf16[32,512]{1,0:T(8,128)(2,1)S(1)}, u32[]{:S(2)}, u32[]{:S(2)}) collective-permute-start(bf16[32,512]{1,0:T(8,128)(2,1)S(1)} %pad_maximum_fusion), channel_id=1, source_target_pairs={{0,31},{1,0},{2,1},{3,2},{4,3},{5,4},{6,5},{7,6},{8,7},{9,8},{10,9... | collective-permute-start | bytes 98312 | tf_op jit(solution)/shard_map/ppermute | solution.py:584
  28.8 28.2 %collective-permute-start = (bf16[16,768]{1,0:T(8,128)(2,1)S(1)}, bf16[16,768]{1,0:T(8,128)(2,1)S(1)}, u32[]{:S(2)}, u32[]{:S(2)}) collective-permute-start(bf16[16,768]{1,0:T(8,128)(2,1)S(1)} %convolution_convert_fusion.1), channel_id=1, source_target_pairs={{0,31},{1,0},{2,1},{3,2},{4,3},{5,4},{6,5},{7,6},{8,7},{9,8},{10,9... | collective-permute-start | bytes 73736 | tf_op jit(solution)/shard_map/ppermute | solution.py:658
  83.2 2.9 collective-permute-start.2
  106.9 3.7 %collective-permute-start.3 = (bf16[1024,512]{1,0:T(8,128)(2,1)}, bf16[1024,512]{1,0:T(8,128)(2,1)S(1)}, u32[]{:S(2)}, u32[]{:S(2)}) collective-permute-start(bf16[1024,512]{1,0:T(8,128)(2,1)} %get-tuple-element.74), channel_id=1, source_target_pairs={{0,1},{1,0},{2,3},{3,2},{4,5},{5,4},{6,7},{7,6},{8,9},{9,8},{10,11... | collective-permute-start | bytes 3145736 | tf_op jit(solution)/shard_map/ppermute | solution.py:494
  107.1 17.9 %all-to-all-start.1 = ((bf16[4,256,512]{2,1,0:T(8,128)(2,1)}), bf16[4,256,512]{2,1,0:T(8,128)(2,1)S(1)}, u32[]{:S(2)}, u32[]{:S(2)}) async-start(bf16[4,256,512]{2,1,0:T(8,128)(2,1)} %bitcast.13), calls=%async_computation.1 | async-start | bytes 2097152 | tf_op jit(solution)/shard_map/all_to_all | solution.py:498
  125.1 31.7 %copy-start.4 = (bf16[4,256,512]{2,1,0:T(8,128)(2,1)}, bf16[4,256,512]{2,1,0:T(8,128)(2,1)S(1)}, u32[]{:S(2)}) copy-start(bf16[4,256,512]{2,1,0:T(8,128)(2,1)S(1)} %all-to-all-done.1.refs_0_) | copy-start | bytes 3145732
  125.1 31.8 %all-to-all-start.2 = ((bf16[4,256,512]{2,1,0:T(8,128)(2,1)}), bf16[4,256,512]{2,1,0:T(8,128)(2,1)S(1)}, u32[]{:S(2)}, u32[]{:S(2)}) async-start(bf16[4,256,512]{2,1,0:T(8,128)(2,1)} %bitcast.46), calls=%async_computation.2 | async-start | bytes 2097152 | tf_op jit(solution)/shard_map/all_to_all | solution.py:498
  156.8 7.1 %collective-permute-start.4 = (bf16[1024,512]{1,0:T(8,128)(2,1)}, bf16[1024,512]{1,0:T(8,128)(2,1)S(1)}, u32[]{:S(2)}, u32[]{:S(2)}) collective-permute-start(bf16[1024,512]{1,0:T(8,128)(2,1)} %get-tuple-element.89), channel_id=1, source_target_pairs={{0,1},{1,0},{2,3},{3,2},{4,5},{5,4},{6,7},{7,6},{8,9},{9,8},{10,11... | collective-permute-start | bytes 3145736 | tf_op jit(solution)/shard_map/ppermute | solution.py:494
  160.5 18.9 %all-to-all-start.3 = ((bf16[4,128,512]{2,1,0:T(8,128)(2,1)}), bf16[4,128,512]{2,1,0:T(8,128)(2,1)S(1)}, u32[]{:S(2)}, u32[]{:S(2)}) async-start(bf16[4,128,512]{2,1,0:T(8,128)(2,1)} %shard_map.378.after_a), calls=%async_computation.3 | async-start | bytes 1048576 | tf_op jit(solution)/shard_map/all_to_all | solution.py:498
  179.3 22.2 %all-to-all-start.5 = ((bf16[4,256,512]{2,1,0:T(8,128)(2,1)}), bf16[4,256,512]{2,1,0:T(8,128)(2,1)S(1)}, u32[]{:S(2)}, u32[]{:S(2)}) async-start(bf16[4,256,512]{2,1,0:T(8,128)(2,1)} %bitcast.45), calls=%async_computation.5 | async-start | bytes 2097152 | tf_op jit(solution)/shard_map/all_to_all | solution.py:498
  196.5 2.2 collective-permute-start.5
  201.6 26.7 %copy-start.6 = (bf16[4,256,512]{2,1,0:T(8,128)(2,1)}, bf16[4,256,512]{2,1,0:T(8,128)(2,1)S(1)}, u32[]{:S(2)}) copy-start(bf16[4,256,512]{2,1,0:T(8,128)(2,1)S(1)} %all-to-all-done.5.refs_0_) | copy-start | bytes 3145732
  201.6 12.5 %all-to-all-start.6 = ((bf16[4,128,512]{2,1,0:T(8,128)(2,1)}), bf16[4,128,512]{2,1,0:T(8,128)(2,1)S(1)}, u32[]{:S(2)}, u32[]{:S(2)}) async-start(bf16[4,128,512]{2,1,0:T(8,128)(2,1)} %bitcast.49), calls=%async_computation.6 | async-start | bytes 1048576 | tf_op jit(solution)/shard_map/all_to_all | solution.py:498
  214.1 17.4 %all-to-all-start.8 = ((bf16[4,128,512]{2,1,0:T(8,128)(2,1)}), bf16[4,128,512]{2,1,0:T(8,128)(2,1)S(1)}, u32[]{:S(2)}, u32[]{:S(2)}) async-start(bf16[4,128,512]{2,1,0:T(8,128)(2,1)} %shard_map.382.after), calls=%async_computation.8 | async-start | bytes 1048576 | tf_op jit(solution)/shard_map/all_to_all | solution.py:498
  231.5 14.7 %all-to-all-start.7 = ((bf16[4,96,512]{2,1,0:T(8,128)(2,1)}), bf16[4,96,512]{2,1,0:T(8,128)(2,1)S(1)}, u32[]{:S(2)}, u32[]{:S(2)}) async-start(bf16[4,96,512]{2,1,0:T(8,128)(2,1)} %shard_map.384.after), calls=%async_computation.7 | async-start | bytes 786432 | tf_op jit(solution)/shard_map/all_to_all | solution.py:498
  284.8 23.5 %all-to-all-start.11 = ((bf16[4,4,128,512]{3,2,1,0:T(8,128)(2,1)}), bf16[4,4,128,512]{3,2,1,0:T(8,128)(2,1)S(1)}, u32[]{:S(2)}, u32[]{:S(2)}) async-start(bf16[4,4,128,512]{3,2,1,0:T(8,128)(2,1)} %shard_map.385.after), calls=%async_computation.11 | async-start | bytes 4194304 | tf_op jit(solution)/shard_map/all_to_all | solution.py:498
  288.6 45.8 %copy-start.7 = (bf16[768,512]{1,0:T(8,128)(2,1)S(1)}, bf16[768,512]{1,0:T(8,128)(2,1)}, u32[]{:S(2)}) copy-start(bf16[768,512]{1,0:T(8,128)(2,1)} %embed_w.3) | copy-start | bytes 2359300
  288.6 47.3 %collective-permute-start.8 = (bf16[4,4,96,512]{3,2,1,0:T(8,128)(2,1)}, bf16[4,4,96,512]{3,2,1,0:T(8,128)(2,1)}, u32[]{:S(2)}, u32[]{:S(2)}) collective-permute-start(bf16[4,4,96,512]{3,2,1,0:T(8,128)(2,1)} %all_to_all.74.mine), channel_id=1, source_target_pairs={{0,1},{1,0},{2,3},{3,2},{4,5},{5,4},{6,7},{7,6},{8,9},{9,8},{10,11... | collective-permute-start | bytes 4718600 | tf_op jit(solution)/shard_map/ppermute | solution.py:494
  289.3 19.0 %collective-permute-start.7 = (bf16[16,512]{1,0:T(8,128)(2,1)}, bf16[16,512]{1,0:T(8,128)(2,1)}, u32[]{:S(2)}, u32[]{:S(2)}) collective-permute-start(bf16[16,512]{1,0:T(8,128)(2,1)} %slice.55), channel_id=1, source_target_pairs={{0,1},{1,2},{2,3},{3,4},{4,5},{5,6},{6,7},{7,8},{8,9},{9,10},{10,1... | collective-permute-start | bytes 49160 | tf_op jit(solution)/shard_map/ppermute | solution.py:788
  308.3 27.6 %copy-start.3 = (bf16[4,4,128,512]{3,2,1,0:T(8,128)(2,1)}, bf16[4,4,128,512]{3,2,1,0:T(8,128)(2,1)S(1)}, u32[]{:S(2)}) copy-start(bf16[4,4,128,512]{3,2,1,0:T(8,128)(2,1)S(1)} %all-to-all-done.11) | copy-start | bytes 6291460
  308.3 37.2 %collective-permute-start.9 = (bf16[4,4,2,64,512]{4,3,2,1,0:T(8,128)(2,1)S(1)}, bf16[4,4,2,64,512]{4,3,2,1,0:T(8,128)(2,1)}, u32[]{:S(2)}, u32[]{:S(2)}) collective-permute-start(bf16[4,4,2,64,512]{4,3,2,1,0:T(8,128)(2,1)S(1)} %bitcast.47), channel_id=1, source_target_pairs={{0,1},{1,0},{2,3},{3,2},{4,5},{5,4},{6,7},{7,6},{8,9},{9,8},{10,11... | collective-permute-start | bytes 6291464 | tf_op jit(solution)/shard_map/ppermute | solution.py:494
  310.2 24.2 %all-to-all-start.4 = ((bf16[32,16,512]{2,1,0:T(8,128)(2,1)}), bf16[32,16,512]{2,1,0:T(8,128)(2,1)S(1)}, u32[]{:S(2)}, u32[]{:S(2)}) async-start(bf16[32,16,512]{2,1,0:T(8,128)(2,1)} %bitcast.15), calls=%async_computation.4 | async-start | bytes 1048576 | tf_op jit(solution)/shard_map/all_to_all | solution.py:498
  318.7 14.9 %collective-permute-start.6 = (bf16[16,512]{1,0:T(8,128)(2,1)}, bf16[16,512]{1,0:T(8,128)(2,1)S(1)}, u32[]{:S(2)}, u32[]{:S(2)}) collective-permute-start(bf16[16,512]{1,0:T(8,128)(2,1)} %get-tuple-element.93.refs_2_), channel_id=1, source_target_pairs={{0,1},{1,2},{2,3},{3,4},{4,5},{5,6},{6,7},{7,8},{8,9},{9,10},{10,1... | collective-permute-start | bytes 49160 | tf_op jit(solution)/shard_map/ppermute | solution.py:822
  (15 other events, 106.3 us)

commit v2 on v1

v2 whole, which is shorter than its diff:
```python
from functools import partial

import jax
import jax.numpy as jnp
import numpy as np
from jax import lax
from jax.experimental import pallas as pl
from jax.experimental.pallas import tpu as pltpu
from jax.sharding import Mesh, PartitionSpec as P

HEADS = 16
HD = 32
BANDS = 8
WIN = 4
SHIFT = 2
RIM = SHIFT * BANDS
SPOTS = WIN * WIN
OCT = 8
OCT_D = OCT * HD
OCT_S = OCT * SPOTS
RIM_SLOTS = 128
EPSILON = 1e-06
MASKED = -1e30
SCALE = HD ** (-0.5)
PRECISE = lax.Precision.HIGHEST
VMEM_LIMIT = 60 * 2**20
FEED_PIECE = 1024
bf16 = jnp.bfloat16
f32 = jnp.float32
AXES = ("z", "p", "c")


def mm(a, b):
    return jnp.dot(a, b, preferred_element_type=f32)


def mm_nt(a, b):
    return lax.dot_general(a, b, (((1,), (1,)), ((), ())), preferred_element_type=f32)


def mm_tn(a, b):
    return lax.dot_general(a, b, (((0,), (0,)), ((), ())), preferred_element_type=f32)


def window_order(x):
    return (
        x.reshape(-1, WIN, BANDS // WIN, WIN, x.shape[-1])
        .transpose(0, 2, 1, 3, 4)
        .reshape(x.shape)
    )


def frame_order(x):
    return (
        x.reshape(-1, BANDS // WIN, WIN, WIN, x.shape[-1])
        .transpose(0, 2, 1, 3, 4)
        .reshape(x.shape)
    )


def window_row(token):
    group, rest = token // (WIN * BANDS), token % (WIN * BANDS)
    frame, band = rest // BANDS, rest % BANDS
    return group * (WIN * BANDS) + (band // WIN) * SPOTS + frame * WIN + band % WIN


def spread(x, block_ones):
    return jnp.concatenate([x] * OCT, axis=0) * block_ones


def own_heads(z):
    lane_head = lax.broadcasted_iota(jnp.int32, (SPOTS, 128), 1) // HD
    halves = []
    per = 128 // HD
    for t in range(OCT_D // 128):
        total = None
        for q in range(per):
            piece = z[(t * per + q) * SPOTS : (t * per + q + 1) * SPOTS, t * 128 : (t + 1) * 128]
            piece = jnp.where(lane_head == q, piece, 0.0)
            total = piece if total is None else total + piece
        halves.append(total)
    return jnp.concatenate(halves, axis=1)


def normalized(x):
    centred = x - jnp.mean(x, axis=-1, keepdims=True)
    inverse = lax.rsqrt(jnp.mean(centred * centred, axis=-1, keepdims=True) + EPSILON)
    return centred * inverse, inverse


def norm_back(grad, n, inverse):
    return inverse * (
        grad
        - jnp.mean(grad, axis=-1, keepdims=True)
        - n * jnp.mean(grad * n, axis=-1, keepdims=True)
    )


def slot_onehot(step, rows, places):
    row = lax.broadcasted_iota(jnp.int32, (rows, places.shape[1]), 0) + step * rows
    return jnp.where(row == places, 1.0, 0.0)


def head_slices(w, o):
    return slice(w * SPOTS, (w + 1) * SPOTS), slice(o * OCT_S, (o + 1) * OCT_S)


def forward_kernel(
    cut, arrived, rim, embed_w, embed_b, places, positions, mask_token, gain1, qkv_w, bias,
    across, ones, out_w, out_b, gain2, after, start_o, h_one_o, qkv_o, probs_o, context_o, middle_o,
    h_two_o, slots_s, score_s, context_s,
):
    del after
    rows, width = start_o.shape
    own = arrived.shape[0]
    step = pl.program_id(0)

    @pl.when(step == 0)
    def _():
        slots_s[0:own, :] = (mm(arrived[...], embed_w[...]) + embed_b[...]).astype(bf16)
        slots_s[own:, :] = (mm(rim[...], embed_w[...]) + embed_b[...]).astype(bf16)

    onehot = slot_onehot(step, rows, places[...])
    seen = jnp.sum(onehot, axis=1, keepdims=True)
    start = mm(onehot.astype(bf16), slots_s[...]) + (1.0 - seen) * mask_token[...] + positions[...]
    start_o[...] = start
    h_one = (normalized(start)[0] * gain1[...]).astype(bf16)
    h_one_o[...] = h_one
    qkv_o[...] = mm(h_one, qkv_w[...]).astype(bf16)
    block_ones = ones[...]
    windows = rows // SPOTS
    for w in range(windows):
        cut_w = cut[step * windows + w]
        for o in range(HEADS // OCT):
            r, s = head_slices(w, o)
            q = qkv_o[r, o * OCT_D : (o + 1) * OCT_D]
            k = qkv_o[r, width + o * OCT_D : width + (o + 1) * OCT_D]
            raw = mm_nt(k, spread(q, block_ones)) * SCALE + bias[:, s]
            score_s[r, s] = raw + cut_w * across[:, s]
    scores = score_s[...].reshape(windows, SPOTS, HEADS * SPOTS)
    expd = jnp.exp(scores - jnp.max(scores, axis=1, keepdims=True))
    probs = expd / jnp.sum(expd, axis=1, keepdims=True)
    probs_o[...] = probs.reshape(rows, HEADS * SPOTS)
    for w in range(windows):
        for o in range(HEADS // OCT):
            r, s = head_slices(w, o)
            v = qkv_o[r, 2 * width + o * OCT_D : 2 * width + (o + 1) * OCT_D]
            context_s[r, o * OCT_D : (o + 1) * OCT_D] = own_heads(mm_tn(probs_o[r, s].astype(bf16), v))
    context = context_s[...].astype(bf16)
    context_o[...] = context
    middle = start + mm(context, out_w[...]) + out_b[...]
    middle_o[...] = middle
    h_two_o[...] = (normalized(middle)[0] * gain2[...]).astype(bf16)


def rim_kernel(hot, arrived, after, out):
    del after
    out[...] = mm(hot[...], arrived[...]).astype(bf16)


def act_back_kernel(cotangent, down_w, after, out):
    del after
    out[...] = mm_nt(cotangent[...], down_w[...]).astype(bf16)


def feed_kernel(
    h_two, cotangent, grad_act, up_w, up_b, act_o, grad_h_o, down_o, up_o, bias_o, down_s, up_s
):
    step = pl.program_id(0)

    @pl.when(step == 0)
    def _():
        down_s[...] = jnp.zeros_like(down_s)
        up_s[...] = jnp.zeros_like(up_s)
        bias_o[...] = jnp.zeros_like(bias_o)

    h = h_two[...]
    cot = cotangent[...]
    hidden = up_w.shape[1]
    piece = min(FEED_PIECE, hidden)
    grad_h = None
    for at in range(0, hidden, piece):
        f = slice(at, at + piece)
        up_value = mm(h, up_w[:, f]) + up_b[:, f]
        below = 0.5 * (1.0 + lax.erf(up_value * (0.5**0.5)))
        act = (up_value * below).astype(bf16)
        act_o[:, f] = act
        slope = below + up_value * (jnp.exp(-0.5 * up_value * up_value) * 0.3989422804014327)
        grad_up = grad_act[:, f].astype(f32) * slope
        bias_o[:, f] += jnp.sum(grad_up, axis=0, keepdims=True)
        grad_low = grad_up.astype(bf16)
        down_s[f, :] += mm_tn(act, cot)
        up_s[:, f] += mm_tn(h, grad_low)
        part = mm_nt(grad_low, up_w[:, f])
        grad_h = part if grad_h is None else grad_h + part
    grad_h_o[...] = grad_h

    @pl.when(step == pl.num_programs(0) - 1)
    def _():
        down_o[...] = down_s[...].astype(bf16)
        up_o[...] = up_s[...].astype(bf16)


def attend_back_kernel(
    core, grad_h, cotangent, middle, context, qkv, probs, h_one, gain2, out_w, ones, gqkv_o,
    grad_middle_o, keep_o, send_o, sums_o, rel_o, out_s, qkv_s, score_s,
):
    step = pl.program_id(0)
    rows, width = middle.shape
    windows = rows // SPOTS

    @pl.when(step == 0)
    def _():
        out_s[...] = jnp.zeros_like(out_s)
        qkv_s[...] = jnp.zeros_like(qkv_s)
        sums_o[...] = jnp.zeros_like(sums_o)
        rel_o[...] = jnp.zeros_like(rel_o)

    cot = cotangent[...].astype(f32)
    grad_h_two = grad_h[...]
    n2, r2 = normalized(middle[...])
    sums_o[0:1, :] += jnp.sum(grad_h_two * n2, axis=0, keepdims=True)
    grad_middle = cot + norm_back(grad_h_two * gain2[...], n2, r2)
    grad_middle_o[...] = grad_middle
    sums_o[1:2, :] += jnp.sum(grad_middle, axis=0, keepdims=True)
    sums_o[2:3, :] += jnp.sum(cot, axis=0, keepdims=True)
    grad_middle_low = grad_middle.astype(bf16)
    out_s[...] += mm_tn(context[...], grad_middle_low)
    grad_context = mm_nt(grad_middle_low, out_w[...]).astype(bf16)
    block_ones = ones[...]
    for w in range(windows):
        for o in range(HEADS // OCT):
            r, s = head_slices(w, o)
            heads = slice(o * OCT_D, (o + 1) * OCT_D)
            v_at = slice(2 * width + o * OCT_D, 2 * width + (o + 1) * OCT_D)
            wide = spread(grad_context[r, heads], block_ones)
            score_s[r, s] = mm_nt(qkv[r, v_at], wide)
            gqkv_o[r, v_at] = mm(probs[r, s].astype(bf16), wide).astype(bf16)
    pr = probs[...].reshape(windows, SPOTS, HEADS * SPOTS)
    grad_probs = score_s[...].reshape(windows, SPOTS, HEADS * SPOTS)
    delta = jnp.sum(grad_probs * pr, axis=1, keepdims=True)
    grad_scores = pr * (grad_probs - delta)
    rel_o[...] += jnp.sum(grad_scores, axis=0)
    score_s[...] = grad_scores.reshape(rows, HEADS * SPOTS)
    for w in range(windows):
        for o in range(HEADS // OCT):
            r, s = head_slices(w, o)
            q_at = slice(o * OCT_D, (o + 1) * OCT_D)
            k_at = slice(width + o * OCT_D, width + (o + 1) * OCT_D)
            low = score_s[r, s].astype(bf16)
            gqkv_o[r, q_at] = (own_heads(mm_tn(low, qkv[r, k_at])) * SCALE).astype(bf16)
            gqkv_o[r, k_at] = (mm(low, spread(qkv[r, q_at], block_ones)) * SCALE).astype(bf16)
    qkv_s[...] += mm_tn(h_one[...], gqkv_o[...])

    def give(low_o, high_o):
        low_o[0:width, :] = qkv_s[:, 0:width].astype(bf16)
        low_o[width : 2 * width, :] = qkv_s[:, width : 2 * width].astype(bf16)
        high_o[0:width, :] = qkv_s[:, 2 * width : 3 * width].astype(bf16)
        high_o[width : 2 * width, :] = out_s[...].astype(bf16)

    last = step == pl.num_programs(0) - 1

    @pl.when(last & (core[0] == 0))
    def _():
        give(keep_o, send_o)

    @pl.when(last & (core[0] == 1))
    def _():
        give(send_o, keep_o)


def scatter_back_kernel(
    core, gqkv, start, grad_middle, places, qkv_w, gain1, arrived, rim, sums, rel, up_bias,
    slots_o, keep_o, send_o, slots_s, embed_s, sums_s,
):
    step = pl.program_id(0)
    rows, width = start.shape
    own, e_in = arrived.shape

    @pl.when(step == 0)
    def _():
        slots_s[...] = jnp.zeros_like(slots_s)
        sums_s[...] = jnp.zeros_like(sums_s)
        embed_s[...] = jnp.zeros_like(embed_s)

    grad_h_one = mm_nt(gqkv[...], qkv_w[...])
    n1, r1 = normalized(start[...])
    sums_s[3:4, :] += jnp.sum(grad_h_one * n1, axis=0, keepdims=True)
    grad_start = grad_middle[...] + norm_back(grad_h_one * gain1[...], n1, r1)
    onehot = slot_onehot(step, rows, places[...])
    hidden = 1.0 - jnp.sum(onehot, axis=1, keepdims=True)
    sums_s[4:5, :] += jnp.sum(hidden * grad_start, axis=0, keepdims=True)
    slots_s[...] += mm_tn(onehot.astype(bf16), grad_start.astype(bf16))

    def give(low_o, high_o):
        half = low_o.shape[0]
        low_o[...] = embed_s[0:half, :].astype(bf16)
        left = e_in - half
        high_o[...] = jnp.zeros_like(high_o)
        if left > 0:
            high_o[0:left, :] = embed_s[half:e_in, :].astype(bf16)
        left = max(left, 0)
        high_o[left : left + 16, :] = sums_s[...].astype(bf16)
        high_o[left + 16 : left + 16 + SPOTS, 0 : HEADS * SPOTS] = rel[...].astype(bf16)

    last = step == pl.num_programs(0) - 1

    @pl.when(last)
    def _():
        slots = slots_s[...].astype(bf16)
        slots_o[...] = slots
        embed_s[0:e_in, :] = mm_tn(arrived[...], slots[0:own]) + mm_tn(rim[...], slots[own:])
        sums_s[0:3, :] = sums[0:3, :]
        sums_s[5:6, :] = jnp.sum(slots.astype(f32), axis=0, keepdims=True)
        for block in range(up_bias.shape[1] // width):
            sums_s[6 + block : 7 + block, :] = up_bias[:, block * width : (block + 1) * width]

    @pl.when(last & (core[0] == 0))
    def _():
        give(keep_o, send_o)

    @pl.when(last & (core[0] == 1))
    def _():
        give(send_o, keep_o)


def prepare_kernel(cotangent, next_cot, pos_embed, order, cot_o, positions_o):
    block = order.shape[0]
    tokens = cotangent.shape[0]
    for at in range(0, tokens, block):
        if at + block < tokens:
            rows = cotangent[at + RIM : at + RIM + block, :]
        else:
            rows = jnp.concatenate([cotangent[at + RIM :, :], next_cot[...]], axis=0)
        cot_o[at : at + block, :] = mm(order[...].astype(bf16), rows).astype(bf16)
    grid_rows = pos_embed.shape[0]
    for at in range(0, grid_rows, block):
        if at + block < grid_rows:
            rows = pos_embed[at + RIM : at + RIM + block, :]
        else:
            rows = jnp.concatenate([pos_embed[at + RIM :, :], pos_embed[0:RIM, :]], axis=0)
        positions_o[at : at + block, :] = jnp.dot(
            order[...], rows, precision=PRECISE, preferred_element_type=f32
        )


def out_kernel(
    middle, act, down, down_bias, order, after, out_o, rim_o
):
    del after
    step = pl.program_id(0)
    last = pl.num_programs(0) - 1
    rows = middle.shape[0]
    block = order.shape[0]
    result = (
        middle[...] + mm(act[...], down[...]) + down_bias[...]
    ).astype(bf16)
    result = jnp.concatenate(
        [mm_tn(order[...], result[b : b + block]).astype(bf16) for b in range(0, rows, block)],
        axis=0,
    )

    @pl.when(step < last)
    def _():
        out_o[pl.ds(pl.multiple_of(step * rows + RIM, RIM), rows), :] = result

    @pl.when(step == last)
    def _():
        out_o[pl.ds(pl.multiple_of(step * rows + RIM, RIM), rows - RIM), :] = result[: rows - RIM]
        rim_o[...] = result[rows - RIM :]
        out_o[0:RIM, :] = jnp.zeros((RIM, result.shape[1]), bf16)


def chip_sum_kernel(*refs):
    parts, out = refs[:-1], refs[-1]
    cells = out.shape[0]
    at = 0
    for keep, got in zip(parts[::2], parts[1::2]):
        total = (keep[...].astype(f32) + got[...].astype(f32)).astype(bf16)
        rows = total.shape[0] // cells
        out[:, at : at + rows, :] = total.reshape(cells, rows, total.shape[1])
        at += rows


def plane_sum_kernel(plane, part, after, *outs):
    del after
    total_s = outs[-1]
    outs = outs[:-1]
    total_s[...] = jnp.sum(part[...].astype(f32), axis=0)
    rows = outs[0].shape[0]
    for b, out in enumerate(outs):
        at = pl.multiple_of(lax.bitwise_xor(plane[0], b) * rows, 8)
        out[...] = total_s[pl.ds(at, rows), :].astype(bf16)


def z_sum_kernel(*refs):
    total = refs[0][...].astype(f32)
    for ref in refs[1:-1]:
        total = total + ref[...].astype(f32)
    refs[-1][...] = total.astype(bf16)


def z_join_kernel(plane, *refs):
    out = refs[-1]
    for b, ref in enumerate(refs[:-2]):
        share = ref[...]
        at = lax.bitwise_xor(plane[0], b)
        for cell in range(out.shape[0]):
            out[cell, at] = share


def rest_unpack_kernel(split, core, mine, other, qkv_o, out_o, embed_o, *small_o):
    width = out_o.shape[1]
    e_in = embed_o.shape[0]

    def give(low, high):
        rows = low[:, 0:split].reshape(-1, width).astype(f32)
        qkv_o[:, 0:width] = rows[0:width]
        qkv_o[:, width : 2 * width] = rows[width:]
        rows = high[:, 0:split].reshape(-1, width).astype(f32)
        qkv_o[:, 2 * width :] = rows[0:width]
        out_o[...] = rows[width:]
        rows = low[:, split:].reshape(-1, width).astype(f32)
        half = rows.shape[0]
        embed_o[0 : min(half, e_in), :] = rows[0 : min(half, e_in)]
        rows = high[:, split:].reshape(-1, width).astype(f32)
        left = max(e_in - half, 0)
        if left:
            embed_o[half:e_in, :] = rows[0:left]
        for i, vector_o in enumerate(small_o[:6]):
            vector_o[...] = rows[left + i]
        up_bias_o, rel_o = small_o[6:]
        for i in range(up_bias_o.shape[0] // width):
            up_bias_o[i * width : (i + 1) * width] = rows[left + 6 + i]
        rel_o[...] = rows[left + 16 : left + 16 + SPOTS, 0 : HEADS * SPOTS]

    @pl.when(core[0] == 0)
    def _():
        give(mine, other)

    @pl.when(core[0] == 1)
    def _():
        give(other, mine)


def widen_kernel(down, up, down_o, up_o):
    down_o[...] = down[...].astype(f32)
    up_o[...] = up[...].astype(f32)


ANY = pl.BlockSpec(memory_space=pl.ANY)
SMEM = pl.BlockSpec(memory_space=pltpu.SMEM)


def whole(s):
    return pl.BlockSpec(s, lambda *i: (0,) * len(s))


def tile(rows, width, first=0):
    return pl.BlockSpec((rows, width), lambda i: (i + first, 0))


def params():
    return pltpu.CompilerParams(vmem_limit_bytes=VMEM_LIMIT)


def shape(s, d):
    return jax.ShapeDtypeStruct(s, d)


def at_once(kernel, args, outs, specs=None, scratch=()):
    if specs is None:
        specs = [whole(a.shape) for a in args]
    many = isinstance(outs, (list, tuple))
    out_specs = [whole(o.shape) for o in outs] if many else whole(outs.shape)
    return pl.pallas_call(
        kernel,
        grid=(1,),
        in_specs=specs,
        out_specs=out_specs,
        out_shape=outs,
        scratch_shapes=list(scratch),
        compiler_params=params(),
    )(*args)


def swap_cores(x):
    return lax.ppermute(x, "c", [(0, 1), (1, 0)])


def exchange(x, axis):
    return lax.all_to_all(x, axis, 0, 0, tiled=True)


def across_z(x, bit):
    return lax.ppermute(x, "z", [(i, i ^ bit) for i in range(lax.axis_size("z"))])


def chip_shares(pairs):
    cells = lax.axis_size("p")
    refs = [a for keep, send in pairs for a in (keep, swap_cores(send))]
    rows = sum(keep.shape[0] for keep, _ in pairs) // cells
    return at_once(chip_sum_kernel, refs, shape((cells, rows, refs[0].shape[1]), bf16))


def tree(shares, plane, after, after_z):
    cells, rows, width = shares.shape
    planes = lax.axis_size("z")
    part = exchange(shares, "p")
    sums = at_once(
        plane_sum_kernel,
        (plane, part, after),
        [shape((rows // planes, width), bf16)] * planes,
        [SMEM, whole(part.shape), ANY],
        [pltpu.VMEM((rows, width), f32)],
    )
    total = at_once(
        z_sum_kernel,
        [sums[0]] + [across_z(sums[b], b) for b in range(1, planes)],
        shape(sums[0].shape, bf16),
    )
    shares_z = [total] + [across_z(total, b) for b in range(1, planes)]
    joined = at_once(
        z_join_kernel,
        [plane, *shares_z, after_z],
        shape((cells, planes, rows // planes, width), bf16),
        [SMEM] + [whole(total.shape)] * planes + [ANY],
    )
    return exchange(joined, "p")


def order_matrix(block):
    token = np.arange(block)
    group, rest = token // (WIN * BANDS), token % (WIN * BANDS)
    frame, band = rest // BANDS, rest % BANDS
    row = group * (WIN * BANDS) + (band // WIN) * SPOTS + frame * WIN + band % WIN
    matrix = np.zeros((block, block), np.float32)
    matrix[row, token] = 1.0
    return matrix


def per_device(
    visible, embed_weight, embed_bias, mask_token, pos_embed, norm1_gain, qkv_weight, rel_table,
    out_weight, out_bias, norm2_gain, up_weight, up_bias, down_weight, down_bias, cotangent,
    visible_index, slot_counts, segment_ids,
):
    device_count = lax.axis_size(AXES)
    device_rank = lax.axis_index(AXES)
    core = lax.axis_index("c").reshape(1).astype(jnp.int32)
    plane = lax.axis_index("z").reshape(1).astype(jnp.int32)
    planes, cells = lax.axis_size("z"), lax.axis_size("p")
    tokens, width = cotangent.shape
    frames = tokens // BANDS
    hidden = down_weight.shape[0]
    e_in = visible.shape[1]
    slot_rows = visible_index.shape[2]
    slots = device_count * slot_rows
    ext = slots + RIM_SLOTS
    back = [(i, (i - 1) % device_count) for i in range(device_count)]
    ahead = [(i, (i + 1) % device_count) for i in range(device_count)]
    row = lambda v: v.reshape(1, -1)

    arrived = exchange(visible, AXES)

    spot = visible_index.reshape(slots)
    live = (
        jnp.arange(slot_rows)[None, :] < slot_counts.reshape(device_count, 1)
    ).reshape(slots)
    rim_hot = ((jnp.arange(RIM)[:, None] == spot[None, :]) & live[None, :]).astype(bf16)
    rim_seen = jnp.sum(rim_hot.astype(f32), axis=1, keepdims=True).astype(bf16)
    sent_back = jnp.concatenate(
        [cotangent[:RIM], jnp.broadcast_to(rim_seen, (RIM, width))], axis=0
    )
    from_next = lax.ppermute(sent_back, AXES, back)
    next_seen = from_next[RIM:, 0].astype(f32)
    own_places = jnp.where(live & (spot >= RIM), window_row(spot - RIM), -1)
    rim_places = jnp.where(
        next_seen > 0.5, window_row(tokens - RIM + np.arange(RIM)), -1
    )
    places = jnp.concatenate(
        [own_places, rim_places, np.full((RIM_SLOTS - RIM,), -1, np.int32)]
    ).reshape(1, ext).astype(jnp.int32)

    seg_cycle = jnp.concatenate([segment_ids, segment_ids[:SHIFT]])
    seg_tape = lax.dynamic_slice_in_dim(seg_cycle, device_rank * frames + SHIFT, frames)
    seg_win = seg_tape.reshape(frames // WIN, WIN)
    cut = jnp.repeat(
        (seg_win[:, SHIFT - 1] != seg_win[:, SHIFT]).astype(f32), BANDS // WIN
    )

    spots = np.arange(SPOTS)
    frame_of, band_of = spots // WIN, spots % WIN
    rels = 2 * WIN - 1
    rel_index = (frame_of[:, None] - frame_of[None, :] + WIN - 1) * rels + (
        band_of[:, None] - band_of[None, :] + WIN - 1
    )
    rel_hot = (rel_index[:, :, None] == np.arange(rels * rels)).astype(np.float32)
    bias = jnp.einsum("hr,ijr->jhi", rel_table, rel_hot, precision=PRECISE).reshape(
        SPOTS, HEADS * SPOTS
    )
    halves = frame_of // SHIFT
    across = np.tile(
        np.where(halves[:, None] != halves[None, :], MASKED, 0.0).astype(np.float32), (1, HEADS)
    )
    ones = jnp.asarray(
        np.arange(OCT_S)[:, None] // SPOTS == np.arange(OCT_D)[None, :] // HD, bf16
    )
    order = order_matrix(256)
    cot, positions = at_once(
        prepare_kernel,
        (cotangent, from_next[:RIM], pos_embed, order),
        [shape(cotangent.shape, bf16), shape(pos_embed.shape, f32)],
    )

    tm = min(512, tokens)
    steps = tokens // tm
    grid = (steps,)
    pos_blocks = pos_embed.shape[0] // tm
    forward_outs = [
        (width, f32), (width, bf16), (3 * width, bf16), (HEADS * SPOTS, f32), (width, bf16),
        (width, f32), (width, bf16),
    ]

    rim_rows = at_once(
        rim_kernel,
        (rim_hot, arrived, cot),
        shape((RIM, e_in), bf16),
        [whole(rim_hot.shape), whole(arrived.shape), ANY],
    )
    next_rows = lax.ppermute(rim_rows, AXES, back)
    grad_act = pl.pallas_call(
        act_back_kernel,
        grid=grid,
        in_specs=[tile(tm, width), whole((hidden, width)), ANY],
        out_specs=tile(tm, hidden),
        out_shape=shape((tokens, hidden), bf16),
        compiler_params=params(),
    )(cot, down_weight, rim_rows)
    rim = jnp.pad(next_rows, ((0, RIM_SLOTS - RIM), (0, 0)))
    forward_args = [
        cut, arrived, rim, embed_weight, row(embed_bias), places, positions, row(mask_token),
        row(norm1_gain), qkv_weight, bias, across, ones, out_weight, row(out_bias),
        row(norm2_gain), grad_act,
    ]
    specs = [SMEM] + [whole(a.shape) for a in forward_args[1:-1]] + [ANY]
    specs[6] = pl.BlockSpec((tm, width), lambda i: (lax.rem(i, pos_blocks), 0))
    start, h_one, qkv, probs, context, middle, h_two = pl.pallas_call(
        forward_kernel,
        grid=grid,
        in_specs=specs,
        out_specs=[tile(tm, w) for w, _ in forward_outs],
        out_shape=[shape((tokens, w), d) for w, d in forward_outs],
        scratch_shapes=[
            pltpu.VMEM((ext, width), bf16),
            pltpu.VMEM((tm, HEADS * SPOTS), f32),
            pltpu.VMEM((tm, width), f32),
        ],
        compiler_params=params(),
    )(*forward_args)

    act, grad_h, down_grad, up_grad, up_bias_grad = pl.pallas_call(
        feed_kernel,
        grid=grid,
        in_specs=[
            tile(tm, width),
            tile(tm, width),
            tile(tm, hidden),
            whole((width, hidden)),
            whole((1, hidden)),
        ],
        out_specs=[
            tile(tm, hidden),
            tile(tm, width),
            whole((hidden, width)),
            whole((width, hidden)),
            whole((1, hidden)),
        ],
        out_shape=[
            shape((tokens, hidden), bf16),
            shape((tokens, width), f32),
            shape((hidden, width), bf16),
            shape((width, hidden), bf16),
            shape((1, hidden), f32),
        ],
        scratch_shapes=[pltpu.VMEM((hidden, width), f32), pltpu.VMEM((width, hidden), f32)],
        compiler_params=params(),
    )(h_two, cot, grad_act, up_weight, row(up_bias))
    down_sum, up_sum = lax.psum((down_grad, up_grad), AXES)

    def rest(operands):
        (
            grad_h, cot, middle, context, qkv, probs, h_one, start, act, up_bias_grad, places,
            arrived, rim, rim_hot,
        ) = operands
        gqkv, grad_middle, keep_c, send_c, sums, rel_sum = pl.pallas_call(
            attend_back_kernel,
            grid=grid,
            in_specs=[
                SMEM,
                tile(tm, width),
                tile(tm, width),
                tile(tm, width),
                tile(tm, width),
                tile(tm, 3 * width),
                tile(tm, HEADS * SPOTS),
                tile(tm, width),
                whole((1, width)),
                whole((width, width)),
                whole((OCT_S, OCT_D)),
            ],
            out_specs=[
                tile(tm, 3 * width),
                tile(tm, width),
                whole((2 * width, width)),
                whole((2 * width, width)),
                whole((8, width)),
                whole((SPOTS, HEADS * SPOTS)),
            ],
            out_shape=[
                shape((tokens, 3 * width), bf16),
                shape((tokens, width), f32),
                shape((2 * width, width), bf16),
                shape((2 * width, width), bf16),
                shape((8, width), f32),
                shape((SPOTS, HEADS * SPOTS), f32),
            ],
            scratch_shapes=[
                pltpu.VMEM((width, width), f32),
                pltpu.VMEM((width, 3 * width), f32),
                pltpu.VMEM((tm, HEADS * SPOTS), f32),
            ],
            compiler_params=params(),
        )(
            core, grad_h, cot, middle, context, qkv, probs, h_one, row(norm2_gain),
            out_weight, ones,
        )

        unit = 16 * planes * cells
        half = -(-width // unit) * unit
        grad_slots, keep_d, send_d = pl.pallas_call(
            scatter_back_kernel,
            grid=grid,
            in_specs=[
                SMEM,
                tile(tm, 3 * width),
                tile(tm, width),
                tile(tm, width),
                whole((1, ext)),
                whole((width, 3 * width)),
                whole((1, width)),
                whole((slots, e_in)),
                whole((RIM_SLOTS, e_in)),
                whole((8, width)),
                whole((SPOTS, HEADS * SPOTS)),
                whole((1, hidden)),
            ],
            out_specs=[whole((ext, width)), whole((half, width)), whole((half, width))],
            out_shape=[shape((ext, width), bf16), shape((half, width), bf16), shape((half, width), bf16)],
            scratch_shapes=[
                pltpu.VMEM((ext, width), f32),
                pltpu.VMEM((max(e_in, half), width), f32),
                pltpu.VMEM((16, width), f32),
            ],
            compiler_params=params(),
        )(
            core, gqkv, start, grad_middle, places, qkv_weight, row(norm1_gain), arrived, rim, sums,
            rel_sum, up_bias_grad,
        )
        shares = chip_shares([(keep_c, send_c), (keep_d, send_d)])
        rim_grad = lax.ppermute(grad_slots[slots : slots + RIM], AXES, ahead)

        out, rim_out = pl.pallas_call(
            out_kernel,
            grid=grid,
            in_specs=[
                tile(tm, width),
                tile(tm, hidden),
                whole((hidden, width)),
                whole((1, width)),
                whole(order.shape),
                ANY,
            ],
            out_specs=[whole((tokens, width)), whole((RIM, width))],
            out_shape=[shape((tokens, width), bf16), shape((RIM, width), bf16)],
            compiler_params=params(),
        )(middle, act, down_weight, row(down_bias), jnp.asarray(order, bf16), shares)

        grad_embedded = (
            grad_slots[:slots].astype(f32)
            + lax.dot_general(rim_hot, rim_grad, (((0,), (0,)), ((), ())), preferred_element_type=f32)
        ).astype(bf16)
        returned = exchange(grad_embedded, AXES)
        grad_visible = lax.dot_general(
            returned, embed_weight, (((1,), (1,)), ((), ())), preferred_element_type=f32
        ).astype(bf16)
        rest_all = tree(shares, plane, rim_out, returned).reshape(cells, -1, width)
        first_rows = lax.ppermute(rim_out, AXES, ahead)
        out = lax.dynamic_update_slice(out, first_rows, (0, 0))

        return out, grad_visible, rest_all, swap_cores(rest_all)

    def nothing(operands):
        return tuple(jnp.zeros(o.shape, o.dtype) for o in jax.eval_shape(rest, operands))

    operands = (
        grad_h, cot, middle, context, qkv, probs, h_one, start, act, up_bias_grad, places,
        arrived, rim, rim_hot,
    )
    out, grad_visible, mine, other = lax.cond(device_rank < device_count, rest, nothing, operands)

    vector = shape((width,), f32)
    (
        grad_qkv_weight, grad_out_weight, grad_embed_weight, grad_norm2_gain, grad_out_bias,
        grad_down_bias, grad_norm1_gain, grad_mask_token, grad_embed_bias, grad_up_bias, rel_sums,
    ) = at_once(
        partial(rest_unpack_kernel, 2 * width // cells),
        (core, mine, other),
        [
            shape((width, 3 * width), f32),
            shape((width, width), f32),
            shape((e_in, width), f32),
            *[vector] * 6,
            shape((hidden,), f32),
            shape((SPOTS, HEADS * SPOTS), f32),
        ],
        [SMEM, whole(mine.shape), whole(other.shape)],
    )
    grad_rel = jnp.einsum(
        "jhi,ijr->hr", rel_sums.reshape(SPOTS, HEADS, SPOTS), rel_hot, precision=PRECISE
    )
    grad_down_weight, grad_up_weight = pl.pallas_call(
        widen_kernel,
        grid=(4,),
        in_specs=[tile(hidden // 4, width), tile(width // 4, hidden)],
        out_specs=[tile(hidden // 4, width), tile(width // 4, hidden)],
        out_shape=[shape((hidden, width), f32), shape((width, hidden), f32)],
        compiler_params=params(),
    )(down_sum, up_sum)
    return (
        out,
        grad_visible,
        grad_embed_weight,
        grad_embed_bias,
        grad_mask_token,
        grad_norm1_gain,
        grad_qkv_weight,
        grad_rel,
        grad_out_weight,
        grad_out_bias,
        grad_norm2_gain,
        grad_up_weight,
        grad_up_bias,
        grad_down_weight,
        grad_down_bias,
    )


def solution(mesh):
    planes = 4
    grid = Mesh(mesh.devices.reshape(planes, -1, 2), AXES)
    split = P(AXES)
    in_specs = (split,) + (P(),) * 14 + (split, split, split, P())
    out_specs = (split, split) + (P(),) * 13
    return jax.shard_map(
        per_device, mesh=grid, in_specs=in_specs, out_specs=out_specs, check_vma=False
    )
```

time: 354 us -> 282 us (0.80)
  waiting for transfers between devices: 84.2 us -> 48.3 us
  Pallas kernels: 152 us -> 134 us
  starting transfers between devices: 55.3 us -> 37.4 us
  between operations: 0.95 us -> 14.2 us
  local copies, waits for them, and re-layouts: 17.1 us -> 9.35 us
  blocking collectives: 33.9 us -> 30.3 us
    all_to_all x10 -> x3, waiting for transfers between devices: 63.3 us -> 15.2 us  [exchange(): return lax.all_to_all(x, axis, 0, 0, tiled=True)]
    all_to_all x10 -> x3, starting transfers between devices: 45.9 us -> 18.1 us  [exchange(): return lax.all_to_all(x, axis, 0, 0, tiled=True)]
    pallas_call x13 -> x7, Pallas kernels: 39.1 us -> 20 us  [at_once(): pl.pallas_call(kernel, grid=(1,), in_specs=specs, out_specs=out_specs, ou...]
    ppermute x2 -> x8, waiting for transfers between devices: 14.6 us -> 30.1 us  [the longest x6 18.8 us: across_z(): lax.ppermute(x, 'z', [(i, i ^ bit) for i in range(lax.axis_size('z'))])]
    ppermute x2 -> x8, starting transfers between devices: 0.79 us -> 9.7 us  [the longest x6 8.77 us: across_z(): lax.ppermute(x, 'z', [(i, i ^ bit) for i in range(lax.axis_size('z'))])]
    unnamed x41 -> x21, local copies, waits for them, and re-layouts: 7.6 us -> 1.47 us
    all_to_all x2 -> x1, blocking collectives: 33.9 us -> 30.3 us  [exchange(): return lax.all_to_all(x, axis, 0, 0, tiled=True)]
  transfers between devices with their start and end apart: 20 -> 17, of which waited for: 12 -> 10; matrix products, arithmetic and copies ran while one was open for 5% -> 5% of each run, Pallas kernels for 28% -> 27%
where the time goes in v2:
time: 282 us; the launch traced here: 281 us
  Pallas kernels  134 us (48%)
  waiting for transfers between devices  48.3 us (17%)
  starting transfers between devices  37.4 us (13%)
  blocking collectives  30.3 us (11%)
  between operations  14.2 us (5%)
  local copies, waits for them, and re-layouts  9.35 us (3%)
  matrix products  4.8 us (2%)
    all_to_all x1, blocking collectives, exchange(): return lax.all_to_all(x, axis, 0, 0, tiled=True)  30.3 us
    pallas_call x1, Pallas kernels, per_device(): pl.pallas_call(feed_kernel, grid=grid, in_specs=[tile(tm, width), tile(tm...  27.9 us
    pallas_call x1, Pallas kernels, rest(): pl.pallas_call(attend_back_kernel, grid=grid, in_specs=[SMEM, tile(tm, wi...  26.7 us
    pallas_call x1, Pallas kernels, per_device(): pl.pallas_call(forward_kernel, grid=grid, in_specs=specs, out_specs=[tile...  22.6 us
    pallas_call x7, Pallas kernels, at_once(): pl.pallas_call(kernel, grid=(1,), in_specs=specs, out_specs=out_specs, ou...  20 us
    ppermute x6, waiting for transfers between devices, across_z(): lax.ppermute(x, 'z', [(i, i ^ bit) for i in range(lax.axis_size('z'))])  18.8 us
    all_to_all x3, starting transfers between devices, exchange(): return lax.all_to_all(x, axis, 0, 0, tiled=True)  18.1 us
    all_to_all x3, waiting for transfers between devices, exchange(): return lax.all_to_all(x, axis, 0, 0, tiled=True)  15.2 us
  transfers between devices with their start and end apart: 17, of which 10 were waited for; matrix products, arithmetic and copies ran while one was open for 5% of the time, Pallas kernels for 27%

profile of v2, /device:TPU:0, one launch (start us, length us, event | category | flops | bytes accessed | tf_op | source)
XLA Modules:
  0.0 280.8 jit_solution(8809983273521948322)
XLA Ops:
  7.2 7.3 %all-to-all-start.3 = ((bf16[32,16,768]{2,1,0:T(8,128)(2,1)}), bf16[32,16,768]{2,1,0:T(8,128)(2,1)S(1)}, u32[]{:S(2)}, u32[]{:S(2)}) async-start(bf16[32,16,768]{2,1,0:T(8,128)(2,1)} %bitcast.42), calls=%async_computation.3 | async-start | bytes 1572864 | tf_op jit(solution)/shard_map/all_to_all | solution.py:492
  17.2 5.2 %collective-permute-start.11 = (bf16[32,512]{1,0:T(8,128)(2,1)S(1)}, bf16[32,512]{1,0:T(8,128)(2,1)S(1)}, u32[]{:S(2)}, u32[]{:S(2)}) collective-permute-start(bf16[32,512]{1,0:T(8,128)(2,1)S(1)} %pad_maximum_fusion), channel_id=1, source_target_pairs={{0,31},{1,0},{2,1},{3,2},{4,3},{5,4},{6,5},{7,6},{8,7},{9,8},{10,9... | collective-permute-start | bytes 98312 | tf_op jit(solution)/shard_map/ppermute | solution.py:574
  28.8 4.5 %shard_map.372 = (bf16[2048,512]{1,0:T(8,128)(2,1)S(1)}, f32[512,512]{1,0:T(8,128)}) custom-call(bf16[2048,512]{1,0:T(8,128)(2,1)} %cotangent.1, bf16[16,512]{1,0:T(8,128)(2,1)} %slice.32.next_cot, f32[512,512]{1,0:T(8,128)} %pos_embed.1, f32[256,256]{1,0:T(8,128)} %constant.122.clone.order), custom_call_target="tpu_custom_call" | custom-call | tf_op jit(solution)/shard_map/pallas_call | solution.py:476
  36.0 3.9 %collective-permute-start.12 = (bf16[16,768]{1,0:T(8,128)(2,1)}, bf16[16,768]{1,0:T(8,128)(2,1)S(1)}, u32[]{:S(2)}, u32[]{:S(2)}) collective-permute-start(bf16[16,768]{1,0:T(8,128)(2,1)} %shard_map.373.after), channel_id=1, source_target_pairs={{0,31},{1,0},{2,1},{3,2},{4,3},{5,4},{6,5},{7,6},{8,7},{9,8},{10,9... | collective-permute-start | bytes 73736 | tf_op jit(solution)/shard_map/ppermute | solution.py:630
  40.0 8.3 %shard_map.374.after.grad_act = bf16[2048,2048]{1,0:T(8,128)(2,1)} custom-call(bf16[2048,512]{1,0:T(8,128)(2,1)S(1)} %get-tuple-element.136.after.cotangent, bf16[2048,512]{1,0:T(8,128)(2,1)} %down_w.1, bf16[16,768]{1,0:T(8,128)(2,1)} %shard_map.373.after), custom_call_target="tpu_custom_call" | custom-call | tf_op jit(solution)/shard_map/pallas_call | solution.py:631
  48.3 22.6 %shard_map.375 = (f32[2048,512]{1,0:T(8,128)}, bf16[2048,512]{1,0:T(8,128)(2,1)}, bf16[2048,1536]{1,0:T(8,128)(2,1)}, f32[2048,256]{1,0:T(8,128)}, bf16[2048,512...) custom-call(f32[128]{0:T(128)} %reshape.118.cut, bf16[512,768]{1,0:T(8,128)(2,1)S(1)} %bitcast.38, ...), custom_call_target="tpu_custom_call" | custom-call | tf_op jit(solution)/shard_map/pallas_call | solution.py:647
  70.9 27.9 %shard_map.376 = (bf16[2048,2048]{1,0:T(8,128)(2,1)}, f32[2048,512]{1,0:T(8,128)}, bf16[2048,512]{1,0:T(8,128)(2,1)}, bf16[512,2048]{1,0:T(8,128)(2,1)}, f32[1,2048]{1,0:T(1,128)S(1)}) custom-call(bf16[2048,512]{1,0:T(8,128)(2,1)} %get-tuple-element.138.h_two, bf16[2048,512]{1,0:T(8,128)(2,1)S(1)} %get-tuple-element.136.after.cotangent, ...), custom_call_target="tpu_custom_call" | custom-call | tf_op jit(solution)/shard_map/pallas_call | solution.py:661
  99.5 161.9 %conditional.1 = (bf16[2048,512]{1,0:T(8,128)(2,1)}, bf16[512,768]{1,0:T(8,128)(2,1)}, bf16[4,384,512]{2,1,0:T(8,128)(2,1)}, bf16[4,384,512]{2,1,0:T(8,128)(2,1)}) conditional(s32[]{:T(128)} %convert_element_type.34, () %tuple.16, (f32[512]{0:T(512)S(1)}, f32[512]{0:T(512)S(1)}, s32[1]{0:T(128)}, f32[2048,512]{1,0:T(8,128)}, ...), branch_computations={%region_1.2_spmd, %region_2.3_spmd} | conditional | flops 412221440 | bytes 55608252 | solution.py:809
  99.5 26.7 %branch_1_fun.7 = (bf16[2048,1536]{1,0:T(8,128)(2,1)}, f32[2048,512]{1,0:T(8,128)}, bf16[1024,512]{1,0:T(8,128)(2,1)}, bf16[1024,512]{1,0:T(8,128)(2,1)}, f32[8,512]{1,0:T(8,128)}, /*index=5*/f32[16,256]{1,0:T(8,128)}) custom-call(s32[1]{0:T(128)} %get-tuple-element.55.core, f32[2048,512]{1,0:T(8,128)} %get-tuple-element.56.grad_h, ...), custom_call_target="tpu_custom_call" | custom-call | tf_op jit(solution)/shard_map/cond/branch_1_fun/pallas_call | solution.py:695
  126.3 13.0 %branch_1_fun.8 = (bf16[640,512]{1,0:T(8,128)(2,1)}, bf16[512,512]{1,0:T(8,128)(2,1)}, bf16[512,512]{1,0:T(8,128)(2,1)}) custom-call(s32[1]{0:T(128)} %get-tuple-element.55.core, bf16[2048,1536]{1,0:T(8,128)(2,1)} %get-tuple-element.67.gqkv, f32[2048,512]{1,0:T(8,128)} %get-tuple-element.68.start, f32[2048,512]{1,0:T(8,128)} %get-tuple-element.69.grad_middle, ...), custom_call_target="tpu_custom_call" | custom-call | tf_op jit(solution)/shard_map/cond/branch_1_fun/pallas_call | solution.py:740
  142.6 3.3 %branch_1_fun.9.after = bf16[4,384,512]{2,1,0:T(8,128)(2,1)} custom-call(bf16[1024,512]{1,0:T(8,128)(2,1)} %get-tuple-element.65.refs_0_, bf16[1024,512]{1,0:T(8,128)(2,1)} %copy-done.8, bf16[512,512]{1,0:T(8,128)(2,1)} %get-tuple-element.78.refs_2_, bf16[512,512]{1,0:T(8,128)(2,1)} %copy-done.10), custom_call_target="tpu_custom_call" | custom-call | tf_op jit(solution)/shard_map/cond/branch_1_fun/pallas_call | solution.py:476
  145.9 4.6 %all-to-all-start.1 = ((bf16[4,384,512]{2,1,0:T(8,128)(2,1)}), bf16[4,384,512]{2,1,0:T(8,128)(2,1)}, u32[]{:S(2)}, u32[]{:S(2)}) async-start(bf16[4,384,512]{2,1,0:T(8,128)(2,1)} %branch_1_fun.9.after), calls=%async_computation.1 | async-start | bytes 3145728 | tf_op jit(solution)/shard_map/cond/branch_1_fun/all_to_all | solution.py:492
  151.0 6.5 %collective-permute-done.3 = bf16[16,512]{1,0:T(8,128)(2,1)S(1)} collective-permute-done((bf16[16,512]{1,0:T(8,128)(2,1)S(1)}, bf16[16,512]{1,0:T(8,128)(2,1)S(1)}, u32[]{:S(2)}, u32[]{:S(2)}) %collective-permute-start.3) | collective-permute-done | bytes 16416 | tf_op jit(solution)/shard_map/cond/branch_1_fun/ppermute | solution.py:770
  158.7 13.5 %all-to-all-done.1.part = bf16[4,384,512]{2,1,0:T(8,128)(2,1)} async-done(((bf16[4,384,512]{2,1,0:T(8,128)(2,1)}), bf16[4,384,512]{2,1,0:T(8,128)(2,1)}, u32[]{:S(2)}, u32[]{:S(2)}) %all-to-all-start.1) | async-done | bytes 1572896 | tf_op jit(solution)/shard_map/cond/branch_1_fun/all_to_all | solution.py:492
  172.2 6.2 %all-to-all-start = ((bf16[32,16,512]{2,1,0:T(8,128)(2,1)}), bf16[32,16,512]{2,1,0:T(8,128)(2,1)S(1)}, u32[]{:S(2)}, u32[]{:S(2)}) async-start(bf16[32,16,512]{2,1,0:T(8,128)(2,1)} %bitcast.4), calls=%async_computation | async-start | bytes 1048576 | tf_op jit(solution)/shard_map/cond/branch_1_fun/all_to_all | solution.py:492
  178.4 9.9 %branch_1_fun.10 = (bf16[2048,512]{1,0:T(8,128)(2,1)}, bf16[16,512]{1,0:T(8,128)(2,1)}) custom-call(f32[2048,512]{1,0:T(8,128)} %get-tuple-element.50.middle, bf16[2048,2048]{1,0:T(8,128)(2,1)} %get-tuple-element.51.act, bf16[2048,512]{1,0:T(8,128)(2,1)S(1)} %copy-done.2, f32[1,512]{1,0:T(1,128)S(1)} %bitcast.48, bf16[256,256]{1,0:T(8,128)(2,1)} %constant.124.clone.1.order, ...), custom_call_target="tpu_custom_call" | custom-call | tf_op jit(solution)/shard_map/cond/branch_1_fun/pallas_call | solution.py:772
  195.1 3.6 %collective-permute-done.4.refs_1_ = bf16[96,512]{1,0:T(8,128)(2,1)S(1)} collective-permute-done((bf16[96,512]{1,0:T(8,128)(2,1)}, bf16[96,512]{1,0:T(8,128)(2,1)S(1)}, u32[]{:S(2)}, u32[]{:S(2)}) %collective-permute-start.4) | collective-permute-done | bytes 98336 | tf_op jit(solution)/shard_map/cond/branch_1_fun/ppermute | solution.py:496
  198.7 4.9 %collective-permute-done.5.refs_2_ = bf16[96,512]{1,0:T(8,128)(2,1)S(1)} collective-permute-done((bf16[96,512]{1,0:T(8,128)(2,1)}, bf16[96,512]{1,0:T(8,128)(2,1)S(1)}, u32[]{:S(2)}, u32[]{:S(2)}) %collective-permute-start.5) | collective-permute-done | bytes 98336 | tf_op jit(solution)/shard_map/cond/branch_1_fun/ppermute | solution.py:496
  210.4 4.5 %collective-permute-done.9.refs_3_ = bf16[96,512]{1,0:T(8,128)(2,1)S(1)} collective-permute-done((bf16[96,512]{1,0:T(8,128)(2,1)}, bf16[96,512]{1,0:T(8,128)(2,1)S(1)}, u32[]{:S(2)}, u32[]{:S(2)}) %collective-permute-start.9) | collective-permute-done | bytes 98336 | tf_op jit(solution)/shard_map/cond/branch_1_fun/ppermute | solution.py:496
  214.9 5.9 %collective-permute-done.8.refs_2_ = bf16[96,512]{1,0:T(8,128)(2,1)S(1)} collective-permute-done((bf16[96,512]{1,0:T(8,128)(2,1)}, bf16[96,512]{1,0:T(8,128)(2,1)S(1)}, u32[]{:S(2)}, u32[]{:S(2)}) %collective-permute-start.8) | collective-permute-done | bytes 98336 | tf_op jit(solution)/shard_map/cond/branch_1_fun/ppermute | solution.py:496
  223.8 30.3 %all_to_all.27 = bf16[4,4,96,512]{3,2,1,0:T(8,128)(2,1)} all-to-all(bf16[4,4,96,512]{3,2,1,0:T(8,128)(2,1)} %branch_1_fun.13), channel_id=1, replica_groups=mesh['z'=4,'p'=4,'c'=2] {'p'}, dimensions={0} | all-to-all | bytes 3145728 | tf_op jit(solution)/shard_map/cond/branch_1_fun/all_to_all | solution.py:492
  256.0 4.8 %collective-permute-done.2 = bf16[16,512]{1,0:T(8,128)(2,1)S(1)} collective-permute-done((bf16[16,512]{1,0:T(8,128)(2,1)S(1)}, bf16[16,512]{1,0:T(8,128)(2,1)S(1)}, u32[]{:S(2)}, u32[]{:S(2)}) %collective-permute-start.2) | collective-permute-done | bytes 16416 | tf_op jit(solution)/shard_map/cond/branch_1_fun/ppermute | solution.py:797
  261.4 4.8 %shard_map.377 = (f32[512,1536]{1,0:T(8,128)}, f32[512,512]{1,0:T(8,128)}, f32[768,512]{1,0:T(8,128)}, f32[512]{0:T(512)}, f32[512]{0:T(512)}, /*index=5*/f32[51...) custom-call(s32[1]{0:T(128)} %bitcast.8.core, ...), custom_call_target="tpu_custom_call" | custom-call | tf_op jit(solution)/shard_map/pallas_call | solution.py:476
  268.1 5.8 %shard_map.378 = (f32[2048,512]{1,0:T(8,128)}, f32[512,2048]{1,0:T(8,128)}) custom-call(bf16[2048,512]{1,0:T(8,128)(2,1)} %get-tuple-element.172.down, bf16[512,2048]{1,0:T(8,128)(2,1)} %get-tuple-element.173.up), custom_call_target="tpu_custom_call" | custom-call | tf_op jit(solution)/shard_map/pallas_call | solution.py:831
  (108 shorter events, 38.5 us)
Async XLA Ops:
  7.2 16.9 %copy-start = (f32[16,49]{1,0:T(8,128)S(1)}, f32[16,49]{1,0:T(8,128)}, u32[]{:S(2)}) copy-start(f32[16,49]{1,0:T(8,128)} %param.36) | copy-start | bytes 9412
  7.2 27.9 %all-to-all-start.3 = ((bf16[32,16,768]{2,1,0:T(8,128)(2,1)}), bf16[32,16,768]{2,1,0:T(8,128)(2,1)S(1)}, u32[]{:S(2)}, u32[]{:S(2)}) async-start(bf16[32,16,768]{2,1,0:T(8,128)(2,1)} %bitcast.42), calls=%async_computation.3 | async-start | bytes 1572864 | tf_op jit(solution)/shard_map/all_to_all | solution.py:492
  14.5 253.6 %all-reduce.4.cloned.1.call-start = ((), (), s32[]{:S(2)}) async-start(), calls=%async_computation.4 | async-start | bytes 8388608 | tf_op jit(solution)/shard_map/psum | solution.py:688
  17.2 11.0 %collective-permute-start.11 = (bf16[32,512]{1,0:T(8,128)(2,1)S(1)}, bf16[32,512]{1,0:T(8,128)(2,1)S(1)}, u32[]{:S(2)}, u32[]{:S(2)}) collective-permute-start(bf16[32,512]{1,0:T(8,128)(2,1)S(1)} %pad_maximum_fusion), channel_id=1, source_target_pairs={{0,31},{1,0},{2,1},{3,2},{4,3},{5,4},{6,5},{7,6},{8,7},{9,8},{10,9... | collective-permute-start | bytes 98312 | tf_op jit(solution)/shard_map/ppermute | solution.py:574
  36.0 12.3 %collective-permute-start.12 = (bf16[16,768]{1,0:T(8,128)(2,1)}, bf16[16,768]{1,0:T(8,128)(2,1)S(1)}, u32[]{:S(2)}, u32[]{:S(2)}) collective-permute-start(bf16[16,768]{1,0:T(8,128)(2,1)} %shard_map.373.after), channel_id=1, source_target_pairs={{0,31},{1,0},{2,1},{3,2},{4,3},{5,4},{6,5},{7,6},{8,7},{9,8},{10,9... | collective-permute-start | bytes 73736 | tf_op jit(solution)/shard_map/ppermute | solution.py:630
  48.2 22.7 %copy-start.6 = (bf16[128,768]{1,0:T(8,128)(2,1)}, bf16[128,768]{1,0:T(8,128)(2,1)S(1)}, u32[]{:S(2)}) copy-start(bf16[128,768]{1,0:T(8,128)(2,1)S(1)} %pad.4.rim) | copy-start | bytes 589828
  99.5 26.8 %copy-start.7 = (bf16[128,768]{1,0:T(8,128)(2,1)S(1)}, bf16[128,768]{1,0:T(8,128)(2,1)}, u32[]{:S(2)}) copy-start(bf16[128,768]{1,0:T(8,128)(2,1)} %get-tuple-element.74.rim) | copy-start | bytes 589828 | tf_op jit(solution)/shard_map/cond
  126.2 15.3 %collective-permute-start = (bf16[1024,512]{1,0:T(8,128)(2,1)}, bf16[1024,512]{1,0:T(8,128)(2,1)S(1)}, u32[]{:S(2)}, u32[]{:S(2)}) collective-permute-start(bf16[1024,512]{1,0:T(8,128)(2,1)} %get-tuple-element.66), channel_id=1, source_target_pairs={{0,1},{1,0},{2,3},{3,2},{4,5},{5,4},{6,7},{7,6},{8,9},{9,8},{10,11... | collective-permute-start | bytes 3145736 | tf_op jit(solution)/shard_map/cond/branch_1_fun/ppermute | solution.py:488
  139.3 2.1 collective-permute-start.1
  145.9 32.5 %copy-start.2 = (bf16[2048,512]{1,0:T(8,128)(2,1)S(1)}, bf16[2048,512]{1,0:T(8,128)(2,1)}, u32[]{:S(2)}) copy-start(bf16[2048,512]{1,0:T(8,128)(2,1)} %get-tuple-element.52.down) | copy-start | bytes 6291460 | tf_op jit(solution)/shard_map/cond
  145.9 26.3 %all-to-all-start.1 = ((bf16[4,384,512]{2,1,0:T(8,128)(2,1)}), bf16[4,384,512]{2,1,0:T(8,128)(2,1)}, u32[]{:S(2)}, u32[]{:S(2)}) async-start(bf16[4,384,512]{2,1,0:T(8,128)(2,1)} %branch_1_fun.9.after), calls=%async_computation.1 | async-start | bytes 3145728 | tf_op jit(solution)/shard_map/cond/branch_1_fun/all_to_all | solution.py:492
  150.6 7.0 %collective-permute-start.3 = (bf16[16,512]{1,0:T(8,128)(2,1)S(1)}, bf16[16,512]{1,0:T(8,128)(2,1)S(1)}, u32[]{:S(2)}, u32[]{:S(2)}) collective-permute-start(bf16[16,512]{1,0:T(8,128)(2,1)S(1)} %slice.17), channel_id=1, source_target_pairs={{0,1},{1,2},{2,3},{3,4},{4,5},{5,6},{6,7},{7,8},{8,9},{9,10},{10,1... | collective-permute-start | bytes 49160 | tf_op jit(solution)/shard_map/cond/branch_1_fun/ppermute | solution.py:770
  172.2 38.2 %all-to-all-start = ((bf16[32,16,512]{2,1,0:T(8,128)(2,1)}), bf16[32,16,512]{2,1,0:T(8,128)(2,1)S(1)}, u32[]{:S(2)}, u32[]{:S(2)}) async-start(bf16[32,16,512]{2,1,0:T(8,128)(2,1)} %bitcast.4), calls=%async_computation | async-start | bytes 1048576 | tf_op jit(solution)/shard_map/cond/branch_1_fun/all_to_all | solution.py:492
  190.7 8.0 %collective-permute-start.4 = (bf16[96,512]{1,0:T(8,128)(2,1)}, bf16[96,512]{1,0:T(8,128)(2,1)S(1)}, u32[]{:S(2)}, u32[]{:S(2)}) collective-permute-start(bf16[96,512]{1,0:T(8,128)(2,1)} %get-tuple-element.87), channel_id=1, source_target_pairs={{0,8},{8,0},{16,24},{24,16},{1,9},{9,1},{17,25},{25,17},{2,10},{10... | collective-permute-start | bytes 294920 | tf_op jit(solution)/shard_map/cond/branch_1_fun/ppermute | solution.py:496
  192.5 11.0 %collective-permute-start.5 = (bf16[96,512]{1,0:T(8,128)(2,1)}, bf16[96,512]{1,0:T(8,128)(2,1)S(1)}, u32[]{:S(2)}, u32[]{:S(2)}) collective-permute-start(bf16[96,512]{1,0:T(8,128)(2,1)} %get-tuple-element.88), channel_id=1, source_target_pairs={{0,16},{8,24},{16,0},{24,8},{1,17},{9,25},{17,1},{25,9},{2,18},{10... | collective-permute-start | bytes 294920 | tf_op jit(solution)/shard_map/cond/branch_1_fun/ppermute | solution.py:496
  194.9 8.6 %collective-permute-start.6 = (bf16[96,512]{1,0:T(8,128)(2,1)}, bf16[96,512]{1,0:T(8,128)(2,1)S(1)}, u32[]{:S(2)}, u32[]{:S(2)}) collective-permute-start(bf16[96,512]{1,0:T(8,128)(2,1)} %get-tuple-element.89), channel_id=1, source_target_pairs={{0,24},{8,16},{16,8},{24,0},{1,25},{9,17},{17,9},{25,1},{2,26},{10... | collective-permute-start | bytes 294920 | tf_op jit(solution)/shard_map/cond/branch_1_fun/ppermute | solution.py:496
  206.0 8.9 %collective-permute-start.9 = (bf16[96,512]{1,0:T(8,128)(2,1)}, bf16[96,512]{1,0:T(8,128)(2,1)S(1)}, u32[]{:S(2)}, u32[]{:S(2)}) collective-permute-start(bf16[96,512]{1,0:T(8,128)(2,1)} %branch_1_fun.12.refs_0_), channel_id=1, source_target_pairs={{0,24},{8,16},{16,8},{24,0},{1,25},{9,17},{17,9},{25,1},{2,26},{10... | collective-permute-start | bytes 294920 | tf_op jit(solution)/shard_map/cond/branch_1_fun/ppermute | solution.py:496
  208.3 12.6 %collective-permute-start.8 = (bf16[96,512]{1,0:T(8,128)(2,1)}, bf16[96,512]{1,0:T(8,128)(2,1)S(1)}, u32[]{:S(2)}, u32[]{:S(2)}) collective-permute-start(bf16[96,512]{1,0:T(8,128)(2,1)} %branch_1_fun.12.refs_0_), channel_id=1, source_target_pairs={{0,16},{8,24},{16,0},{24,8},{1,17},{9,25},{17,1},{25,9},{2,18},{10... | collective-permute-start | bytes 294920 | tf_op jit(solution)/shard_map/cond/branch_1_fun/ppermute | solution.py:496
  209.1 11.7 %collective-permute-start.7 = (bf16[96,512]{1,0:T(8,128)(2,1)}, bf16[96,512]{1,0:T(8,128)(2,1)S(1)}, u32[]{:S(2)}, u32[]{:S(2)}) collective-permute-start(bf16[96,512]{1,0:T(8,128)(2,1)} %branch_1_fun.12.refs_0_), channel_id=1, source_target_pairs={{0,8},{8,0},{16,24},{24,16},{1,9},{9,1},{17,25},{25,17},{2,10},{10... | collective-permute-start | bytes 294920 | tf_op jit(solution)/shard_map/cond/branch_1_fun/ppermute | solution.py:496
  223.8 30.3 %copy-start.20 = (bf16[16,512]{1,0:T(8,128)(2,1)S(1)}, bf16[16,512]{1,0:T(8,128)(2,1)}, u32[]{:S(2)}) copy-start(bf16[16,512]{1,0:T(8,128)(2,1)} %get-tuple-element.81.after) | copy-start | bytes 49156 | tf_op jit(solution)/shard_map/cond
  223.8 30.8 %copy-start.5 = (bf16[32,16,512]{2,1,0:T(8,128)(2,1)S(1)}, bf16[32,16,512]{2,1,0:T(8,128)(2,1)}, u32[]{:S(2)}) copy-start(bf16[32,16,512]{2,1,0:T(8,128)(2,1)} %copy-done.4) | copy-start | bytes 1572868 | tf_op jit(solution)/shard_map/cond
  223.8 30.8 %copy-start.9 = (bf16[768,512]{1,0:T(8,128)(2,1)S(1)}, bf16[768,512]{1,0:T(8,128)(2,1)}, u32[]{:S(2)}) copy-start(bf16[768,512]{1,0:T(8,128)(2,1)} %get-tuple-element.84) | copy-start | bytes 2359300 | tf_op jit(solution)/shard_map/cond
  254.0 7.4 %collective-permute-start.10 = (bf16[4,384,512]{2,1,0:T(8,128)(2,1)}, bf16[4,384,512]{2,1,0:T(8,128)(2,1)}, u32[]{:S(2)}, u32[]{:S(2)}) collective-permute-start(bf16[4,384,512]{2,1,0:T(8,128)(2,1)} %bitcast.7), channel_id=1, source_target_pairs={{0,1},{1,0},{2,3},{3,2},{4,5},{5,4},{6,7},{7,6},{8,9},{9,8},{10,11... | collective-permute-start | bytes 4718600 | tf_op jit(solution)/shard_map/cond/branch_1_fun/ppermute | solution.py:488
  254.0 6.8 %collective-permute-start.2 = (bf16[16,512]{1,0:T(8,128)(2,1)S(1)}, bf16[16,512]{1,0:T(8,128)(2,1)S(1)}, u32[]{:S(2)}, u32[]{:S(2)}) collective-permute-start(bf16[16,512]{1,0:T(8,128)(2,1)S(1)} %copy-done.20), channel_id=1, source_target_pairs={{0,1},{1,2},{2,3},{3,4},{4,5},{5,6},{6,7},{7,8},{8,9},{9,10},{10,1... | collective-permute-start | bytes 49160 | tf_op jit(solution)/shard_map/cond/branch_1_fun/ppermute | solution.py:797
  (18 other events, 85.1 us)
Sparse Core Ops, SparseCore 0:
  99.0 161.8 all-reduce.3

commit v3 on v2

v3 whole, which is shorter than its diff:
```python
from functools import partial

import jax
import jax.numpy as jnp
import numpy as np
from jax import lax
from jax.experimental import pallas as pl
from jax.experimental.pallas import tpu as pltpu
from jax.sharding import Mesh, PartitionSpec as P

HEADS = 16
HD = 32
BANDS = 8
WIN = 4
SHIFT = 2
RIM = SHIFT * BANDS
SPOTS = WIN * WIN
OCT = 8
OCT_D = OCT * HD
OCT_S = OCT * SPOTS
RIM_SLOTS = 128
EPSILON = 1e-06
MASKED = -1e30
SCALE = HD ** (-0.5)
PRECISE = lax.Precision.HIGHEST
VMEM_LIMIT = 60 * 2**20
FEED_PIECE = 1024
bf16 = jnp.bfloat16
f32 = jnp.float32
AXES = ("z", "p", "c")


def mm(a, b):
    return jnp.dot(a, b, preferred_element_type=f32)


def mm_nt(a, b):
    return lax.dot_general(a, b, (((1,), (1,)), ((), ())), preferred_element_type=f32)


def mm_tn(a, b):
    return lax.dot_general(a, b, (((0,), (0,)), ((), ())), preferred_element_type=f32)


def window_order(x):
    return (
        x.reshape(-1, WIN, BANDS // WIN, WIN, x.shape[-1])
        .transpose(0, 2, 1, 3, 4)
        .reshape(x.shape)
    )


def frame_order(x):
    return (
        x.reshape(-1, BANDS // WIN, WIN, WIN, x.shape[-1])
        .transpose(0, 2, 1, 3, 4)
        .reshape(x.shape)
    )


def window_row(token):
    group, rest = token // (WIN * BANDS), token % (WIN * BANDS)
    frame, band = rest // BANDS, rest % BANDS
    return group * (WIN * BANDS) + (band // WIN) * SPOTS + frame * WIN + band % WIN


def spread(x, block_ones):
    return jnp.concatenate([x] * OCT, axis=0) * block_ones


def own_heads(z):
    lane_head = lax.broadcasted_iota(jnp.int32, (SPOTS, 128), 1) // HD
    halves = []
    per = 128 // HD
    for t in range(OCT_D // 128):
        total = None
        for q in range(per):
            piece = z[(t * per + q) * SPOTS : (t * per + q + 1) * SPOTS, t * 128 : (t + 1) * 128]
            piece = jnp.where(lane_head == q, piece, 0.0)
            total = piece if total is None else total + piece
        halves.append(total)
    return jnp.concatenate(halves, axis=1)


def normalized(x):
    centred = x - jnp.mean(x, axis=-1, keepdims=True)
    inverse = lax.rsqrt(jnp.mean(centred * centred, axis=-1, keepdims=True) + EPSILON)
    return centred * inverse, inverse


def norm_back(grad, n, inverse):
    return inverse * (
        grad
        - jnp.mean(grad, axis=-1, keepdims=True)
        - n * jnp.mean(grad * n, axis=-1, keepdims=True)
    )


def slot_onehot(step, rows, places):
    row = lax.broadcasted_iota(jnp.int32, (rows, places.shape[1]), 0) + step * rows
    return jnp.where(row == places, 1.0, 0.0)


def head_slices(w, o):
    return slice(w * SPOTS, (w + 1) * SPOTS), slice(o * OCT_S, (o + 1) * OCT_S)


def first_kernel(
    cut, arrived, rim, embed_w, embed_b, places, positions, mask_token, gain1, qkv_w, bias,
    across, ones, out_w, out_b, gain2, cotangent, grad_act, up_w, up_b, down_w, down_b, order,
    start_o, qkv_o, probs_o, grad_context_o, grad_middle_o, down_o, up_o, out_grad_o, sums_o,
    up_bias_o, out_o, rim_o, slots_s, score_s, context_s, down_s, up_s, out_s,
):
    rows, width = start_o.shape
    own = arrived.shape[0]
    hidden = up_w.shape[1]
    step = pl.program_id(0)
    last = step == pl.num_programs(0) - 1

    @pl.when(step == 0)
    def _():
        slots_s[0:own, :] = (mm(arrived[...], embed_w[...]) + embed_b[...]).astype(bf16)
        slots_s[own:, :] = (mm(rim[...], embed_w[...]) + embed_b[...]).astype(bf16)
        down_s[...] = jnp.zeros_like(down_s)
        up_s[...] = jnp.zeros_like(up_s)
        out_s[...] = jnp.zeros_like(out_s)
        up_bias_o[...] = jnp.zeros_like(up_bias_o)
        sums_o[...] = jnp.zeros_like(sums_o)

    onehot = slot_onehot(step, rows, places[...])
    seen = jnp.sum(onehot, axis=1, keepdims=True)
    start = mm(onehot.astype(bf16), slots_s[...]) + (1.0 - seen) * mask_token[...] + positions[...]
    start_o[...] = start
    h_one = (normalized(start)[0] * gain1[...]).astype(bf16)
    qkv_o[...] = mm(h_one, qkv_w[...]).astype(bf16)
    block_ones = ones[...]
    windows = rows // SPOTS
    for w in range(windows):
        cut_w = cut[step * windows + w]
        for o in range(HEADS // OCT):
            r, s = head_slices(w, o)
            q = qkv_o[r, o * OCT_D : (o + 1) * OCT_D]
            k = qkv_o[r, width + o * OCT_D : width + (o + 1) * OCT_D]
            raw = mm_nt(k, spread(q, block_ones)) * SCALE + bias[:, s]
            score_s[r, s] = raw + cut_w * across[:, s]
    scores = score_s[...].reshape(windows, SPOTS, HEADS * SPOTS)
    expd = jnp.exp(scores - jnp.max(scores, axis=1, keepdims=True))
    probs = expd / jnp.sum(expd, axis=1, keepdims=True)
    probs_o[...] = probs.reshape(rows, HEADS * SPOTS)
    for w in range(windows):
        for o in range(HEADS // OCT):
            r, s = head_slices(w, o)
            v = qkv_o[r, 2 * width + o * OCT_D : 2 * width + (o + 1) * OCT_D]
            context_s[r, o * OCT_D : (o + 1) * OCT_D] = own_heads(
                mm_tn(probs_o[r, s].astype(bf16), v)
            ).astype(bf16)
    middle = start_o[...] + mm(context_s[...], out_w[...]) + out_b[...]
    n2, r2 = normalized(middle)
    h_two = (n2 * gain2[...]).astype(bf16)

    cot = cotangent[...]
    piece = min(FEED_PIECE, hidden)
    grad_h = None
    result = middle + down_b[...]
    for at in range(0, hidden, piece):
        f = slice(at, at + piece)
        up_value = mm(h_two, up_w[:, f]) + up_b[:, f]
        below = 0.5 * (1.0 + lax.erf(up_value * (0.5**0.5)))
        act = (up_value * below).astype(bf16)
        slope = below + up_value * (jnp.exp(-0.5 * up_value * up_value) * 0.3989422804014327)
        grad_up = grad_act[:, f].astype(f32) * slope
        up_bias_o[:, f] += jnp.sum(grad_up, axis=0, keepdims=True)
        grad_low = grad_up.astype(bf16)
        result = result + mm(act, down_w[f, :])
        down_s[f, :] += mm_tn(act, cot)
        up_s[:, f] += mm_tn(h_two, grad_low)
        part = mm_nt(grad_low, up_w[:, f])
        grad_h = part if grad_h is None else grad_h + part

    result = result.astype(bf16)
    block = order.shape[0]
    result = jnp.concatenate(
        [mm_tn(order[...], result[b : b + block]).astype(bf16) for b in range(0, rows, block)],
        axis=0,
    )

    @pl.when(jnp.logical_not(last))
    def _():
        out_o[pl.ds(pl.multiple_of(step * rows + RIM, RIM), rows), :] = result

    @pl.when(last)
    def _():
        out_o[pl.ds(pl.multiple_of(step * rows + RIM, RIM), rows - RIM), :] = result[: rows - RIM]
        rim_o[...] = result[rows - RIM :]
        out_o[0:RIM, :] = jnp.zeros((RIM, width), bf16)

    wide_cot = cot.astype(f32)
    sums_o[0:1, :] += jnp.sum(grad_h * n2, axis=0, keepdims=True)
    grad_middle = wide_cot + norm_back(grad_h * gain2[...], n2, r2)
    grad_middle_o[...] = grad_middle
    sums_o[1:2, :] += jnp.sum(grad_middle, axis=0, keepdims=True)
    sums_o[2:3, :] += jnp.sum(wide_cot, axis=0, keepdims=True)
    grad_middle_low = grad_middle.astype(bf16)
    out_s[...] += mm_tn(context_s[...], grad_middle_low)
    grad_context_o[...] = mm_nt(grad_middle_low, out_w[...]).astype(bf16)

    @pl.when(last)
    def _():
        down_o[...] = down_s[...].astype(bf16)
        up_o[...] = up_s[...].astype(bf16)
        out_grad_o[...] = out_s[...].astype(bf16)


def second_kernel(
    core, grad_context, qkv, probs, start, grad_middle, places, qkv_w, gain1, ones, arrived, rim,
    out_grad, sums, up_bias, slots_o, keep_c_o, send_c_o, keep_d_o, send_d_o, gqkv_s,
    qkv_s, score_s, slots_s, embed_s, sums_s, rel_s,
):
    step = pl.program_id(0)
    rows, width = start.shape
    own, e_in = arrived.shape
    windows = rows // SPOTS

    @pl.when(step == 0)
    def _():
        qkv_s[...] = jnp.zeros_like(qkv_s)
        slots_s[...] = jnp.zeros_like(slots_s)
        sums_s[...] = jnp.zeros_like(sums_s)
        embed_s[...] = jnp.zeros_like(embed_s)
        rel_s[...] = jnp.zeros_like(rel_s)

    block_ones = ones[...]
    for w in range(windows):
        for o in range(HEADS // OCT):
            r, s = head_slices(w, o)
            heads = slice(o * OCT_D, (o + 1) * OCT_D)
            v_at = slice(2 * width + o * OCT_D, 2 * width + (o + 1) * OCT_D)
            wide = spread(grad_context[r, heads], block_ones)
            score_s[r, s] = mm_nt(qkv[r, v_at], wide)
            gqkv_s[r, v_at] = mm(probs[r, s].astype(bf16), wide).astype(bf16)
    pr = probs[...].reshape(windows, SPOTS, HEADS * SPOTS)
    grad_probs = score_s[...].reshape(windows, SPOTS, HEADS * SPOTS)
    delta = jnp.sum(grad_probs * pr, axis=1, keepdims=True)
    grad_scores = pr * (grad_probs - delta)
    rel_s[...] += jnp.sum(grad_scores, axis=0)
    score_s[...] = grad_scores.reshape(rows, HEADS * SPOTS)
    for w in range(windows):
        for o in range(HEADS // OCT):
            r, s = head_slices(w, o)
            q_at = slice(o * OCT_D, (o + 1) * OCT_D)
            k_at = slice(width + o * OCT_D, width + (o + 1) * OCT_D)
            low = score_s[r, s].astype(bf16)
            gqkv_s[r, q_at] = (own_heads(mm_tn(low, qkv[r, k_at])) * SCALE).astype(bf16)
            gqkv_s[r, k_at] = (mm(low, spread(qkv[r, q_at], block_ones)) * SCALE).astype(bf16)

    n1, r1 = normalized(start[...])
    h_one = (n1 * gain1[...]).astype(bf16)
    qkv_s[...] += mm_tn(h_one, gqkv_s[...])
    grad_h_one = mm_nt(gqkv_s[...], qkv_w[...])
    sums_s[3:4, :] += jnp.sum(grad_h_one * n1, axis=0, keepdims=True)
    grad_start = grad_middle[...] + norm_back(grad_h_one * gain1[...], n1, r1)
    onehot = slot_onehot(step, rows, places[...])
    hidden = 1.0 - jnp.sum(onehot, axis=1, keepdims=True)
    sums_s[4:5, :] += jnp.sum(hidden * grad_start, axis=0, keepdims=True)
    slots_s[...] += mm_tn(onehot.astype(bf16), grad_start.astype(bf16))

    def give_c(low_o, high_o):
        low_o[0:width, :] = qkv_s[:, 0:width].astype(bf16)
        low_o[width : 2 * width, :] = qkv_s[:, width : 2 * width].astype(bf16)
        high_o[0:width, :] = qkv_s[:, 2 * width : 3 * width].astype(bf16)
        high_o[width : 2 * width, :] = out_grad[...]

    def give_d(low_o, high_o):
        half = low_o.shape[0]
        low_o[...] = embed_s[0:half, :].astype(bf16)
        left = e_in - half
        high_o[...] = jnp.zeros_like(high_o)
        if left > 0:
            high_o[0:left, :] = embed_s[half:e_in, :].astype(bf16)
        left = max(left, 0)
        high_o[left : left + 16, :] = sums_s[...].astype(bf16)
        high_o[left + 16 : left + 16 + SPOTS, 0 : HEADS * SPOTS] = rel_s[...].astype(bf16)

    last = step == pl.num_programs(0) - 1

    @pl.when(last)
    def _():
        slots = slots_s[...].astype(bf16)
        slots_o[...] = slots
        embed_s[0:e_in, :] = mm_tn(arrived[...], slots[0:own]) + mm_tn(rim[...], slots[own:])
        sums_s[0:3, :] = sums[0:3, :]
        sums_s[5:6, :] = jnp.sum(slots.astype(f32), axis=0, keepdims=True)
        for block in range(up_bias.shape[1] // width):
            sums_s[6 + block : 7 + block, :] = up_bias[:, block * width : (block + 1) * width]

    @pl.when(last & (core[0] == 0))
    def _():
        give_c(keep_c_o, send_c_o)
        give_d(keep_d_o, send_d_o)

    @pl.when(last & (core[0] == 1))
    def _():
        give_c(send_c_o, keep_c_o)
        give_d(send_d_o, keep_d_o)


def rim_kernel(hot, arrived, after, out):
    del after
    out[...] = mm(hot[...], arrived[...]).astype(bf16)


def rim_back_kernel(hot, rim_grad, grad_slots, after_a, after_b, out):
    del after_a, after_b
    slots = out.shape[0]
    out[...] = (grad_slots[0:slots, :].astype(f32) + mm_tn(hot[...], rim_grad[...])).astype(bf16)


def act_back_kernel(cotangent, down_w, after, out):
    del after
    out[...] = mm_nt(cotangent[...], down_w[...]).astype(bf16)


def prepare_kernel(cotangent, next_cot, pos_embed, order, cot_o, positions_o):
    block = order.shape[0]
    tokens = cotangent.shape[0]
    for at in range(0, tokens, block):
        if at + block < tokens:
            rows = cotangent[at + RIM : at + RIM + block, :]
        else:
            rows = jnp.concatenate([cotangent[at + RIM :, :], next_cot[...]], axis=0)
        cot_o[at : at + block, :] = mm(order[...].astype(bf16), rows).astype(bf16)
    grid_rows = pos_embed.shape[0]
    for at in range(0, grid_rows, block):
        if at + block < grid_rows:
            rows = pos_embed[at + RIM : at + RIM + block, :]
        else:
            rows = jnp.concatenate([pos_embed[at + RIM :, :], pos_embed[0:RIM, :]], axis=0)
        positions_o[at : at + block, :] = jnp.dot(
            order[...], rows, precision=PRECISE, preferred_element_type=f32
        )


def chip_join_kernel(count, *refs):
    parts, out = refs[: 2 * count], refs[-1]
    at = 0
    for keep, got in zip(parts[::2], parts[1::2]):
        rows = keep.shape[1]
        out[0, at : at + rows, :] = (keep[0].astype(f32) + got[0].astype(f32)).astype(bf16)
        at += rows


def plane_sum_kernel(count, place, *refs):
    parts, outs, total_s = refs[:count], refs[count + 1 : -1], refs[-1]
    if count == 1:
        total_s[...] = jnp.sum(parts[0][...].astype(f32), axis=0)
    else:
        total = parts[0][...].astype(f32)
        for part in parts[1:]:
            total = total + part[...].astype(f32)
        total_s[...] = total
    rows = outs[0].shape[0]
    for b, out in enumerate(outs):
        at = pl.multiple_of(lax.bitwise_xor(place[0], b) * rows, 8)
        out[...] = total_s[pl.ds(at, rows), :].astype(bf16)


def z_sum_kernel(count, *refs):
    parts, out = refs[:count], refs[-1]
    total = parts[0][...].astype(f32)
    for part in parts[1:]:
        total = total + part[...].astype(f32)
    out[...] = total.astype(bf16)


def z_join_kernel(count, place, *refs):
    out = refs[-1]
    for b, ref in enumerate(refs[:count]):
        share = ref[...]
        at = lax.bitwise_xor(place[0], b)
        for cell in range(out.shape[0]):
            out[cell, at] = share


def widen_kernel(down, up, down_o, up_o):
    down_o[...] = down[...].astype(f32)
    up_o[...] = up[...].astype(f32)


def rest_unpack_kernel(split, core, mine, other, qkv_o, out_o, embed_o, *small_o):
    width = out_o.shape[1]
    e_in = embed_o.shape[0]

    def give(low, high):
        rows = low[:, 0:split].reshape(-1, width).astype(f32)
        qkv_o[:, 0:width] = rows[0:width]
        qkv_o[:, width : 2 * width] = rows[width:]
        rows = high[:, 0:split].reshape(-1, width).astype(f32)
        qkv_o[:, 2 * width :] = rows[0:width]
        out_o[...] = rows[width:]
        rows = low[:, split:].reshape(-1, width).astype(f32)
        half = rows.shape[0]
        embed_o[0 : min(half, e_in), :] = rows[0 : min(half, e_in)]
        rows = high[:, split:].reshape(-1, width).astype(f32)
        left = max(e_in - half, 0)
        if left:
            embed_o[half:e_in, :] = rows[0:left]
        for i, vector_o in enumerate(small_o[:6]):
            vector_o[...] = rows[left + i]
        up_bias_o, rel_o = small_o[6:]
        for i in range(up_bias_o.shape[0] // width):
            up_bias_o[i * width : (i + 1) * width] = rows[left + 6 + i]
        rel_o[...] = rows[left + 16 : left + 16 + SPOTS, 0 : HEADS * SPOTS]

    @pl.when(core[0] == 0)
    def _():
        give(mine, other)

    @pl.when(core[0] == 1)
    def _():
        give(other, mine)


ANY = pl.BlockSpec(memory_space=pl.ANY)
SMEM = pl.BlockSpec(memory_space=pltpu.SMEM)


def whole(s):
    return pl.BlockSpec(s, lambda *i: (0,) * len(s))


def held(s):
    return pl.BlockSpec(s, lambda *i: (0,) * len(s), pipeline_mode=pl.Buffered(1))


def tile(rows, width, first=0):
    return pl.BlockSpec((rows, width), lambda i: (i + first, 0))


def params():
    return pltpu.CompilerParams(vmem_limit_bytes=VMEM_LIMIT)


def shape(s, d):
    return jax.ShapeDtypeStruct(s, d)


def at_once(kernel, args, outs, specs=None, scratch=()):
    if specs is None:
        specs = [whole(a.shape) for a in args]
    many = isinstance(outs, (list, tuple))
    out_specs = [whole(o.shape) for o in outs] if many else whole(outs.shape)
    return pl.pallas_call(
        kernel,
        grid=(1,),
        in_specs=specs,
        out_specs=out_specs,
        out_shape=outs,
        scratch_shapes=list(scratch),
        compiler_params=params(),
    )(*args)


def swap_cores(x):
    return lax.ppermute(x, "c", [(0, 1), (1, 0)])


def exchange(x, axis):
    return lax.all_to_all(x, axis, 0, 0, tiled=True)


def across(x, axis):
    size = lax.axis_size(axis)
    return [lax.ppermute(x[b], axis, [(i, i ^ b) for i in range(size)]) for b in range(1, size)]


def chip_join(pairs, after):
    cells = lax.axis_size("p")
    width = pairs[0][0].shape[1]
    refs = [a.reshape(cells, -1, width) for keep, send in pairs for a in (keep, swap_cores(send))]
    rows = sum(r.shape[1] for r in refs[::2])
    return pl.pallas_call(
        partial(chip_join_kernel, len(pairs)),
        grid=(cells,),
        in_specs=[pl.BlockSpec((1, *r.shape[1:]), lambda i: (i, 0, 0)) for r in refs] + [ANY] * len(after),
        out_specs=pl.BlockSpec((1, rows, width), lambda i: (i, 0, 0)),
        out_shape=shape((cells, rows, width), bf16),
        compiler_params=params(),
    )(*refs, *after)


def plane_sum(place, parts, after):
    planes = lax.axis_size("z")
    rows, width = parts[0].shape[-2:]
    return at_once(
        partial(plane_sum_kernel, len(parts)),
        (place, *parts, after),
        [shape((rows // planes, width), bf16)] * planes,
        [SMEM] + [whole(p.shape) for p in parts] + [ANY],
        [pltpu.VMEM((rows, width), f32)],
    )


def z_sum(parts, after):
    return at_once(
        partial(z_sum_kernel, len(parts)),
        (*parts, *after),
        shape(parts[0].shape, bf16),
        [whole(p.shape) for p in parts] + [ANY] * len(after),
    )


def z_join(place, parts, after):
    cells = lax.axis_size("p")
    return at_once(
        partial(z_join_kernel, len(parts)),
        (place, *parts, *after),
        shape((cells, len(parts), *parts[0].shape), bf16),
        [SMEM] + [whole(p.shape) for p in parts] + [ANY] * len(after),
    )


def order_matrix(block):
    token = np.arange(block)
    group, rest = token // (WIN * BANDS), token % (WIN * BANDS)
    frame, band = rest // BANDS, rest % BANDS
    row = group * (WIN * BANDS) + (band // WIN) * SPOTS + frame * WIN + band % WIN
    matrix = np.zeros((block, block), np.float32)
    matrix[row, token] = 1.0
    return matrix


def per_device(
    visible, embed_weight, embed_bias, mask_token, pos_embed, norm1_gain, qkv_weight, rel_table,
    out_weight, out_bias, norm2_gain, up_weight, up_bias, down_weight, down_bias, cotangent,
    visible_index, slot_counts, segment_ids,
):
    device_count = lax.axis_size(AXES)
    device_rank = lax.axis_index(AXES)
    core = lax.axis_index("c").reshape(1).astype(jnp.int32)
    z_place = lax.axis_index("z").reshape(1).astype(jnp.int32)
    planes, cells = lax.axis_size("z"), lax.axis_size("p")
    tokens, width = cotangent.shape
    frames = tokens // BANDS
    hidden = down_weight.shape[0]
    e_in = visible.shape[1]
    slot_rows = visible_index.shape[2]
    slots = device_count * slot_rows
    ext = slots + RIM_SLOTS
    back = [(i, (i - 1) % device_count) for i in range(device_count)]
    ahead = [(i, (i + 1) % device_count) for i in range(device_count)]
    row = lambda v: v.reshape(1, -1)

    arrived = exchange(visible, AXES)

    spot = visible_index.reshape(slots)
    live = (
        jnp.arange(slot_rows)[None, :] < slot_counts.reshape(device_count, 1)
    ).reshape(slots)
    rim_hot = ((jnp.arange(RIM)[:, None] == spot[None, :]) & live[None, :]).astype(bf16)
    rim_seen = jnp.sum(rim_hot.astype(f32), axis=1, keepdims=True).astype(bf16)
    sent_back = jnp.concatenate(
        [cotangent[:RIM], jnp.broadcast_to(rim_seen, (RIM, width))], axis=0
    )
    from_next = lax.ppermute(sent_back, AXES, back)
    next_seen = from_next[RIM:, 0].astype(f32)
    own_places = jnp.where(live & (spot >= RIM), window_row(spot - RIM), -1)
    rim_places = jnp.where(
        next_seen > 0.5, window_row(tokens - RIM + np.arange(RIM)), -1
    )
    places = jnp.concatenate(
        [own_places, rim_places, np.full((RIM_SLOTS - RIM,), -1, np.int32)]
    ).reshape(1, ext).astype(jnp.int32)

    seg_cycle = jnp.concatenate([segment_ids, segment_ids[:SHIFT]])
    seg_tape = lax.dynamic_slice_in_dim(seg_cycle, device_rank * frames + SHIFT, frames)
    seg_win = seg_tape.reshape(frames // WIN, WIN)
    cut = jnp.repeat(
        (seg_win[:, SHIFT - 1] != seg_win[:, SHIFT]).astype(f32), BANDS // WIN
    )

    spots = np.arange(SPOTS)
    frame_of, band_of = spots // WIN, spots % WIN
    rels = 2 * WIN - 1
    rel_index = (frame_of[:, None] - frame_of[None, :] + WIN - 1) * rels + (
        band_of[:, None] - band_of[None, :] + WIN - 1
    )
    rel_hot = (rel_index[:, :, None] == np.arange(rels * rels)).astype(np.float32)
    bias = jnp.einsum("hr,ijr->jhi", rel_table, rel_hot, precision=PRECISE).reshape(
        SPOTS, HEADS * SPOTS
    )
    halves = frame_of // SHIFT
    apart = np.tile(
        np.where(halves[:, None] != halves[None, :], MASKED, 0.0).astype(np.float32), (1, HEADS)
    )
    ones = jnp.asarray(
        np.arange(OCT_S)[:, None] // SPOTS == np.arange(OCT_D)[None, :] // HD, bf16
    )
    order = order_matrix(256)
    cot, positions = at_once(
        prepare_kernel,
        (cotangent, from_next[:RIM], pos_embed, order),
        [shape(cotangent.shape, bf16), shape(pos_embed.shape, f32)],
    )

    tm = min(512, tokens)
    grid = (tokens // tm,)
    pos_blocks = pos_embed.shape[0] // tm
    rim_rows = at_once(
        rim_kernel,
        (rim_hot, arrived, cot),
        shape((RIM, e_in), bf16),
        [whole(rim_hot.shape), whole(arrived.shape), ANY],
    )
    next_rows = lax.ppermute(rim_rows, AXES, back)
    grad_act = pl.pallas_call(
        act_back_kernel,
        grid=grid,
        in_specs=[tile(tm, width), whole((hidden, width)), ANY],
        out_specs=tile(tm, hidden),
        out_shape=shape((tokens, hidden), bf16),
        compiler_params=params(),
    )(cot, down_weight, rim_rows)
    rim = jnp.pad(next_rows, ((0, RIM_SLOTS - RIM), (0, 0)))
    first_args = [
        cut, arrived, rim, embed_weight, row(embed_bias), places, positions,
        row(mask_token), row(norm1_gain), qkv_weight, bias, apart, ones, out_weight,
        row(out_bias), row(norm2_gain), cot, grad_act, up_weight, row(up_bias), down_weight,
        row(down_bias), jnp.asarray(order, bf16),
    ]
    specs = [SMEM] + [held(a.shape) for a in first_args[1:]]
    specs[6] = pl.BlockSpec((tm, width), lambda i: (lax.rem(i, pos_blocks), 0))
    specs[16] = tile(tm, width)
    specs[17] = tile(tm, hidden)
    (
        start, qkv, probs, grad_context, grad_middle, down_grad, up_grad, out_grad, sums,
        up_bias_grad, out, rim_out,
    ) = pl.pallas_call(
        first_kernel,
        grid=grid,
        in_specs=specs,
        out_specs=[
            tile(tm, width),
            tile(tm, 3 * width),
            tile(tm, HEADS * SPOTS),
            tile(tm, width),
            tile(tm, width),
            whole((hidden, width)),
            whole((width, hidden)),
            whole((width, width)),
            whole((8, width)),
            whole((1, hidden)),
            whole((tokens, width)),
            whole((RIM, width)),
        ],
        out_shape=[
            shape((tokens, width), f32),
            shape((tokens, 3 * width), bf16),
            shape((tokens, HEADS * SPOTS), f32),
            shape((tokens, width), bf16),
            shape((tokens, width), f32),
            shape((hidden, width), bf16),
            shape((width, hidden), bf16),
            shape((width, width), bf16),
            shape((8, width), f32),
            shape((1, hidden), f32),
            shape((tokens, width), bf16),
            shape((RIM, width), bf16),
        ],
        scratch_shapes=[
            pltpu.VMEM((ext, width), bf16),
            pltpu.VMEM((tm, HEADS * SPOTS), f32),
            pltpu.VMEM((tm, width), bf16),
            pltpu.VMEM((hidden, width), f32),
            pltpu.VMEM((width, hidden), f32),
            pltpu.VMEM((width, width), f32),
        ],
        compiler_params=params(),
    )(*first_args)
    down_sum, up_sum = lax.psum((down_grad, up_grad), AXES)

    unit = 16 * planes * cells
    half = -(-width // unit) * unit
    def rest(operands):
        (
            grad_context, qkv, probs, start, grad_middle, places, arrived, rim, rim_hot, out_grad,
            sums, up_bias_grad, out, rim_out,
        ) = operands
        grad_slots, keep_c, send_c, keep_d, send_d = pl.pallas_call(
            second_kernel,
            grid=grid,
            in_specs=[
                SMEM,
                tile(tm, width),
                tile(tm, 3 * width),
                tile(tm, HEADS * SPOTS),
                tile(tm, width),
                tile(tm, width),
                held((1, ext)),
                held((width, 3 * width)),
                held((1, width)),
                held((OCT_S, OCT_D)),
                held((slots, e_in)),
                held((RIM_SLOTS, e_in)),
                held((width, width)),
                held((8, width)),
                held((1, hidden)),
            ],
            out_specs=[
                whole((ext, width)),
                whole((2 * width, width)),
                whole((2 * width, width)),
                whole((half, width)),
                whole((half, width)),
            ],
            out_shape=[
                shape((ext, width), bf16),
                shape((2 * width, width), bf16),
                shape((2 * width, width), bf16),
                shape((half, width), bf16),
                shape((half, width), bf16),
            ],
            scratch_shapes=[
                pltpu.VMEM((tm, 3 * width), bf16),
                pltpu.VMEM((width, 3 * width), f32),
                pltpu.VMEM((tm, HEADS * SPOTS), f32),
                pltpu.VMEM((ext, width), f32),
                pltpu.VMEM((max(e_in, half), width), f32),
                pltpu.VMEM((16, width), f32),
                pltpu.VMEM((SPOTS, HEADS * SPOTS), f32),
            ],
            compiler_params=params(),
        )(
            core, grad_context, qkv, probs, start, grad_middle, places, qkv_weight, row(norm1_gain),
            ones, arrived, rim, out_grad, sums, up_bias_grad,
        )
        rim_grad = lax.ppermute(grad_slots[slots : slots + RIM], AXES, ahead)
        shares = chip_join([(keep_c, send_c), (keep_d, send_d)], ())
        part = exchange(shares, "p")
        first_rows = lax.ppermute(rim_out, AXES, ahead)
        out = lax.dynamic_update_slice(out, first_rows, (0, 0))
        grad_embedded = at_once(
            rim_back_kernel,
            (rim_hot, rim_grad, grad_slots, shares, first_rows),
            shape((slots, width), bf16),
            [whole(a.shape) for a in (rim_hot, rim_grad, grad_slots)] + [ANY, ANY],
        )
        returned = exchange(grad_embedded, AXES)
        grad_visible = lax.dot_general(
            returned, embed_weight, (((1,), (1,)), ((), ())), preferred_element_type=f32
        ).astype(bf16)
        sums_c = plane_sum(z_place, [part], grad_embedded)
        total = z_sum([sums_c[0], *across(sums_c, "z")], ())
        joined = z_join(z_place, [total, *across([total] * planes, "z")], (returned,))
        mine = exchange(joined, "p").reshape(cells, -1, width)
        return out, grad_visible, mine, swap_cores(mine)

    def nothing(operands):
        return tuple(jnp.zeros(o.shape, o.dtype) for o in jax.eval_shape(rest, operands))

    operands = (
        grad_context, qkv, probs, start, grad_middle, places, arrived, rim, rim_hot, out_grad,
        sums, up_bias_grad, out, rim_out,
    )
    out, grad_visible, mine, other = lax.cond(device_rank < device_count, rest, nothing, operands)

    vector = shape((width,), f32)
    (
        grad_qkv_weight, grad_out_weight, grad_embed_weight, grad_norm2_gain, grad_out_bias,
        grad_down_bias, grad_norm1_gain, grad_mask_token, grad_embed_bias, grad_up_bias, rel_sums,
    ) = at_once(
        partial(rest_unpack_kernel, 2 * width // cells),
        (core, mine, other),
        [
            shape((width, 3 * width), f32),
            shape((width, width), f32),
            shape((e_in, width), f32),
            *[vector] * 6,
            shape((hidden,), f32),
            shape((SPOTS, HEADS * SPOTS), f32),
        ],
        [SMEM, whole(mine.shape), whole(other.shape)],
    )
    grad_rel = jnp.einsum(
        "jhi,ijr->hr", rel_sums.reshape(SPOTS, HEADS, SPOTS), rel_hot, precision=PRECISE
    )
    grad_down_weight, grad_up_weight = pl.pallas_call(
        widen_kernel,
        grid=(4,),
        in_specs=[tile(hidden // 4, width), tile(width // 4, hidden)],
        out_specs=[tile(hidden // 4, width), tile(width // 4, hidden)],
        out_shape=[shape((hidden, width), f32), shape((width, hidden), f32)],
        compiler_params=params(),
    )(down_sum, up_sum)
    return (
        out,
        grad_visible,
        grad_embed_weight,
        grad_embed_bias,
        grad_mask_token,
        grad_norm1_gain,
        grad_qkv_weight,
        grad_rel,
        grad_out_weight,
        grad_out_bias,
        grad_norm2_gain,
        grad_up_weight,
        grad_up_bias,
        grad_down_weight,
        grad_down_bias,
    )


def solution(mesh):
    planes = 4
    grid = Mesh(mesh.devices.reshape(planes, -1, 2), AXES)
    split = P(AXES)
    in_specs = (split,) + (P(),) * 14 + (split, split, split, P())
    out_specs = (split, split) + (P(),) * 13
    return jax.shard_map(
        per_device, mesh=grid, in_specs=in_specs, out_specs=out_specs, check_vma=False
    )
```

time: 282 us -> 277 us (0.982)
  Pallas kernels: 134 us -> 124 us
  waiting for transfers between devices: 48.3 us -> 52.5 us
    pallas_call x5 -> x3, Pallas kernels: 100 us -> 90.3 us  [the longest x1 57 us: per_device(): pl.pallas_call(first_kernel, grid=grid, in_specs=specs, out_specs=[tile(t...]
    ppermute x6, waiting for transfers between devices: 18.8 us -> 24.9 us  [across(): lax.ppermute(x[b], axis, [(i, i ^ b) for i in range(size)])]
    ppermute x1, waiting for transfers between devices: 6.55 us -> 0.86 us  [rest(): rim_grad = lax.ppermute(grad_slots[slots:slots + RIM], AXES, ahead)]
    psum x1, waiting for transfers between devices: 0.01 us -> 5.38 us  [per_device(): down_sum, up_sum = lax.psum((down_grad, up_grad), AXES)]
    all_to_all x3, waiting for transfers between devices: 15.2 us -> 11.2 us  [exchange(): return lax.all_to_all(x, axis, 0, 0, tiled=True)]
    ppermute x3, waiting for transfers between devices: 1.75 us -> 4.76 us  [swap_cores(): return lax.ppermute(x, 'c', [(0, 1), (1, 0)])]
  transfers between devices with their start and end apart: 17 -> 17, of which waited for: 10 -> 12; matrix products, arithmetic and copies ran while one was open for 5% -> 5% of each run, Pallas kernels for 27% -> 22%
where the time goes in v3:
time: 277 us; the launch traced here: 276 us
  Pallas kernels  124 us (45%)
  waiting for transfers between devices  52.5 us (19%)
  starting transfers between devices  39.9 us (14%)
  blocking collectives  30.2 us (11%)
  between operations  14.2 us (5%)
  local copies, waits for them, and re-layouts  10 us (4%)
  matrix products  3.67 us (1%)
    pallas_call x1, Pallas kernels, per_device(): pl.pallas_call(first_kernel, grid=grid, in_specs=specs, out_specs=[tile(t...  57 us
    all_to_all x1, blocking collectives, exchange(): return lax.all_to_all(x, axis, 0, 0, tiled=True)  30.2 us
    pallas_call x1, Pallas kernels, rest(): pl.pallas_call(second_kernel, grid=grid, in_specs=[SMEM, tile(tm, width),...  29.3 us
    ppermute x6, waiting for transfers between devices, across(): lax.ppermute(x[b], axis, [(i, i ^ b) for i in range(size)])  24.9 us
    all_to_all x3, starting transfers between devices, exchange(): return lax.all_to_all(x, axis, 0, 0, tiled=True)  19.4 us
    pallas_call x7, Pallas kernels, at_once(): pl.pallas_call(kernel, grid=(1,), in_specs=specs, out_specs=out_specs, ou...  18.8 us
    all_to_all x3, waiting for transfers between devices, exchange(): return lax.all_to_all(x, axis, 0, 0, tiled=True)  11.2 us
    ppermute x6, starting transfers between devices, across(): lax.ppermute(x[b], axis, [(i, i ^ b) for i in range(size)])  8.77 us
  transfers between devices with their start and end apart: 17, of which 12 were waited for; matrix products, arithmetic and copies ran while one was open for 5% of the time, Pallas kernels for 22%

profile of v3, /device:TPU:0, one launch (start us, length us, event | category | flops | bytes accessed | tf_op | source)
XLA Modules:
  0.0 276.3 jit_solution(7736324820973622319)
XLA Ops:
  7.2 7.3 %all-to-all-start.3 = ((bf16[32,16,768]{2,1,0:T(8,128)(2,1)}), bf16[32,16,768]{2,1,0:T(8,128)(2,1)S(1)}, u32[]{:S(2)}, u32[]{:S(2)}) async-start(bf16[32,16,768]{2,1,0:T(8,128)(2,1)} %bitcast.40), calls=%async_computation.3 | async-start | bytes 1572864 | tf_op jit(solution)/shard_map/all_to_all | solution.py:468
  17.2 5.2 %collective-permute-start.11 = (bf16[32,512]{1,0:T(8,128)(2,1)S(1)}, bf16[32,512]{1,0:T(8,128)(2,1)S(1)}, u32[]{:S(2)}, u32[]{:S(2)}) collective-permute-start(bf16[32,512]{1,0:T(8,128)(2,1)S(1)} %pad_maximum_fusion), channel_id=1, source_target_pairs={{0,31},{1,0},{2,1},{3,2},{4,3},{5,4},{6,5},{7,6},{8,7},{9,8},{10,9... | collective-permute-start | bytes 98312 | tf_op jit(solution)/shard_map/ppermute | solution.py:564
  28.8 4.5 %shard_map.370 = (bf16[2048,512]{1,0:T(8,128)(2,1)}, f32[512,512]{1,0:T(8,128)}) custom-call(bf16[2048,512]{1,0:T(8,128)(2,1)} %cotangent.1, bf16[16,512]{1,0:T(8,128)(2,1)} %slice.29.next_cot, f32[512,512]{1,0:T(8,128)} %pos_embed.1, f32[256,256]{1,0:T(8,128)} %constant.122.clone.order), custom_call_target="tpu_custom_call" | custom-call | tf_op jit(solution)/shard_map/pallas_call | solution.py:452
  36.0 3.9 %collective-permute-start.12 = (bf16[16,768]{1,0:T(8,128)(2,1)}, bf16[16,768]{1,0:T(8,128)(2,1)S(1)}, u32[]{:S(2)}, u32[]{:S(2)}) collective-permute-start(bf16[16,768]{1,0:T(8,128)(2,1)} %shard_map.371.after), channel_id=1, source_target_pairs={{0,31},{1,0},{2,1},{3,2},{4,3},{5,4},{6,5},{7,6},{8,7},{9,8},{10,9... | collective-permute-start | bytes 73736 | tf_op jit(solution)/shard_map/ppermute | solution.py:614
  40.0 8.7 %shard_map.372.grad_act = bf16[2048,2048]{1,0:T(8,128)(2,1)} custom-call(bf16[2048,512]{1,0:T(8,128)(2,1)} %get-tuple-element.115.after.cotangent, bf16[2048,512]{1,0:T(8,128)(2,1)} %down_w.3, bf16[16,768]{1,0:T(8,128)(2,1)} %shard_map.371.after), custom_call_target="tpu_custom_call" | custom-call | tf_op jit(solution)/shard_map/pallas_call | solution.py:615
  48.7 57.0 %shard_map.373 = (f32[2048,512]{1,0:T(8,128)}, bf16[2048,1536]{1,0:T(8,128)(2,1)}, f32[2048,256]{1,0:T(8,128)}, bf16[2048,512]{1,0:T(8,128)(2,1)}, f32[2048,512]...) custom-call(f32[128]{0:T(128)} %reshape.126.cut, ...), custom_call_target="tpu_custom_call" | custom-call | tf_op jit(solution)/shard_map/pallas_call | solution.py:637
  105.8 145.8 %conditional.1 = (bf16[2048,512]{1,0:T(8,128)(2,1)}, bf16[512,768]{1,0:T(8,128)(2,1)}, bf16[4,384,512]{2,1,0:T(8,128)(2,1)}, bf16[4,384,512]{2,1,0:T(8,128)(2,1)}) conditional(s32[]{:T(128)} %convert_element_type.28, () %tuple.16, (bf16[16,512]{1,0:T(8,128)(2,1)S(1)}, bf16[2048,512]{1,0:T(8,128)(2,1)}, f32[512]{0:T(512)S(1)}, s32[1]{0:T(128)}, ...), branch_computations={%region_1.2_spmd, %region_2.3_spmd} | conditional | flops 403046400 | bytes 46007200 | solution.py:764
  105.8 29.3 %branch_1_fun.6 = (bf16[640,512]{1,0:T(8,128)(2,1)}, bf16[1024,512]{1,0:T(8,128)(2,1)}, bf16[1024,512]{1,0:T(8,128)(2,1)}, bf16[512,512]{1,0:T(8,128)(2,1)}, bf16[512,512]{1,0:T(8,128)(2,1)}) custom-call(s32[1]{0:T(128)} %get-tuple-element.43.core, bf16[2048,512]{1,0:T(8,128)(2,1)} %get-tuple-element.44.grad_context, ...), custom_call_target="tpu_custom_call" | custom-call | tf_op jit(solution)/shard_map/cond/branch_1_fun/pallas_call | solution.py:688
  135.6 3.1 %collective-permute-done.3 = bf16[512,512]{1,0:T(8,128)(2,1)S(1)} collective-permute-done((bf16[512,512]{1,0:T(8,128)(2,1)}, bf16[512,512]{1,0:T(8,128)(2,1)S(1)}, u32[]{:S(2)}, u32[]{:S(2)}) %collective-permute-start.3) | collective-permute-done | bytes 524320 | tf_op jit(solution)/shard_map/cond/branch_1_fun/ppermute | solution.py:464
  139.9 3.9 %branch_1_fun.7.after_a = bf16[4,384,512]{2,1,0:T(8,128)(2,1)} custom-call(bf16[4,256,512]{2,1,0:T(8,128)(2,1)} %bitcast.38, bf16[4,256,512]{2,1,0:T(8,128)(2,1)} %bitcast.39, bf16[4,128,512]{2,1,0:T(8,128)(2,1)} %bitcast.41, bf16[4,128,512]{2,1,0:T(8,128)(2,1)} %bitcast.42), custom_call_target="tpu_custom_call" | custom-call | tf_op jit(solution)/shard_map/cond/branch_1_fun/pallas_call | solution.py:481
  143.8 3.6 %all-to-all-start.1 = ((bf16[4,384,512]{2,1,0:T(8,128)(2,1)}), bf16[4,384,512]{2,1,0:T(8,128)(2,1)S(1)}, u32[]{:S(2)}, u32[]{:S(2)}) async-start(bf16[4,384,512]{2,1,0:T(8,128)(2,1)} %branch_1_fun.7.after_a), calls=%async_computation.1 | async-start | bytes 3145728 | tf_op jit(solution)/shard_map/cond/branch_1_fun/all_to_all | solution.py:468
  150.2 4.2 %collective-permute-done.after_b = bf16[16,512]{1,0:T(8,128)(2,1)S(1)} collective-permute-done((bf16[16,512]{1,0:T(8,128)(2,1)S(1)}, bf16[16,512]{1,0:T(8,128)(2,1)S(1)}, u32[]{:S(2)}, u32[]{:S(2)}) %collective-permute-start) | collective-permute-done | bytes 16416 | tf_op jit(solution)/shard_map/cond/branch_1_fun/ppermute | solution.py:739
  158.0 9.5 %all-to-all-done.1.refs_0_ = bf16[4,384,512]{2,1,0:T(8,128)(2,1)S(1)} async-done(((bf16[4,384,512]{2,1,0:T(8,128)(2,1)}), bf16[4,384,512]{2,1,0:T(8,128)(2,1)S(1)}, u32[]{:S(2)}, u32[]{:S(2)}) %all-to-all-start.1) | async-done | bytes 1572896 | tf_op jit(solution)/shard_map/cond/branch_1_fun/all_to_all | solution.py:468
  167.6 8.5 %all-to-all-start = ((bf16[32,16,512]{2,1,0:T(8,128)(2,1)}), bf16[32,16,512]{2,1,0:T(8,128)(2,1)S(1)}, u32[]{:S(2)}, u32[]{:S(2)}) async-start(bf16[32,16,512]{2,1,0:T(8,128)(2,1)} %bitcast.35), calls=%async_computation | async-start | bytes 1048576 | tf_op jit(solution)/shard_map/cond/branch_1_fun/all_to_all | solution.py:468
  176.1 2.4 branch_1_fun.9
  182.9 6.4 %collective-permute-done.4.refs_1_ = bf16[96,512]{1,0:T(8,128)(2,1)S(1)} collective-permute-done((bf16[96,512]{1,0:T(8,128)(2,1)}, bf16[96,512]{1,0:T(8,128)(2,1)S(1)}, u32[]{:S(2)}, u32[]{:S(2)}) %collective-permute-start.4) | collective-permute-done | bytes 98336 | tf_op jit(solution)/shard_map/cond/branch_1_fun/ppermute | solution.py:473
  189.3 10.7 %collective-permute-done.5.refs_2_ = bf16[96,512]{1,0:T(8,128)(2,1)S(1)} collective-permute-done((bf16[96,512]{1,0:T(8,128)(2,1)}, bf16[96,512]{1,0:T(8,128)(2,1)S(1)}, u32[]{:S(2)}, u32[]{:S(2)}) %collective-permute-start.5) | collective-permute-done | bytes 98336 | tf_op jit(solution)/shard_map/cond/branch_1_fun/ppermute | solution.py:473
  203.4 3.2 %collective-permute-start.8 = (bf16[96,512]{1,0:T(8,128)(2,1)}, bf16[96,512]{1,0:T(8,128)(2,1)S(1)}, u32[]{:S(2)}, u32[]{:S(2)}) collective-permute-start(bf16[96,512]{1,0:T(8,128)(2,1)} %branch_1_fun.10.refs_0_), channel_id=1, source_target_pairs={{0,16},{8,24},{16,0},{24,8},{1,17},{9,25},{17,1},{25,9},{2,18},{10... | collective-permute-start | bytes 294920 | tf_op jit(solution)/shard_map/cond/branch_1_fun/ppermute | solution.py:473
  206.8 3.2 %collective-permute-done.9.refs_3_ = bf16[96,512]{1,0:T(8,128)(2,1)S(1)} collective-permute-done((bf16[96,512]{1,0:T(8,128)(2,1)}, bf16[96,512]{1,0:T(8,128)(2,1)S(1)}, u32[]{:S(2)}, u32[]{:S(2)}) %collective-permute-start.9) | collective-permute-done | bytes 98336 | tf_op jit(solution)/shard_map/cond/branch_1_fun/ppermute | solution.py:473
  210.0 4.6 %collective-permute-done.8.refs_2_ = bf16[96,512]{1,0:T(8,128)(2,1)S(1)} collective-permute-done((bf16[96,512]{1,0:T(8,128)(2,1)}, bf16[96,512]{1,0:T(8,128)(2,1)S(1)}, u32[]{:S(2)}, u32[]{:S(2)}) %collective-permute-start.8) | collective-permute-done | bytes 98336 | tf_op jit(solution)/shard_map/cond/branch_1_fun/ppermute | solution.py:473
  217.6 30.2 %all_to_all.27 = bf16[4,4,96,512]{3,2,1,0:T(8,128)(2,1)} all-to-all(bf16[4,4,96,512]{3,2,1,0:T(8,128)(2,1)} %branch_1_fun.11), channel_id=1, replica_groups=mesh['z'=4,'p'=4,'c'=2] {'p'}, dimensions={0} | all-to-all | bytes 3145728 | tf_op jit(solution)/shard_map/cond/branch_1_fun/all_to_all | solution.py:468
  251.5 4.9 %shard_map.374 = (f32[512,1536]{1,0:T(8,128)}, f32[512,512]{1,0:T(8,128)}, f32[768,512]{1,0:T(8,128)}, f32[512]{0:T(512)}, f32[512]{0:T(512)}, /*index=5*/f32[51...) custom-call(s32[1]{0:T(128)} %bitcast.21.core, ...), custom_call_target="tpu_custom_call" | custom-call | tf_op jit(solution)/shard_map/pallas_call | solution.py:452
  258.2 5.4 %all-reduce.4.cloned.1.call-done = (bf16[2048,512]{1,0:T(8,128)(2,1)}, bf16[512,2048]{1,0:T(8,128)(2,1)}) async-done(((bf16[2048,512]{1,0:T(8,128)(2,1)}, bf16[512,2048]{1,0:T(8,128)(2,1)}), (bf16[2048,512]{1,0:T(8,128)(2,1)}, bf16[512,2048]{1,0:T(8,128)(2,1)})) %all-reduce.4.cloned.1.call-update) | async-done | bytes 4194320 | tf_op jit(solution)/shard_map/psum | solution.py:679
  263.6 5.8 %shard_map.375 = (f32[2048,512]{1,0:T(8,128)}, f32[512,2048]{1,0:T(8,128)}) custom-call(bf16[2048,512]{1,0:T(8,128)(2,1)} %get-tuple-element.147.down, bf16[512,2048]{1,0:T(8,128)(2,1)} %get-tuple-element.148.up), custom_call_target="tpu_custom_call" | custom-call | tf_op jit(solution)/shard_map/pallas_call | solution.py:786
  (99 shorter events, 36.4 us)
Async XLA Ops:
  7.2 16.9 %copy-start = (f32[16,49]{1,0:T(8,128)S(1)}, f32[16,49]{1,0:T(8,128)}, u32[]{:S(2)}) copy-start(f32[16,49]{1,0:T(8,128)} %param.36) | copy-start | bytes 9412
  7.2 27.9 %all-to-all-start.3 = ((bf16[32,16,768]{2,1,0:T(8,128)(2,1)}), bf16[32,16,768]{2,1,0:T(8,128)(2,1)S(1)}, u32[]{:S(2)}, u32[]{:S(2)}) async-start(bf16[32,16,768]{2,1,0:T(8,128)(2,1)} %bitcast.40), calls=%async_computation.3 | async-start | bytes 1572864 | tf_op jit(solution)/shard_map/all_to_all | solution.py:468
  14.5 249.1 %all-reduce.4.cloned.1.call-start = ((), (), s32[]{:S(2)}) async-start(), calls=%async_computation.4 | async-start | bytes 8388608 | tf_op jit(solution)/shard_map/psum | solution.py:679
  17.2 11.0 %collective-permute-start.11 = (bf16[32,512]{1,0:T(8,128)(2,1)S(1)}, bf16[32,512]{1,0:T(8,128)(2,1)S(1)}, u32[]{:S(2)}, u32[]{:S(2)}) collective-permute-start(bf16[32,512]{1,0:T(8,128)(2,1)S(1)} %pad_maximum_fusion), channel_id=1, source_target_pairs={{0,31},{1,0},{2,1},{3,2},{4,3},{5,4},{6,5},{7,6},{8,7},{9,8},{10,9... | collective-permute-start | bytes 98312 | tf_op jit(solution)/shard_map/ppermute | solution.py:564
  24.1 9.2 %copy-start.21 = (s32[16,1]{1,0:T(8,128)S(1)}, s32[16,1]{1,0:T(8,128)}, u32[]{:S(2)}) copy-start(s32[16,1]{1,0:T(8,128)} %constant.129) | copy-start | bytes 196
  36.0 12.7 %collective-permute-start.12 = (bf16[16,768]{1,0:T(8,128)(2,1)}, bf16[16,768]{1,0:T(8,128)(2,1)S(1)}, u32[]{:S(2)}, u32[]{:S(2)}) collective-permute-start(bf16[16,768]{1,0:T(8,128)(2,1)} %shard_map.371.after), channel_id=1, source_target_pairs={{0,31},{1,0},{2,1},{3,2},{4,3},{5,4},{6,5},{7,6},{8,7},{9,8},{10,9... | collective-permute-start | bytes 73736 | tf_op jit(solution)/shard_map/ppermute | solution.py:614
  39.9 8.8 %copy-start.9 = (bf16[128,256]{1,0:T(8,128)(2,1)S(1)}, bf16[128,256]{1,0:T(8,128)(2,1)}, u32[]{:S(2)}) copy-start(bf16[128,256]{1,0:T(8,128)(2,1)} %constant.121.clone.ones) | copy-start | bytes 196612
  40.0 8.8 %copy-start.20 = (f32[512]{0:T(512)S(1)}, f32[512]{0:T(512)}, u32[]{:S(2)}) copy-start(f32[512]{0:T(512)} %param.34) | copy-start | bytes 6148
  135.1 3.6 %collective-permute-start.2 = (bf16[1024,512]{1,0:T(8,128)(2,1)}, bf16[1024,512]{1,0:T(8,128)(2,1)S(1)}, u32[]{:S(2)}, u32[]{:S(2)}) collective-permute-start(bf16[1024,512]{1,0:T(8,128)(2,1)} %get-tuple-element.60), channel_id=1, source_target_pairs={{0,1},{1,0},{2,3},{3,2},{4,5},{5,4},{6,7},{7,6},{8,9},{9,8},{10,11... | collective-permute-start | bytes 3145736 | tf_op jit(solution)/shard_map/cond/branch_1_fun/ppermute | solution.py:464
  135.1 3.6 %collective-permute-start.3 = (bf16[512,512]{1,0:T(8,128)(2,1)}, bf16[512,512]{1,0:T(8,128)(2,1)S(1)}, u32[]{:S(2)}, u32[]{:S(2)}) collective-permute-start(bf16[512,512]{1,0:T(8,128)(2,1)} %get-tuple-element.62), channel_id=1, source_target_pairs={{0,1},{1,0},{2,3},{3,2},{4,5},{5,4},{6,7},{7,6},{8,9},{9,8},{10,11... | collective-permute-start | bytes 1572872 | tf_op jit(solution)/shard_map/cond/branch_1_fun/ppermute | solution.py:464
  143.8 23.8 %all-to-all-start.1 = ((bf16[4,384,512]{2,1,0:T(8,128)(2,1)}), bf16[4,384,512]{2,1,0:T(8,128)(2,1)S(1)}, u32[]{:S(2)}, u32[]{:S(2)}) async-start(bf16[4,384,512]{2,1,0:T(8,128)(2,1)} %branch_1_fun.7.after_a), calls=%async_computation.1 | async-start | bytes 3145728 | tf_op jit(solution)/shard_map/cond/branch_1_fun/all_to_all | solution.py:468
  147.4 7.0 %collective-permute-start = (bf16[16,512]{1,0:T(8,128)(2,1)S(1)}, bf16[16,512]{1,0:T(8,128)(2,1)S(1)}, u32[]{:S(2)}, u32[]{:S(2)}) collective-permute-start(bf16[16,512]{1,0:T(8,128)(2,1)S(1)} %get-tuple-element.41), channel_id=1, source_target_pairs={{0,1},{1,2},{2,3},{3,4},{4,5},{5,6},{6,7},{7,8},{8,9},{9,10},{10,1... | collective-permute-start | bytes 49160 | tf_op jit(solution)/shard_map/cond/branch_1_fun/ppermute | solution.py:739
  148.3 6.9 %collective-permute-start.1 = (bf16[16,512]{1,0:T(8,128)(2,1)S(1)}, bf16[16,512]{1,0:T(8,128)(2,1)S(1)}, u32[]{:S(2)}, u32[]{:S(2)}) collective-permute-start(bf16[16,512]{1,0:T(8,128)(2,1)S(1)} %slice.14), channel_id=1, source_target_pairs={{0,1},{1,2},{2,3},{3,4},{4,5},{5,6},{6,7},{7,8},{8,9},{9,10},{10,1... | collective-permute-start | bytes 49160 | tf_op jit(solution)/shard_map/cond/branch_1_fun/ppermute | solution.py:736
  167.6 39.2 %all-to-all-start = ((bf16[32,16,512]{2,1,0:T(8,128)(2,1)}), bf16[32,16,512]{2,1,0:T(8,128)(2,1)S(1)}, u32[]{:S(2)}, u32[]{:S(2)}) async-start(bf16[32,16,512]{2,1,0:T(8,128)(2,1)} %bitcast.35), calls=%async_computation | async-start | bytes 1048576 | tf_op jit(solution)/shard_map/cond/branch_1_fun/all_to_all | solution.py:468
  178.5 10.8 %collective-permute-start.4 = (bf16[96,512]{1,0:T(8,128)(2,1)}, bf16[96,512]{1,0:T(8,128)(2,1)S(1)}, u32[]{:S(2)}, u32[]{:S(2)}) collective-permute-start(bf16[96,512]{1,0:T(8,128)(2,1)} %get-tuple-element.66), channel_id=1, source_target_pairs={{0,8},{8,0},{16,24},{24,16},{1,9},{9,1},{17,25},{25,17},{2,10},{10... | collective-permute-start | bytes 294920 | tf_op jit(solution)/shard_map/cond/branch_1_fun/ppermute | solution.py:473
  180.3 19.7 %collective-permute-start.5 = (bf16[96,512]{1,0:T(8,128)(2,1)}, bf16[96,512]{1,0:T(8,128)(2,1)S(1)}, u32[]{:S(2)}, u32[]{:S(2)}) collective-permute-start(bf16[96,512]{1,0:T(8,128)(2,1)} %get-tuple-element.67), channel_id=1, source_target_pairs={{0,16},{8,24},{16,0},{24,8},{1,17},{9,25},{17,1},{25,9},{2,18},{10... | collective-permute-start | bytes 294920 | tf_op jit(solution)/shard_map/cond/branch_1_fun/ppermute | solution.py:473
  182.7 17.3 %collective-permute-start.6 = (bf16[96,512]{1,0:T(8,128)(2,1)}, bf16[96,512]{1,0:T(8,128)(2,1)S(1)}, u32[]{:S(2)}, u32[]{:S(2)}) collective-permute-start(bf16[96,512]{1,0:T(8,128)(2,1)} %get-tuple-element.68), channel_id=1, source_target_pairs={{0,24},{8,16},{16,8},{24,0},{1,25},{9,17},{17,9},{25,1},{2,26},{10... | collective-permute-start | bytes 294920 | tf_op jit(solution)/shard_map/cond/branch_1_fun/ppermute | solution.py:473
  189.3 10.7 %copy-start.14 = (bf16[96,512]{1,0:T(8,128)(2,1)}, bf16[96,512]{1,0:T(8,128)(2,1)S(1)}, u32[]{:S(2)}) copy-start(bf16[96,512]{1,0:T(8,128)(2,1)S(1)} %collective-permute-done.4.refs_1_) | copy-start | bytes 294916 | tf_op jit(solution)/shard_map/cond
  202.4 7.6 %collective-permute-start.9 = (bf16[96,512]{1,0:T(8,128)(2,1)}, bf16[96,512]{1,0:T(8,128)(2,1)S(1)}, u32[]{:S(2)}, u32[]{:S(2)}) collective-permute-start(bf16[96,512]{1,0:T(8,128)(2,1)} %branch_1_fun.10.refs_0_), channel_id=1, source_target_pairs={{0,24},{8,16},{16,8},{24,0},{1,25},{9,17},{17,9},{25,1},{2,26},{10... | collective-permute-start | bytes 294920 | tf_op jit(solution)/shard_map/cond/branch_1_fun/ppermute | solution.py:473
  203.4 11.2 %collective-permute-start.8 = (bf16[96,512]{1,0:T(8,128)(2,1)}, bf16[96,512]{1,0:T(8,128)(2,1)S(1)}, u32[]{:S(2)}, u32[]{:S(2)}) collective-permute-start(bf16[96,512]{1,0:T(8,128)(2,1)} %branch_1_fun.10.refs_0_), channel_id=1, source_target_pairs={{0,16},{8,24},{16,0},{24,8},{1,17},{9,25},{17,1},{25,9},{2,18},{10... | collective-permute-start | bytes 294920 | tf_op jit(solution)/shard_map/cond/branch_1_fun/ppermute | solution.py:473
  206.7 8.0 %collective-permute-start.7 = (bf16[96,512]{1,0:T(8,128)(2,1)}, bf16[96,512]{1,0:T(8,128)(2,1)S(1)}, u32[]{:S(2)}, u32[]{:S(2)}) collective-permute-start(bf16[96,512]{1,0:T(8,128)(2,1)} %branch_1_fun.10.refs_0_), channel_id=1, source_target_pairs={{0,8},{8,0},{16,24},{24,16},{1,9},{9,1},{17,25},{25,17},{2,10},{10... | collective-permute-start | bytes 294920 | tf_op jit(solution)/shard_map/cond/branch_1_fun/ppermute | solution.py:473
  217.6 30.2 %copy-start.18 = (bf16[16,512]{1,0:T(8,128)(2,1)S(1)}, bf16[16,512]{1,0:T(8,128)(2,1)}, u32[]{:S(2)}) copy-start(bf16[16,512]{1,0:T(8,128)(2,1)} %copy-done.17) | copy-start | bytes 49156 | tf_op jit(solution)/shard_map/cond
  217.6 30.8 %copy-start.5 = (bf16[32,16,512]{2,1,0:T(8,128)(2,1)S(1)}, bf16[32,16,512]{2,1,0:T(8,128)(2,1)}, u32[]{:S(2)}) copy-start(bf16[32,16,512]{2,1,0:T(8,128)(2,1)} %copy-done.4) | copy-start | bytes 1572868 | tf_op jit(solution)/shard_map/cond
  247.8 3.8 %collective-permute-start.10 = (bf16[4,384,512]{2,1,0:T(8,128)(2,1)}, bf16[4,384,512]{2,1,0:T(8,128)(2,1)}, u32[]{:S(2)}, u32[]{:S(2)}) collective-permute-start(bf16[4,384,512]{2,1,0:T(8,128)(2,1)} %bitcast.8), channel_id=1, source_target_pairs={{0,1},{1,0},{2,3},{3,2},{4,5},{5,4},{6,7},{7,6},{8,9},{9,8},{10,11... | collective-permute-start | bytes 4718600 | tf_op jit(solution)/shard_map/cond/branch_1_fun/ppermute | solution.py:464
  (15 other events, 56.0 us)
Sparse Core Ops, SparseCore 0:
  105.9 157.6 all-reduce.3

commit v4 on v3

--- a/solution.py
+++ b/solution.py
@@ -24,7 +24,7 @@
 SCALE = HD ** (-0.5)
 PRECISE = lax.Precision.HIGHEST
 VMEM_LIMIT = 60 * 2**20
-FEED_PIECE = 1024
+FEED_PIECE = 2048
 bf16 = jnp.bfloat16
 f32 = jnp.float32
 AXES = ("z", "p", "c")
@@ -107,9 +107,8 @@
 
 def first_kernel(
     cut, arrived, rim, embed_w, embed_b, places, positions, mask_token, gain1, qkv_w, bias,
-    across, ones, out_w, out_b, gain2, cotangent, grad_act, up_w, up_b, down_w, down_b, order,
-    start_o, qkv_o, probs_o, grad_context_o, grad_middle_o, down_o, up_o, out_grad_o, sums_o,
-    up_bias_o, out_o, rim_o, slots_s, score_s, context_s, down_s, up_s, out_s,
+    across, ones, out_w, out_b, gain2, cotangent, down_w, up_w, up_b, start_o, qkv_o, probs_o,
+    context_o, middle_o, act_o, grad_up_o, down_o, up_o, up_bias_o, slots_s, score_s, down_s, up_s,
 ):
     rows, width = start_o.shape
     own = arrived.shape[0]
@@ -123,9 +122,7 @@
         slots_s[own:, :] = (mm(rim[...], embed_w[...]) + embed_b[...]).astype(bf16)
         down_s[...] = jnp.zeros_like(down_s)
         up_s[...] = jnp.zeros_like(up_s)
-        out_s[...] = jnp.zeros_like(out_s)
         up_bias_o[...] = jnp.zeros_like(up_bias_o)
-        sums_o[...] = jnp.zeros_like(sums_o)
 
     onehot = slot_onehot(step, rows, places[...])
     seen = jnp.sum(onehot, axis=1, keepdims=True)
@@ -151,70 +148,39 @@
         for o in range(HEADS // OCT):
             r, s = head_slices(w, o)
             v = qkv_o[r, 2 * width + o * OCT_D : 2 * width + (o + 1) * OCT_D]
-            context_s[r, o * OCT_D : (o + 1) * OCT_D] = own_heads(
+            context_o[r, o * OCT_D : (o + 1) * OCT_D] = own_heads(
                 mm_tn(probs_o[r, s].astype(bf16), v)
             ).astype(bf16)
-    middle = start_o[...] + mm(context_s[...], out_w[...]) + out_b[...]
-    n2, r2 = normalized(middle)
-    h_two = (n2 * gain2[...]).astype(bf16)
+    middle = start_o[...] + mm(context_o[...], out_w[...]) + out_b[...]
+    middle_o[...] = middle
+    h_two = (normalized(middle)[0] * gain2[...]).astype(bf16)
 
     cot = cotangent[...]
     piece = min(FEED_PIECE, hidden)
-    grad_h = None
-    result = middle + down_b[...]
     for at in range(0, hidden, piece):
         f = slice(at, at + piece)
         up_value = mm(h_two, up_w[:, f]) + up_b[:, f]
         below = 0.5 * (1.0 + lax.erf(up_value * (0.5**0.5)))
         act = (up_value * below).astype(bf16)
+        act_o[:, f] = act
         slope = below + up_value * (jnp.exp(-0.5 * up_value * up_value) * 0.3989422804014327)
-        grad_up = grad_act[:, f].astype(f32) * slope
+        grad_up = mm_nt(cot, down_w[f, :]) * slope
         up_bias_o[:, f] += jnp.sum(grad_up, axis=0, keepdims=True)
         grad_low = grad_up.astype(bf16)
-        result = result + mm(act, down_w[f, :])
+        grad_up_o[:, f] = grad_low
         down_s[f, :] += mm_tn(act, cot)
         up_s[:, f] += mm_tn(h_two, grad_low)
-        part = mm_nt(grad_low, up_w[:, f])
-        grad_h = part if grad_h is None else grad_h + part
-
-    result = result.astype(bf16)
-    block = order.shape[0]
-    result = jnp.concatenate(
-        [mm_tn(order[...], result[b : b + block]).astype(bf16) for b in range(0, rows, block)],
-        axis=0,
-    )
-
-    @pl.when(jnp.logical_not(last))
-    def _():
-        out_o[pl.ds(pl.multiple_of(step * rows + RIM, RIM), rows), :] = result
-
-    @pl.when(last)
-    def _():
-        out_o[pl.ds(pl.multiple_of(step * rows + RIM, RIM), rows - RIM), :] = result[: rows - RIM]
-        rim_o[...] = result[rows - RIM :]
-        out_o[0:RIM, :] = jnp.zeros((RIM, width), bf16)
-
-    wide_cot = cot.astype(f32)
-    sums_o[0:1, :] += jnp.sum(grad_h * n2, axis=0, keepdims=True)
-    grad_middle = wide_cot + norm_back(grad_h * gain2[...], n2, r2)
-    grad_middle_o[...] = grad_middle
-    sums_o[1:2, :] += jnp.sum(grad_middle, axis=0, keepdims=True)
-    sums_o[2:3, :] += jnp.sum(wide_cot, axis=0, keepdims=True)
-    grad_middle_low = grad_middle.astype(bf16)
-    out_s[...] += mm_tn(context_s[...], grad_middle_low)
-    grad_context_o[...] = mm_nt(grad_middle_low, out_w[...]).astype(bf16)
 
     @pl.when(last)
     def _():
         down_o[...] = down_s[...].astype(bf16)
         up_o[...] = up_s[...].astype(bf16)
-        out_grad_o[...] = out_s[...].astype(bf16)
 
 
 def second_kernel(
-    core, grad_context, qkv, probs, start, grad_middle, places, qkv_w, gain1, ones, arrived, rim,
-    out_grad, sums, up_bias, slots_o, keep_c_o, send_c_o, keep_d_o, send_d_o, gqkv_s,
-    qkv_s, score_s, slots_s, embed_s, sums_s, rel_s,
+    core, qkv, probs, start, grad_up, middle, context, cotangent, places, qkv_w, gain1, ones,
+    arrived, rim, up_bias, up_w, gain2, out_w, slots_o, keep_c_o, send_c_o, keep_d_o, send_d_o,
+    gqkv_s, qkv_s, score_s, slots_s, embed_s, sums_s, rel_s, out_s, grad_context_s, grad_middle_s,
 ):
     step = pl.program_id(0)
     rows, width = start.shape
@@ -228,14 +194,26 @@
         sums_s[...] = jnp.zeros_like(sums_s)
         embed_s[...] = jnp.zeros_like(embed_s)
         rel_s[...] = jnp.zeros_like(rel_s)
-
+        out_s[...] = jnp.zeros_like(out_s)
+
+    cot = cotangent[...].astype(f32)
+    grad_h_two = mm_nt(grad_up[...], up_w[...])
+    n2, r2 = normalized(middle[...])
+    sums_s[0:1, :] += jnp.sum(grad_h_two * n2, axis=0, keepdims=True)
+    grad_middle = cot + norm_back(grad_h_two * gain2[...], n2, r2)
+    grad_middle_s[...] = grad_middle
+    sums_s[1:2, :] += jnp.sum(grad_middle, axis=0, keepdims=True)
+    sums_s[2:3, :] += jnp.sum(cot, axis=0, keepdims=True)
+    grad_middle_low = grad_middle.astype(bf16)
+    out_s[...] += mm_tn(context[...], grad_middle_low)
+    grad_context_s[...] = mm_nt(grad_middle_low, out_w[...]).astype(bf16)
     block_ones = ones[...]
     for w in range(windows):
         for o in range(HEADS // OCT):
             r, s = head_slices(w, o)
             heads = slice(o * OCT_D, (o + 1) * OCT_D)
             v_at = slice(2 * width + o * OCT_D, 2 * width + (o + 1) * OCT_D)
-            wide = spread(grad_context[r, heads], block_ones)
+            wide = spread(grad_context_s[r, heads], block_ones)
             score_s[r, s] = mm_nt(qkv[r, v_at], wide)
             gqkv_s[r, v_at] = mm(probs[r, s].astype(bf16), wide).astype(bf16)
     pr = probs[...].reshape(windows, SPOTS, HEADS * SPOTS)
@@ -258,7 +236,7 @@
     qkv_s[...] += mm_tn(h_one, gqkv_s[...])
     grad_h_one = mm_nt(gqkv_s[...], qkv_w[...])
     sums_s[3:4, :] += jnp.sum(grad_h_one * n1, axis=0, keepdims=True)
-    grad_start = grad_middle[...] + norm_back(grad_h_one * gain1[...], n1, r1)
+    grad_start = grad_middle_s[...] + norm_back(grad_h_one * gain1[...], n1, r1)
     onehot = slot_onehot(step, rows, places[...])
     hidden = 1.0 - jnp.sum(onehot, axis=1, keepdims=True)
     sums_s[4:5, :] += jnp.sum(hidden * grad_start, axis=0, keepdims=True)
@@ -268,7 +246,7 @@
         low_o[0:width, :] = qkv_s[:, 0:width].astype(bf16)
         low_o[width : 2 * width, :] = qkv_s[:, width : 2 * width].astype(bf16)
         high_o[0:width, :] = qkv_s[:, 2 * width : 3 * width].astype(bf16)
-        high_o[width : 2 * width, :] = out_grad[...]
+        high_o[width : 2 * width, :] = out_s[...].astype(bf16)
 
     def give_d(low_o, high_o):
         half = low_o.shape[0]
@@ -288,7 +266,6 @@
         slots = slots_s[...].astype(bf16)
         slots_o[...] = slots
         embed_s[0:e_in, :] = mm_tn(arrived[...], slots[0:own]) + mm_tn(rim[...], slots[own:])
-        sums_s[0:3, :] = sums[0:3, :]
         sums_s[5:6, :] = jnp.sum(slots.astype(f32), axis=0, keepdims=True)
         for block in range(up_bias.shape[1] // width):
             sums_s[6 + block : 7 + block, :] = up_bias[:, block * width : (block + 1) * width]
@@ -302,22 +279,12 @@
     def _():
         give_c(send_c_o, keep_c_o)
         give_d(send_d_o, keep_d_o)
-
-
-def rim_kernel(hot, arrived, after, out):
-    del after
-    out[...] = mm(hot[...], arrived[...]).astype(bf16)
 
 
 def rim_back_kernel(hot, rim_grad, grad_slots, after_a, after_b, out):
     del after_a, after_b
     slots = out.shape[0]
     out[...] = (grad_slots[0:slots, :].astype(f32) + mm_tn(hot[...], rim_grad[...])).astype(bf16)
-
-
-def act_back_kernel(cotangent, down_w, after, out):
-    del after
-    out[...] = mm_nt(cotangent[...], down_w[...]).astype(bf16)
 
 
 def prepare_kernel(cotangent, next_cot, pos_embed, order, cot_o, positions_o):
@@ -338,6 +305,33 @@
         positions_o[at : at + block, :] = jnp.dot(
             order[...], rows, precision=PRECISE, preferred_element_type=f32
         )
+
+
+def out_kernel(
+    middle, act, down, down_bias, order, after, out_o, rim_o
+):
+    del after
+    step = pl.program_id(0)
+    last = pl.num_programs(0) - 1
+    rows = middle.shape[0]
+    block = order.shape[0]
+    result = (
+        middle[...] + mm(act[...], down[...]) + down_bias[...]
+    ).astype(bf16)
+    result = jnp.concatenate(
+        [mm_tn(order[...], result[b : b + block]).astype(bf16) for b in range(0, rows, block)],
+        axis=0,
+    )
+
+    @pl.when(step < last)
+    def _():
+        out_o[pl.ds(pl.multiple_of(step * rows + RIM, RIM), rows), :] = result
+
+    @pl.when(step == last)
+    def _():
+        out_o[pl.ds(pl.multiple_of(step * rows + RIM, RIM), rows - RIM), :] = result[: rows - RIM]
+        rim_o[...] = result[rows - RIM :]
+        out_o[0:RIM, :] = jnp.zeros((RIM, result.shape[1]), bf16)
 
 
 def chip_join_kernel(count, *refs):
@@ -605,94 +599,74 @@
     tm = min(512, tokens)
     grid = (tokens // tm,)
     pos_blocks = pos_embed.shape[0] // tm
-    rim_rows = at_once(
-        rim_kernel,
-        (rim_hot, arrived, cot),
-        shape((RIM, e_in), bf16),
-        [whole(rim_hot.shape), whole(arrived.shape), ANY],
-    )
+    rim_rows = jnp.dot(rim_hot, arrived, preferred_element_type=f32).astype(bf16)
     next_rows = lax.ppermute(rim_rows, AXES, back)
-    grad_act = pl.pallas_call(
-        act_back_kernel,
-        grid=grid,
-        in_specs=[tile(tm, width), whole((hidden, width)), ANY],
-        out_specs=tile(tm, hidden),
-        out_shape=shape((tokens, hidden), bf16),
-        compiler_params=params(),
-    )(cot, down_weight, rim_rows)
     rim = jnp.pad(next_rows, ((0, RIM_SLOTS - RIM), (0, 0)))
     first_args = [
         cut, arrived, rim, embed_weight, row(embed_bias), places, positions,
         row(mask_token), row(norm1_gain), qkv_weight, bias, apart, ones, out_weight,
-        row(out_bias), row(norm2_gain), cot, grad_act, up_weight, row(up_bias), down_weight,
-        row(down_bias), jnp.asarray(order, bf16),
+        row(out_bias), row(norm2_gain), cot, down_weight, up_weight, row(up_bias),
     ]
     specs = [SMEM] + [held(a.shape) for a in first_args[1:]]
     specs[6] = pl.BlockSpec((tm, width), lambda i: (lax.rem(i, pos_blocks), 0))
     specs[16] = tile(tm, width)
-    specs[17] = tile(tm, hidden)
-    (
-        start, qkv, probs, grad_context, grad_middle, down_grad, up_grad, out_grad, sums,
-        up_bias_grad, out, rim_out,
-    ) = pl.pallas_call(
-        first_kernel,
-        grid=grid,
-        in_specs=specs,
-        out_specs=[
-            tile(tm, width),
-            tile(tm, 3 * width),
-            tile(tm, HEADS * SPOTS),
-            tile(tm, width),
-            tile(tm, width),
-            whole((hidden, width)),
-            whole((width, hidden)),
-            whole((width, width)),
-            whole((8, width)),
-            whole((1, hidden)),
-            whole((tokens, width)),
-            whole((RIM, width)),
-        ],
-        out_shape=[
-            shape((tokens, width), f32),
-            shape((tokens, 3 * width), bf16),
-            shape((tokens, HEADS * SPOTS), f32),
-            shape((tokens, width), bf16),
-            shape((tokens, width), f32),
-            shape((hidden, width), bf16),
-            shape((width, hidden), bf16),
-            shape((width, width), bf16),
-            shape((8, width), f32),
-            shape((1, hidden), f32),
-            shape((tokens, width), bf16),
-            shape((RIM, width), bf16),
-        ],
-        scratch_shapes=[
-            pltpu.VMEM((ext, width), bf16),
-            pltpu.VMEM((tm, HEADS * SPOTS), f32),
-            pltpu.VMEM((tm, width), bf16),
-            pltpu.VMEM((hidden, width), f32),
-            pltpu.VMEM((width, hidden), f32),
-            pltpu.VMEM((width, width), f32),
-        ],
-        compiler_params=params(),
-    )(*first_args)
+    start, qkv, probs, context, middle, act, grad_up, down_grad, up_grad, up_bias_grad = (
+        pl.pallas_call(
+            first_kernel,
+            grid=grid,
+            in_specs=specs,
+            out_specs=[
+                tile(tm, width),
+                tile(tm, 3 * width),
+                tile(tm, HEADS * SPOTS),
+                tile(tm, width),
+                tile(tm, width),
+                tile(tm, hidden),
+                tile(tm, hidden),
+                whole((hidden, width)),
+                whole((width, hidden)),
+                whole((1, hidden)),
+            ],
+            out_shape=[
+                shape((tokens, width), f32),
+                shape((tokens, 3 * width), bf16),
+                shape((tokens, HEADS * SPOTS), f32),
+                shape((tokens, width), bf16),
+                shape((tokens, width), f32),
+                shape((tokens, hidden), bf16),
+                shape((tokens, hidden), bf16),
+                shape((hidden, width), bf16),
+                shape((width, hidden), bf16),
+                shape((1, hidden), f32),
+            ],
+            scratch_shapes=[
+                pltpu.VMEM((ext, width), bf16),
+                pltpu.VMEM((tm, HEADS * SPOTS), f32),
+                pltpu.VMEM((hidden, width), f32),
+                pltpu.VMEM((width, hidden), f32),
+            ],
+            compiler_params=params(),
+        )(*first_args)
+    )
     down_sum, up_sum = lax.psum((down_grad, up_grad), AXES)
 
     unit = 16 * planes * cells
     half = -(-width // unit) * unit
     def rest(operands):
         (
-            grad_context, qkv, probs, start, grad_middle, places, arrived, rim, rim_hot, out_grad,
-            sums, up_bias_grad, out, rim_out,
+            qkv, probs, start, grad_up, middle, context, cot, act, places, arrived, rim, rim_hot,
+            up_bias_grad,
         ) = operands
         grad_slots, keep_c, send_c, keep_d, send_d = pl.pallas_call(
             second_kernel,
             grid=grid,
             in_specs=[
                 SMEM,
-                tile(tm, width),
                 tile(tm, 3 * width),
                 tile(tm, HEADS * SPOTS),
+                tile(tm, width),
+                tile(tm, hidden),
+                tile(tm, width),
                 tile(tm, width),
                 tile(tm, width),
                 held((1, ext)),
@@ -701,9 +675,10 @@
                 held((OCT_S, OCT_D)),
                 held((slots, e_in)),
                 held((RIM_SLOTS, e_in)),
+                held((1, hidden)),
+                held((width, hidden)),
+                held((1, width)),
                 held((width, width)),
-                held((8, width)),
-                held((1, hidden)),
             ],
             out_specs=[
                 whole((ext, width)),
@@ -727,20 +702,40 @@
                 pltpu.VMEM((max(e_in, half), width), f32),
                 pltpu.VMEM((16, width), f32),
                 pltpu.VMEM((SPOTS, HEADS * SPOTS), f32),
+                pltpu.VMEM((width, width), f32),
+                pltpu.VMEM((tm, width), bf16),
+                pltpu.VMEM((tm, width), f32),
             ],
             compiler_params=params(),
         )(
-            core, grad_context, qkv, probs, start, grad_middle, places, qkv_weight, row(norm1_gain),
-            ones, arrived, rim, out_grad, sums, up_bias_grad,
+            core, qkv, probs, start, grad_up, middle, context, cot, places, qkv_weight,
+            row(norm1_gain), ones, arrived, rim, up_bias_grad, up_weight, row(norm2_gain),
+            out_weight,
         )
         rim_grad = lax.ppermute(grad_slots[slots : slots + RIM], AXES, ahead)
         shares = chip_join([(keep_c, send_c), (keep_d, send_d)], ())
         part = exchange(shares, "p")
+        out, rim_out = pl.pallas_call(
+            out_kernel,
+            grid=grid,
+            in_specs=[
+                tile(tm, width),
+                tile(tm, hidden),
+                held((hidden, width)),
+                held((1, width)),
+                held(order.shape),
+                ANY,
+            ],
+            out_specs=[whole((tokens, width)), whole((RIM, width))],
+            out_shape=[shape((tokens, width), bf16), shape((RIM, width), bf16)],
+            compiler_params=params(),
+        )(middle, act, down_weight, row(down_bias), jnp.asarray(order, bf16), shares)
         first_rows = lax.ppermute(rim_out, AXES, ahead)
         out = lax.dynamic_update_slice(out, first_rows, (0, 0))
+        sums_c = plane_sum(z_place, [part], rim_out)
         grad_embedded = at_once(
             rim_back_kernel,
-            (rim_hot, rim_grad, grad_slots, shares, first_rows),
+            (rim_hot, rim_grad, grad_slots, sums_c[0], first_rows),
             shape((slots, width), bf16),
             [whole(a.shape) for a in (rim_hot, rim_grad, grad_slots)] + [ANY, ANY],
         )
@@ -748,7 +743,6 @@
         grad_visible = lax.dot_general(
             returned, embed_weight, (((1,), (1,)), ((), ())), preferred_element_type=f32
         ).astype(bf16)
-        sums_c = plane_sum(z_place, [part], grad_embedded)
         total = z_sum([sums_c[0], *across(sums_c, "z")], ())
         joined = z_join(z_place, [total, *across([total] * planes, "z")], (returned,))
         mine = exchange(joined, "p").reshape(cells, -1, width)
@@ -758,8 +752,8 @@
         return tuple(jnp.zeros(o.shape, o.dtype) for o in jax.eval_shape(rest, operands))
 
     operands = (
-        grad_context, qkv, probs, start, grad_middle, places, arrived, rim, rim_hot, out_grad,
-        sums, up_bias_grad, out, rim_out,
+        qkv, probs, start, grad_up, middle, context, cot, act, places, arrived, rim, rim_hot,
+        up_bias_grad,
     )
     out, grad_visible, mine, other = lax.cond(device_rank < device_count, rest, nothing, operands)
 

time: 277 us -> 268 us (0.968)
  starting transfers between devices: 39.9 us -> 34.3 us
  blocking collectives: 30.2 us -> 25.3 us
  waiting for transfers between devices: 52.5 us -> 49.7 us
    pallas_call x2, Pallas kernels: 38 us -> 50.5 us  [the longest x1 40.7 us: rest(): pl.pallas_call(second_kernel, grid=grid, in_specs=[SMEM, tile(tm, 3 * wid...]
    pallas_call x1, Pallas kernels: 57 us -> 47.5 us  [per_device(): pl.pallas_call(first_kernel, grid=grid, in_specs=specs, out_specs=[tile(t...]
    psum x1, waiting for transfers between devices: 5.38 us -> 0.01 us  [per_device(): down_sum, up_sum = lax.psum((down_grad, up_grad), AXES)]
    all_to_all x3, starting transfers between devices: 19.4 us -> 14.2 us  [exchange(): return lax.all_to_all(x, axis, 0, 0, tiled=True)]
    all_to_all x1, blocking collectives: 30.2 us -> 25.3 us  [exchange(): return lax.all_to_all(x, axis, 0, 0, tiled=True)]
    ppermute x1, waiting for transfers between devices: 4.15 us -> 0.01 us  [rest(): first_rows = lax.ppermute(rim_out, AXES, ahead)]
    all_to_all x3, waiting for transfers between devices: 11.2 us -> 15.2 us  [exchange(): return lax.all_to_all(x, axis, 0, 0, tiled=True)]
    ppermute x6, waiting for transfers between devices: 24.9 us -> 28.5 us  [across(): lax.ppermute(x[b], axis, [(i, i ^ b) for i in range(size)])]
  transfers between devices with their start and end apart: 17 -> 17, of which waited for: 12 -> 9; matrix products, arithmetic and copies ran while one was open for 5% -> 5% of each run, Pallas kernels for 22% -> 27%
where the time goes in v4:
time: 268 us; the launch traced here: 267 us
  Pallas kernels  126 us (47%)
  waiting for transfers between devices  49.7 us (19%)
  starting transfers between devices  34.3 us (13%)
  blocking collectives  25.3 us (9%)
  between operations  14.2 us (5%)
  local copies, waits for them, and re-layouts  11.4 us (4%)
  matrix products  3.87 us (1%)
    pallas_call x1, Pallas kernels, per_device(): pl.pallas_call(first_kernel, grid=grid, in_specs=specs, out_specs=[tile(t...  47.5 us
    pallas_call x1, Pallas kernels, rest(): pl.pallas_call(second_kernel, grid=grid, in_specs=[SMEM, tile(tm, 3 * wid...  40.7 us
    ppermute x6, waiting for transfers between devices, across(): lax.ppermute(x[b], axis, [(i, i ^ b) for i in range(size)])  28.5 us
    all_to_all x1, blocking collectives, exchange(): return lax.all_to_all(x, axis, 0, 0, tiled=True)  25.3 us
    pallas_call x6, Pallas kernels, at_once(): pl.pallas_call(kernel, grid=(1,), in_specs=specs, out_specs=out_specs, ou...  18 us
    all_to_all x3, waiting for transfers between devices, exchange(): return lax.all_to_all(x, axis, 0, 0, tiled=True)  15.2 us
    all_to_all x3, starting transfers between devices, exchange(): return lax.all_to_all(x, axis, 0, 0, tiled=True)  14.2 us
    pallas_call x1, Pallas kernels, rest(): pl.pallas_call(out_kernel, grid=grid, in_specs=[tile(tm, width), tile(tm,...  9.81 us
  transfers between devices with their start and end apart: 17, of which 9 were waited for; matrix products, arithmetic and copies ran while one was open for 5% of the time, Pallas kernels for 27%

profile of v4, /device:TPU:0, one launch (start us, length us, event | category | flops | bytes accessed | tf_op | source)
XLA Modules:
  0.0 267.0 jit_solution(9043029527997424779)
XLA Ops:
  7.2 7.3 %all-to-all-start.3 = ((bf16[32,16,768]{2,1,0:T(8,128)(2,1)}), bf16[32,16,768]{2,1,0:T(8,128)(2,1)S(1)}, u32[]{:S(2)}, u32[]{:S(2)}) async-start(bf16[32,16,768]{2,1,0:T(8,128)(2,1)} %bitcast.42), calls=%async_computation.3 | async-start | bytes 1572864 | tf_op jit(solution)/shard_map/all_to_all | solution.py:462
  17.2 5.2 %collective-permute-start.12 = (bf16[32,512]{1,0:T(8,128)(2,1)S(1)}, bf16[32,512]{1,0:T(8,128)(2,1)S(1)}, u32[]{:S(2)}, u32[]{:S(2)}) collective-permute-start(bf16[32,512]{1,0:T(8,128)(2,1)S(1)} %pad_maximum_fusion), channel_id=1, source_target_pairs={{0,31},{1,0},{2,1},{3,2},{4,3},{5,4},{6,5},{7,6},{8,7},{9,8},{10,9... | collective-permute-start | bytes 98312 | tf_op jit(solution)/shard_map/ppermute | solution.py:558
  28.4 6.8 %all-to-all-done.3 = bf16[32,16,768]{2,1,0:T(8,128)(2,1)S(1)} async-done(((bf16[32,16,768]{2,1,0:T(8,128)(2,1)}), bf16[32,16,768]{2,1,0:T(8,128)(2,1)S(1)}, u32[]{:S(2)}, u32[]{:S(2)}) %all-to-all-start.3) | async-done | bytes 786464 | tf_op jit(solution)/shard_map/all_to_all | solution.py:462
  35.4 2.9 %collective-permute-start.11 = (bf16[16,768]{1,0:T(8,128)(2,1)S(1)}, bf16[16,768]{1,0:T(8,128)(2,1)S(1)}, u32[]{:S(2)}, u32[]{:S(2)}) collective-permute-start(bf16[16,768]{1,0:T(8,128)(2,1)S(1)} %convolution_convert_fusion.1), channel_id=1, source_target_pairs={{0,31},{1,0},{2,1},{3,2},{4,3},{5,4},{6,5},{7,6},{8,7},{9,8},{10,9... | collective-permute-start | bytes 73736 | tf_op jit(solution)/shard_map/ppermute | solution.py:603
  39.0 4.5 %shard_map.372 = (bf16[2048,512]{1,0:T(8,128)(2,1)}, f32[512,512]{1,0:T(8,128)}) custom-call(bf16[2048,512]{1,0:T(8,128)(2,1)} %cotangent.1, bf16[16,512]{1,0:T(8,128)(2,1)} %slice.30.next_cot, f32[512,512]{1,0:T(8,128)} %pos_embed.1, f32[256,256]{1,0:T(8,128)} %constant.122.clone.order), custom_call_target="tpu_custom_call" | custom-call | tf_op jit(solution)/shard_map/pallas_call | solution.py:446
  43.6 47.5 %shard_map.373 = (f32[2048,512]{1,0:T(8,128)}, bf16[2048,1536]{1,0:T(8,128)(2,1)}, f32[2048,256]{1,0:T(8,128)}, bf16[2048,512]{1,0:T(8,128)(2,1)}, f32[2048,512]...) custom-call(f32[128]{0:T(128)} %reshape.130.cut, ...), custom_call_target="tpu_custom_call" | custom-call | tf_op jit(solution)/shard_map/pallas_call | solution.py:614
  91.8 155.8 %conditional.1 = (bf16[2048,512]{1,0:T(8,128)(2,1)}, bf16[512,768]{1,0:T(8,128)(2,1)}, bf16[4,384,512]{2,1,0:T(8,128)(2,1)}, bf16[4,384,512]{2,1,0:T(8,128)(2,1)}) conditional(s32[]{:T(128)} %convert_element_type.31, () %tuple.16, (f32[512]{0:T(512)S(1)}, f32[512]{0:T(512)S(1)}, f32[512]{0:T(512)S(1)}, s32[1]{0:T(128)}, bf16[2048,1536]{1,0:T(8,128)(2,1)}, ...), branch_computations={%region_1.2_spmd, %region_2.3_spmd} | conditional | flops 403046400 | bytes 44041204 | solution.py:758
  91.8 40.7 %branch_1_fun.7 = (bf16[640,512]{1,0:T(8,128)(2,1)}, bf16[1024,512]{1,0:T(8,128)(2,1)}, bf16[1024,512]{1,0:T(8,128)(2,1)}, bf16[512,512]{1,0:T(8,128)(2,1)}, bf16[512,512]{1,0:T(8,128)(2,1)}) custom-call(s32[1]{0:T(128)} %get-tuple-element.55.core, bf16[2048,1536]{1,0:T(8,128)(2,1)} %get-tuple-element.56.qkv, f32[2048,256]{1,0:T(8,128)} %get-tuple-element.57.probs, ...), custom_call_target="tpu_custom_call" | custom-call | tf_op jit(solution)/shard_map/cond/branch_1_fun/pallas_call | solution.py:660
  133.1 3.1 %collective-permute-done.1 = bf16[512,512]{1,0:T(8,128)(2,1)S(1)} collective-permute-done((bf16[512,512]{1,0:T(8,128)(2,1)}, bf16[512,512]{1,0:T(8,128)(2,1)S(1)}, u32[]{:S(2)}, u32[]{:S(2)}) %collective-permute-start.1) | collective-permute-done | bytes 524320 | tf_op jit(solution)/shard_map/cond/branch_1_fun/ppermute | solution.py:458
  137.3 3.9 %branch_1_fun.8.after = bf16[4,384,512]{2,1,0:T(8,128)(2,1)} custom-call(bf16[4,256,512]{2,1,0:T(8,128)(2,1)} %bitcast.40, bf16[4,256,512]{2,1,0:T(8,128)(2,1)} %bitcast.41, bf16[4,128,512]{2,1,0:T(8,128)(2,1)} %bitcast.43, bf16[4,128,512]{2,1,0:T(8,128)(2,1)} %bitcast.44), custom_call_target="tpu_custom_call" | custom-call | tf_op jit(solution)/shard_map/cond/branch_1_fun/pallas_call | solution.py:475
  141.3 4.3 %all-to-all-start = ((bf16[4,384,512]{2,1,0:T(8,128)(2,1)}), bf16[4,384,512]{2,1,0:T(8,128)(2,1)}, u32[]{:S(2)}, u32[]{:S(2)}) async-start(bf16[4,384,512]{2,1,0:T(8,128)(2,1)} %branch_1_fun.8.after), calls=%async_computation | async-start | bytes 3145728 | tf_op jit(solution)/shard_map/cond/branch_1_fun/all_to_all | solution.py:462
  146.5 9.8 %branch_1_fun.9 = (bf16[2048,512]{1,0:T(8,128)(2,1)}, bf16[16,512]{1,0:T(8,128)(2,1)}) custom-call(f32[2048,512]{1,0:T(8,128)} %get-tuple-element.50.middle, bf16[2048,2048]{1,0:T(8,128)(2,1)} %get-tuple-element.51.act, bf16[2048,512]{1,0:T(8,128)(2,1)S(1)} %get-tuple-element.52.down, f32[1,512]{1,0:T(1,128)S(1)} %bitcast.50, ...), custom_call_target="tpu_custom_call" | custom-call | tf_op jit(solution)/shard_map/cond/branch_1_fun/pallas_call | solution.py:718
  158.2 8.4 %all-to-all-done.refs_0_ = bf16[4,384,512]{2,1,0:T(8,128)(2,1)} async-done(((bf16[4,384,512]{2,1,0:T(8,128)(2,1)}), bf16[4,384,512]{2,1,0:T(8,128)(2,1)}, u32[]{:S(2)}, u32[]{:S(2)}) %all-to-all-start) | async-done | bytes 1572896 | tf_op jit(solution)/shard_map/cond/branch_1_fun/all_to_all | solution.py:462
  166.7 2.4 branch_1_fun.10
  171.9 2.6 all-to-all-start.1
  176.3 2.5 collective-permute-start.5
  179.0 8.5 %collective-permute-done.4.refs_1_ = bf16[96,512]{1,0:T(8,128)(2,1)S(1)} collective-permute-done((bf16[96,512]{1,0:T(8,128)(2,1)S(1)}, bf16[96,512]{1,0:T(8,128)(2,1)S(1)}, u32[]{:S(2)}, u32[]{:S(2)}) %collective-permute-start.4) | collective-permute-done | bytes 98336 | tf_op jit(solution)/shard_map/cond/branch_1_fun/ppermute | solution.py:467
  187.5 11.7 %collective-permute-done.5.refs_2_ = bf16[96,512]{1,0:T(8,128)(2,1)S(1)} collective-permute-done((bf16[96,512]{1,0:T(8,128)(2,1)S(1)}, bf16[96,512]{1,0:T(8,128)(2,1)S(1)}, u32[]{:S(2)}, u32[]{:S(2)}) %collective-permute-start.5) | collective-permute-done | bytes 98336 | tf_op jit(solution)/shard_map/cond/branch_1_fun/ppermute | solution.py:467
  203.1 4.0 %collective-permute-start.8 = (bf16[96,512]{1,0:T(8,128)(2,1)}, bf16[96,512]{1,0:T(8,128)(2,1)S(1)}, u32[]{:S(2)}, u32[]{:S(2)}) collective-permute-start(bf16[96,512]{1,0:T(8,128)(2,1)} %branch_1_fun.12.refs_0_), channel_id=1, source_target_pairs={{0,16},{8,24},{16,0},{24,8},{1,17},{9,25},{17,1},{25,9},{2,18},{10... | collective-permute-start | bytes 294920 | tf_op jit(solution)/shard_map/cond/branch_1_fun/ppermute | solution.py:467
  207.1 2.4 collective-permute-done.9.refs_3_
  209.4 5.9 %collective-permute-done.8.refs_2_ = bf16[96,512]{1,0:T(8,128)(2,1)S(1)} collective-permute-done((bf16[96,512]{1,0:T(8,128)(2,1)}, bf16[96,512]{1,0:T(8,128)(2,1)S(1)}, u32[]{:S(2)}, u32[]{:S(2)}) %collective-permute-start.8) | collective-permute-done | bytes 98336 | tf_op jit(solution)/shard_map/cond/branch_1_fun/ppermute | solution.py:467
  218.5 25.3 %all_to_all.27 = bf16[4,4,96,512]{3,2,1,0:T(8,128)(2,1)} all-to-all(bf16[4,4,96,512]{3,2,1,0:T(8,128)(2,1)} %branch_1_fun.13), channel_id=1, replica_groups=mesh['z'=4,'p'=4,'c'=2] {'p'}, dimensions={0} | all-to-all | bytes 3145728 | tf_op jit(solution)/shard_map/cond/branch_1_fun/all_to_all | solution.py:462
  247.6 4.8 %shard_map.374 = (f32[512,1536]{1,0:T(8,128)}, f32[512,512]{1,0:T(8,128)}, f32[768,512]{1,0:T(8,128)}, f32[512]{0:T(512)}, f32[512]{0:T(512)}, /*index=5*/f32[51...) custom-call(s32[1]{0:T(128)} %bitcast.11.core, ...), custom_call_target="tpu_custom_call" | custom-call | tf_op jit(solution)/shard_map/pallas_call | solution.py:446
  254.3 5.8 %shard_map.375 = (f32[2048,512]{1,0:T(8,128)}, f32[512,2048]{1,0:T(8,128)}) custom-call(bf16[2048,512]{1,0:T(8,128)(2,1)} %get-tuple-element.164.down, bf16[512,2048]{1,0:T(8,128)(2,1)} %get-tuple-element.165.up), custom_call_target="tpu_custom_call" | custom-call | tf_op jit(solution)/shard_map/pallas_call | solution.py:780
  (111 shorter events, 32.0 us)
Async XLA Ops:
  7.2 16.9 %copy-start = (f32[16,49]{1,0:T(8,128)S(1)}, f32[16,49]{1,0:T(8,128)}, u32[]{:S(2)}) copy-start(f32[16,49]{1,0:T(8,128)} %param.36) | copy-start | bytes 9412
  7.2 21.1 %copy-start.21 = (s32[16,1]{1,0:T(8,128)S(1)}, s32[16,1]{1,0:T(8,128)}, u32[]{:S(2)}) copy-start(s32[16,1]{1,0:T(8,128)} %constant.129) | copy-start | bytes 196
  7.2 27.9 %all-to-all-start.3 = ((bf16[32,16,768]{2,1,0:T(8,128)(2,1)}), bf16[32,16,768]{2,1,0:T(8,128)(2,1)S(1)}, u32[]{:S(2)}, u32[]{:S(2)}) async-start(bf16[32,16,768]{2,1,0:T(8,128)(2,1)} %bitcast.42), calls=%async_computation.3 | async-start | bytes 1572864 | tf_op jit(solution)/shard_map/all_to_all | solution.py:462
  14.5 239.8 %all-reduce.4.cloned.1.call-start = ((), (), s32[]{:S(2)}) async-start(), calls=%async_computation.4 | async-start | bytes 8388608 | tf_op jit(solution)/shard_map/psum | solution.py:651
  17.2 11.0 %collective-permute-start.12 = (bf16[32,512]{1,0:T(8,128)(2,1)S(1)}, bf16[32,512]{1,0:T(8,128)(2,1)S(1)}, u32[]{:S(2)}, u32[]{:S(2)}) collective-permute-start(bf16[32,512]{1,0:T(8,128)(2,1)S(1)} %pad_maximum_fusion), channel_id=1, source_target_pairs={{0,31},{1,0},{2,1},{3,2},{4,3},{5,4},{6,5},{7,6},{8,7},{9,8},{10,9... | collective-permute-start | bytes 98312 | tf_op jit(solution)/shard_map/ppermute | solution.py:558
  35.4 8.1 %collective-permute-start.11 = (bf16[16,768]{1,0:T(8,128)(2,1)S(1)}, bf16[16,768]{1,0:T(8,128)(2,1)S(1)}, u32[]{:S(2)}, u32[]{:S(2)}) collective-permute-start(bf16[16,768]{1,0:T(8,128)(2,1)S(1)} %convolution_convert_fusion.1), channel_id=1, source_target_pairs={{0,31},{1,0},{2,1},{3,2},{4,3},{5,4},{6,5},{7,6},{8,7},{9,8},{10,9... | collective-permute-start | bytes 73736 | tf_op jit(solution)/shard_map/ppermute | solution.py:603
  43.5 47.6 %copy-start.6 = (bf16[128,768]{1,0:T(8,128)(2,1)}, bf16[128,768]{1,0:T(8,128)(2,1)S(1)}, u32[]{:S(2)}) copy-start(bf16[128,768]{1,0:T(8,128)(2,1)S(1)} %pad.4.rim) | copy-start | bytes 589828
  132.6 3.6 %collective-permute-start = (bf16[1024,512]{1,0:T(8,128)(2,1)}, bf16[1024,512]{1,0:T(8,128)(2,1)S(1)}, u32[]{:S(2)}, u32[]{:S(2)}) collective-permute-start(bf16[1024,512]{1,0:T(8,128)(2,1)} %get-tuple-element.73), channel_id=1, source_target_pairs={{0,1},{1,0},{2,3},{3,2},{4,5},{5,4},{6,7},{7,6},{8,9},{9,8},{10,11... | collective-permute-start | bytes 3145736 | tf_op jit(solution)/shard_map/cond/branch_1_fun/ppermute | solution.py:458
  132.6 3.6 %collective-permute-start.1 = (bf16[512,512]{1,0:T(8,128)(2,1)}, bf16[512,512]{1,0:T(8,128)(2,1)S(1)}, u32[]{:S(2)}, u32[]{:S(2)}) collective-permute-start(bf16[512,512]{1,0:T(8,128)(2,1)} %get-tuple-element.75), channel_id=1, source_target_pairs={{0,1},{1,0},{2,3},{3,2},{4,5},{5,4},{6,7},{7,6},{8,9},{9,8},{10,11... | collective-permute-start | bytes 1572872 | tf_op jit(solution)/shard_map/cond/branch_1_fun/ppermute | solution.py:458
  141.3 25.4 %all-to-all-start = ((bf16[4,384,512]{2,1,0:T(8,128)(2,1)}), bf16[4,384,512]{2,1,0:T(8,128)(2,1)}, u32[]{:S(2)}, u32[]{:S(2)}) async-start(bf16[4,384,512]{2,1,0:T(8,128)(2,1)} %branch_1_fun.8.after), calls=%async_computation | async-start | bytes 3145728 | tf_op jit(solution)/shard_map/cond/branch_1_fun/all_to_all | solution.py:462
  146.3 22.8 %collective-permute-start.3 = (bf16[16,512]{1,0:T(8,128)(2,1)S(1)}, bf16[16,512]{1,0:T(8,128)(2,1)S(1)}, u32[]{:S(2)}, u32[]{:S(2)}) collective-permute-start(bf16[16,512]{1,0:T(8,128)(2,1)S(1)} %slice.14), channel_id=1, source_target_pairs={{0,1},{1,2},{2,3},{3,4},{4,5},{5,6},{6,7},{7,8},{8,9},{9,10},{10,1... | collective-permute-start | bytes 49160 | tf_op jit(solution)/shard_map/cond/branch_1_fun/ppermute | solution.py:715
  156.3 12.8 %collective-permute-start.2 = (bf16[16,512]{1,0:T(8,128)(2,1)}, bf16[16,512]{1,0:T(8,128)(2,1)S(1)}, u32[]{:S(2)}, u32[]{:S(2)}) collective-permute-start(bf16[16,512]{1,0:T(8,128)(2,1)} %get-tuple-element.77.refs_1_), channel_id=1, source_target_pairs={{0,1},{1,2},{2,3},{3,4},{4,5},{5,6},{6,7},{7,8},{8,9},{9,10},{10,1... | collective-permute-start | bytes 49160 | tf_op jit(solution)/shard_map/cond/branch_1_fun/ppermute | solution.py:733
  171.9 43.4 %all-to-all-start.1 = ((bf16[32,16,512]{2,1,0:T(8,128)(2,1)}), bf16[32,16,512]{2,1,0:T(8,128)(2,1)S(1)}, u32[]{:S(2)}, u32[]{:S(2)}) async-start(bf16[32,16,512]{2,1,0:T(8,128)(2,1)} %bitcast.39), calls=%async_computation.1 | async-start | bytes 1048576 | tf_op jit(solution)/shard_map/cond/branch_1_fun/all_to_all | solution.py:462
  174.6 12.9 %collective-permute-start.4 = (bf16[96,512]{1,0:T(8,128)(2,1)S(1)}, bf16[96,512]{1,0:T(8,128)(2,1)S(1)}, u32[]{:S(2)}, u32[]{:S(2)}) collective-permute-start(bf16[96,512]{1,0:T(8,128)(2,1)S(1)} %copy-done.27), channel_id=1, source_target_pairs={{0,8},{8,0},{16,24},{24,16},{1,9},{9,1},{17,25},{25,17},{2,10},{10... | collective-permute-start | bytes 294920 | tf_op jit(solution)/shard_map/cond/branch_1_fun/ppermute | solution.py:467
  176.3 22.9 %collective-permute-start.5 = (bf16[96,512]{1,0:T(8,128)(2,1)S(1)}, bf16[96,512]{1,0:T(8,128)(2,1)S(1)}, u32[]{:S(2)}, u32[]{:S(2)}) collective-permute-start(bf16[96,512]{1,0:T(8,128)(2,1)S(1)} %copy-done.26), channel_id=1, source_target_pairs={{0,16},{8,24},{16,0},{24,8},{1,17},{9,25},{17,1},{25,9},{2,18},{10... | collective-permute-start | bytes 294920 | tf_op jit(solution)/shard_map/cond/branch_1_fun/ppermute | solution.py:467
  178.8 20.4 %collective-permute-start.6 = (bf16[96,512]{1,0:T(8,128)(2,1)S(1)}, bf16[96,512]{1,0:T(8,128)(2,1)S(1)}, u32[]{:S(2)}, u32[]{:S(2)}) collective-permute-start(bf16[96,512]{1,0:T(8,128)(2,1)S(1)} %copy-done.25), channel_id=1, source_target_pairs={{0,24},{8,16},{16,8},{24,0},{1,25},{9,17},{17,9},{25,1},{2,26},{10... | collective-permute-start | bytes 294920 | tf_op jit(solution)/shard_map/cond/branch_1_fun/ppermute | solution.py:467
  187.5 11.8 %copy-start.15 = (bf16[96,512]{1,0:T(8,128)(2,1)}, bf16[96,512]{1,0:T(8,128)(2,1)S(1)}, u32[]{:S(2)}) copy-start(bf16[96,512]{1,0:T(8,128)(2,1)S(1)} %collective-permute-done.4.refs_1_) | copy-start | bytes 294916 | tf_op jit(solution)/shard_map/cond
  202.2 7.2 %collective-permute-start.9 = (bf16[96,512]{1,0:T(8,128)(2,1)}, bf16[96,512]{1,0:T(8,128)(2,1)S(1)}, u32[]{:S(2)}, u32[]{:S(2)}) collective-permute-start(bf16[96,512]{1,0:T(8,128)(2,1)} %branch_1_fun.12.refs_0_), channel_id=1, source_target_pairs={{0,24},{8,16},{16,8},{24,0},{1,25},{9,17},{17,9},{25,1},{2,26},{10... | collective-permute-start | bytes 294920 | tf_op jit(solution)/shard_map/cond/branch_1_fun/ppermute | solution.py:467
  203.1 12.3 %collective-permute-start.8 = (bf16[96,512]{1,0:T(8,128)(2,1)}, bf16[96,512]{1,0:T(8,128)(2,1)S(1)}, u32[]{:S(2)}, u32[]{:S(2)}) collective-permute-start(bf16[96,512]{1,0:T(8,128)(2,1)} %branch_1_fun.12.refs_0_), channel_id=1, source_target_pairs={{0,16},{8,24},{16,0},{24,8},{1,17},{9,25},{17,1},{25,9},{2,18},{10... | collective-permute-start | bytes 294920 | tf_op jit(solution)/shard_map/cond/branch_1_fun/ppermute | solution.py:467
  207.1 8.3 %collective-permute-start.7 = (bf16[96,512]{1,0:T(8,128)(2,1)}, bf16[96,512]{1,0:T(8,128)(2,1)S(1)}, u32[]{:S(2)}, u32[]{:S(2)}) collective-permute-start(bf16[96,512]{1,0:T(8,128)(2,1)} %branch_1_fun.12.refs_0_), channel_id=1, source_target_pairs={{0,8},{8,0},{16,24},{24,16},{1,9},{9,1},{17,25},{25,17},{2,10},{10... | collective-permute-start | bytes 294920 | tf_op jit(solution)/shard_map/cond/branch_1_fun/ppermute | solution.py:467
  218.5 25.4 %copy-start.19 = (bf16[16,512]{1,0:T(8,128)(2,1)S(1)}, bf16[16,512]{1,0:T(8,128)(2,1)}, u32[]{:S(2)}) copy-start(bf16[16,512]{1,0:T(8,128)(2,1)} %copy-done.18) | copy-start | bytes 49156 | tf_op jit(solution)/shard_map/cond
  218.5 26.0 %copy-start.5 = (bf16[32,16,512]{2,1,0:T(8,128)(2,1)S(1)}, bf16[32,16,512]{2,1,0:T(8,128)(2,1)}, u32[]{:S(2)}) copy-start(bf16[32,16,512]{2,1,0:T(8,128)(2,1)} %copy-done.4) | copy-start | bytes 1572868 | tf_op jit(solution)/shard_map/cond
  218.5 26.0 %copy-start.8 = (bf16[768,512]{1,0:T(8,128)(2,1)S(1)}, bf16[768,512]{1,0:T(8,128)(2,1)}, u32[]{:S(2)}) copy-start(bf16[768,512]{1,0:T(8,128)(2,1)} %get-tuple-element.82) | copy-start | bytes 2359300 | tf_op jit(solution)/shard_map/cond
  243.9 3.8 %collective-permute-start.10 = (bf16[4,384,512]{2,1,0:T(8,128)(2,1)}, bf16[4,384,512]{2,1,0:T(8,128)(2,1)}, u32[]{:S(2)}, u32[]{:S(2)}) collective-permute-start(bf16[4,384,512]{2,1,0:T(8,128)(2,1)} %bitcast.10), channel_id=1, source_target_pairs={{0,1},{1,0},{2,3},{3,2},{4,5},{5,4},{6,7},{7,6},{8,9},{9,8},{10,11... | collective-permute-start | bytes 4718600 | tf_op jit(solution)/shard_map/cond/branch_1_fun/ppermute | solution.py:458
  (21 other events, 89.2 us)
Sparse Core Ops, SparseCore 0:
  91.3 150.3 all-reduce.3

commit v5 on v4

--- a/solution.py
+++ b/solution.py
@@ -24,7 +24,7 @@
 SCALE = HD ** (-0.5)
 PRECISE = lax.Precision.HIGHEST
 VMEM_LIMIT = 60 * 2**20
-FEED_PIECE = 2048
+FEED_PIECE = 1024
 bf16 = jnp.bfloat16
 f32 = jnp.float32
 AXES = ("z", "p", "c")
@@ -375,12 +375,10 @@
             out[cell, at] = share
 
 
-def widen_kernel(down, up, down_o, up_o):
+def unpack_kernel(split, core, down, up, mine, other, down_o, up_o, qkv_o, out_o, embed_o, *small_o):
+    step = pl.program_id(0)
     down_o[...] = down[...].astype(f32)
     up_o[...] = up[...].astype(f32)
-
-
-def rest_unpack_kernel(split, core, mine, other, qkv_o, out_o, embed_o, *small_o):
     width = out_o.shape[1]
     e_in = embed_o.shape[0]
 
@@ -405,11 +403,11 @@
             up_bias_o[i * width : (i + 1) * width] = rows[left + 6 + i]
         rel_o[...] = rows[left + 16 : left + 16 + SPOTS, 0 : HEADS * SPOTS]
 
-    @pl.when(core[0] == 0)
+    @pl.when((step == 0) & (core[0] == 0))
     def _():
         give(mine, other)
 
-    @pl.when(core[0] == 1)
+    @pl.when((step == 0) & (core[0] == 1))
     def _():
         give(other, mine)
 
@@ -758,33 +756,31 @@
     out, grad_visible, mine, other = lax.cond(device_rank < device_count, rest, nothing, operands)
 
     vector = shape((width,), f32)
+    unpacked = [
+        shape((width, 3 * width), f32),
+        shape((width, width), f32),
+        shape((e_in, width), f32),
+        *[vector] * 6,
+        shape((hidden,), f32),
+        shape((SPOTS, HEADS * SPOTS), f32),
+    ]
+    turns = 4
+    wide = [tile(hidden // turns, width), tile(width // turns, hidden)]
     (
-        grad_qkv_weight, grad_out_weight, grad_embed_weight, grad_norm2_gain, grad_out_bias,
-        grad_down_bias, grad_norm1_gain, grad_mask_token, grad_embed_bias, grad_up_bias, rel_sums,
-    ) = at_once(
-        partial(rest_unpack_kernel, 2 * width // cells),
-        (core, mine, other),
-        [
-            shape((width, 3 * width), f32),
-            shape((width, width), f32),
-            shape((e_in, width), f32),
-            *[vector] * 6,
-            shape((hidden,), f32),
-            shape((SPOTS, HEADS * SPOTS), f32),
-        ],
-        [SMEM, whole(mine.shape), whole(other.shape)],
-    )
+        grad_down_weight, grad_up_weight, grad_qkv_weight, grad_out_weight, grad_embed_weight,
+        grad_norm2_gain, grad_out_bias, grad_down_bias, grad_norm1_gain, grad_mask_token,
+        grad_embed_bias, grad_up_bias, rel_sums,
+    ) = pl.pallas_call(
+        partial(unpack_kernel, 2 * width // cells),
+        grid=(turns,),
+        in_specs=[SMEM, *wide, held(mine.shape), held(other.shape)],
+        out_specs=wide + [whole(o.shape) for o in unpacked],
+        out_shape=[shape((hidden, width), f32), shape((width, hidden), f32), *unpacked],
+        compiler_params=params(),
+    )(core, down_sum, up_sum, mine, other)
     grad_rel = jnp.einsum(
         "jhi,ijr->hr", rel_sums.reshape(SPOTS, HEADS, SPOTS), rel_hot, precision=PRECISE
     )
-    grad_down_weight, grad_up_weight = pl.pallas_call(
-        widen_kernel,
-        grid=(4,),
-        in_specs=[tile(hidden // 4, width), tile(width // 4, hidden)],
-        out_specs=[tile(hidden // 4, width), tile(width // 4, hidden)],
-        out_shape=[shape((hidden, width), f32), shape((width, hidden), f32)],
-        compiler_params=params(),
-    )(down_sum, up_sum)
     return (
         out,
         grad_visible,

time: 268 us -> 266 us (level)
    pallas_call x6 -> x5, Pallas kernels: 18 us -> 13.1 us  [at_once(): pl.pallas_call(kernel, grid=(1,), in_specs=specs, out_specs=out_specs, ou...]
    pallas_call x1, Pallas kernels: 5.82 us -> 9.2 us  [per_device(): pl.pallas_call(partial(unpack_kernel, 2 * width // cells), grid=(turns,),...]
  transfers between devices with their start and end apart: 17 -> 17, of which waited for: 9 -> 9; matrix products, arithmetic and copies ran while one was open for 5% -> 4% of each run, Pallas kernels for 27% -> 25%
where the time goes in v5:
time: 266 us; the launch traced here: 265 us
  Pallas kernels  124 us (47%)
  waiting for transfers between devices  49.2 us (18%)
  starting transfers between devices  34.2 us (13%)
  blocking collectives  26 us (10%)
  between operations  14.2 us (5%)
  local copies, waits for them, and re-layouts  11.4 us (4%)
  matrix products  3.88 us (1%)
    pallas_call x1, Pallas kernels, per_device(): pl.pallas_call(first_kernel, grid=grid, in_specs=specs, out_specs=[tile(t...  47.4 us
    pallas_call x1, Pallas kernels, rest(): pl.pallas_call(second_kernel, grid=grid, in_specs=[SMEM, tile(tm, 3 * wid...  40.7 us
    ppermute x6, waiting for transfers between devices, across(): lax.ppermute(x[b], axis, [(i, i ^ b) for i in range(size)])  27.9 us
    all_to_all x1, blocking collectives, exchange(): return lax.all_to_all(x, axis, 0, 0, tiled=True)  26 us
    all_to_all x3, waiting for transfers between devices, exchange(): return lax.all_to_all(x, axis, 0, 0, tiled=True)  15.2 us
    all_to_all x3, starting transfers between devices, exchange(): return lax.all_to_all(x, axis, 0, 0, tiled=True)  14.2 us
    pallas_call x5, Pallas kernels, at_once(): pl.pallas_call(kernel, grid=(1,), in_specs=specs, out_specs=out_specs, ou...  13.1 us
    pallas_call x1, Pallas kernels, rest(): pl.pallas_call(out_kernel, grid=grid, in_specs=[tile(tm, width), tile(tm,...  9.81 us
  transfers between devices with their start and end apart: 17, of which 9 were waited for; matrix products, arithmetic and copies ran while one was open for 4% of the time, Pallas kernels for 25%

profile of v5, /device:TPU:0, one launch (start us, length us, event | category | flops | bytes accessed | tf_op | source)
XLA Modules:
  0.0 265.4 jit_solution(12615018892121293613)
XLA Ops:
  7.2 7.3 %all-to-all-start.3 = ((bf16[32,16,768]{2,1,0:T(8,128)(2,1)}), bf16[32,16,768]{2,1,0:T(8,128)(2,1)S(1)}, u32[]{:S(2)}, u32[]{:S(2)}) async-start(bf16[32,16,768]{2,1,0:T(8,128)(2,1)} %bitcast.42), calls=%async_computation.3 | async-start | bytes 1572864 | tf_op jit(solution)/shard_map/all_to_all | solution.py:460
  17.2 5.2 %collective-permute-start.12 = (bf16[32,512]{1,0:T(8,128)(2,1)S(1)}, bf16[32,512]{1,0:T(8,128)(2,1)S(1)}, u32[]{:S(2)}, u32[]{:S(2)}) collective-permute-start(bf16[32,512]{1,0:T(8,128)(2,1)S(1)} %pad_maximum_fusion), channel_id=1, source_target_pairs={{0,31},{1,0},{2,1},{3,2},{4,3},{5,4},{6,5},{7,6},{8,7},{9,8},{10,9... | collective-permute-start | bytes 98312 | tf_op jit(solution)/shard_map/ppermute | solution.py:556
  28.4 6.8 %all-to-all-done.3 = bf16[32,16,768]{2,1,0:T(8,128)(2,1)S(1)} async-done(((bf16[32,16,768]{2,1,0:T(8,128)(2,1)}), bf16[32,16,768]{2,1,0:T(8,128)(2,1)S(1)}, u32[]{:S(2)}, u32[]{:S(2)}) %all-to-all-start.3) | async-done | bytes 786464 | tf_op jit(solution)/shard_map/all_to_all | solution.py:460
  35.4 2.9 %collective-permute-start.11 = (bf16[16,768]{1,0:T(8,128)(2,1)S(1)}, bf16[16,768]{1,0:T(8,128)(2,1)S(1)}, u32[]{:S(2)}, u32[]{:S(2)}) collective-permute-start(bf16[16,768]{1,0:T(8,128)(2,1)S(1)} %convolution_convert_fusion.1), channel_id=1, source_target_pairs={{0,31},{1,0},{2,1},{3,2},{4,3},{5,4},{6,5},{7,6},{8,7},{9,8},{10,9... | collective-permute-start | bytes 73736 | tf_op jit(solution)/shard_map/ppermute | solution.py:601
  39.0 4.5 %shard_map.372 = (bf16[2048,512]{1,0:T(8,128)(2,1)}, f32[512,512]{1,0:T(8,128)}) custom-call(bf16[2048,512]{1,0:T(8,128)(2,1)} %cotangent.1, bf16[16,512]{1,0:T(8,128)(2,1)} %slice.30.next_cot, f32[512,512]{1,0:T(8,128)} %pos_embed.1, f32[256,256]{1,0:T(8,128)} %constant.122.clone.order), custom_call_target="tpu_custom_call" | custom-call | tf_op jit(solution)/shard_map/pallas_call | solution.py:444
  43.6 47.4 %shard_map.373 = (f32[2048,512]{1,0:T(8,128)}, bf16[2048,1536]{1,0:T(8,128)(2,1)}, f32[2048,256]{1,0:T(8,128)}, bf16[2048,512]{1,0:T(8,128)(2,1)}, f32[2048,512]...) custom-call(f32[128]{0:T(128)} %reshape.130.cut, ...), custom_call_target="tpu_custom_call" | custom-call | tf_op jit(solution)/shard_map/pallas_call | solution.py:612
  91.7 155.8 %conditional.1 = (bf16[2048,512]{1,0:T(8,128)(2,1)}, bf16[512,768]{1,0:T(8,128)(2,1)}, bf16[4,384,512]{2,1,0:T(8,128)(2,1)}, bf16[4,384,512]{2,1,0:T(8,128)(2,1)}) conditional(s32[]{:T(128)} %convert_element_type.31, () %tuple.16, (f32[512]{0:T(512)S(1)}, f32[512]{0:T(512)S(1)}, f32[512]{0:T(512)S(1)}, s32[1]{0:T(128)}, bf16[2048,1536]{1,0:T(8,128)(2,1)}, ...), branch_computations={%region_1.2_spmd, %region_2.3_spmd} | conditional | flops 403046400 | bytes 44041204 | solution.py:756
  91.7 40.7 %branch_1_fun.7 = (bf16[640,512]{1,0:T(8,128)(2,1)}, bf16[1024,512]{1,0:T(8,128)(2,1)}, bf16[1024,512]{1,0:T(8,128)(2,1)}, bf16[512,512]{1,0:T(8,128)(2,1)}, bf16[512,512]{1,0:T(8,128)(2,1)}) custom-call(s32[1]{0:T(128)} %get-tuple-element.55.core, bf16[2048,1536]{1,0:T(8,128)(2,1)} %get-tuple-element.56.qkv, f32[2048,256]{1,0:T(8,128)} %get-tuple-element.57.probs, ...), custom_call_target="tpu_custom_call" | custom-call | tf_op jit(solution)/shard_map/cond/branch_1_fun/pallas_call | solution.py:658
  132.9 3.1 %collective-permute-done.1 = bf16[512,512]{1,0:T(8,128)(2,1)S(1)} collective-permute-done((bf16[512,512]{1,0:T(8,128)(2,1)}, bf16[512,512]{1,0:T(8,128)(2,1)S(1)}, u32[]{:S(2)}, u32[]{:S(2)}) %collective-permute-start.1) | collective-permute-done | bytes 524320 | tf_op jit(solution)/shard_map/cond/branch_1_fun/ppermute | solution.py:456
  137.2 4.0 %branch_1_fun.8.after = bf16[4,384,512]{2,1,0:T(8,128)(2,1)} custom-call(bf16[4,256,512]{2,1,0:T(8,128)(2,1)} %bitcast.40, bf16[4,256,512]{2,1,0:T(8,128)(2,1)} %bitcast.41, bf16[4,128,512]{2,1,0:T(8,128)(2,1)} %bitcast.43, bf16[4,128,512]{2,1,0:T(8,128)(2,1)} %bitcast.44), custom_call_target="tpu_custom_call" | custom-call | tf_op jit(solution)/shard_map/cond/branch_1_fun/pallas_call | solution.py:473
  141.1 4.3 %all-to-all-start = ((bf16[4,384,512]{2,1,0:T(8,128)(2,1)}), bf16[4,384,512]{2,1,0:T(8,128)(2,1)}, u32[]{:S(2)}, u32[]{:S(2)}) async-start(bf16[4,384,512]{2,1,0:T(8,128)(2,1)} %branch_1_fun.8.after), calls=%async_computation | async-start | bytes 3145728 | tf_op jit(solution)/shard_map/cond/branch_1_fun/all_to_all | solution.py:460
  146.3 9.8 %branch_1_fun.9 = (bf16[2048,512]{1,0:T(8,128)(2,1)}, bf16[16,512]{1,0:T(8,128)(2,1)}) custom-call(f32[2048,512]{1,0:T(8,128)} %get-tuple-element.50.middle, bf16[2048,2048]{1,0:T(8,128)(2,1)} %get-tuple-element.51.act, bf16[2048,512]{1,0:T(8,128)(2,1)S(1)} %get-tuple-element.52.down, f32[1,512]{1,0:T(1,128)S(1)} %bitcast.50, ...), custom_call_target="tpu_custom_call" | custom-call | tf_op jit(solution)/shard_map/cond/branch_1_fun/pallas_call | solution.py:716
  158.1 8.5 %all-to-all-done.refs_0_ = bf16[4,384,512]{2,1,0:T(8,128)(2,1)} async-done(((bf16[4,384,512]{2,1,0:T(8,128)(2,1)}), bf16[4,384,512]{2,1,0:T(8,128)(2,1)}, u32[]{:S(2)}, u32[]{:S(2)}) %all-to-all-start) | async-done | bytes 1572896 | tf_op jit(solution)/shard_map/cond/branch_1_fun/all_to_all | solution.py:460
  166.6 2.4 branch_1_fun.10
  171.8 2.6 all-to-all-start.1
  176.2 2.5 collective-permute-start.5
  178.9 8.7 %collective-permute-done.4.refs_1_ = bf16[96,512]{1,0:T(8,128)(2,1)S(1)} collective-permute-done((bf16[96,512]{1,0:T(8,128)(2,1)S(1)}, bf16[96,512]{1,0:T(8,128)(2,1)S(1)}, u32[]{:S(2)}, u32[]{:S(2)}) %collective-permute-start.4) | collective-permute-done | bytes 98336 | tf_op jit(solution)/shard_map/cond/branch_1_fun/ppermute | solution.py:465
  187.6 11.5 %collective-permute-done.5.refs_2_ = bf16[96,512]{1,0:T(8,128)(2,1)S(1)} collective-permute-done((bf16[96,512]{1,0:T(8,128)(2,1)S(1)}, bf16[96,512]{1,0:T(8,128)(2,1)S(1)}, u32[]{:S(2)}, u32[]{:S(2)}) %collective-permute-start.5) | collective-permute-done | bytes 98336 | tf_op jit(solution)/shard_map/cond/branch_1_fun/ppermute | solution.py:465
  202.9 3.9 %collective-permute-start.8 = (bf16[96,512]{1,0:T(8,128)(2,1)}, bf16[96,512]{1,0:T(8,128)(2,1)S(1)}, u32[]{:S(2)}, u32[]{:S(2)}) collective-permute-start(bf16[96,512]{1,0:T(8,128)(2,1)} %branch_1_fun.12.refs_0_), channel_id=1, source_target_pairs={{0,16},{8,24},{16,0},{24,8},{1,17},{9,25},{17,1},{25,9},{2,18},{10... | collective-permute-start | bytes 294920 | tf_op jit(solution)/shard_map/cond/branch_1_fun/ppermute | solution.py:465
  206.8 2.7 %collective-permute-done.9.refs_3_ = bf16[96,512]{1,0:T(8,128)(2,1)S(1)} collective-permute-done((bf16[96,512]{1,0:T(8,128)(2,1)}, bf16[96,512]{1,0:T(8,128)(2,1)S(1)}, u32[]{:S(2)}, u32[]{:S(2)}) %collective-permute-start.9) | collective-permute-done | bytes 98336 | tf_op jit(solution)/shard_map/cond/branch_1_fun/ppermute | solution.py:465
  209.6 5.0 %collective-permute-done.8.refs_2_ = bf16[96,512]{1,0:T(8,128)(2,1)S(1)} collective-permute-done((bf16[96,512]{1,0:T(8,128)(2,1)}, bf16[96,512]{1,0:T(8,128)(2,1)S(1)}, u32[]{:S(2)}, u32[]{:S(2)}) %collective-permute-start.8) | collective-permute-done | bytes 98336 | tf_op jit(solution)/shard_map/cond/branch_1_fun/ppermute | solution.py:465
  215.4 2.3 branch_1_fun.13
  217.7 26.0 %all_to_all.27 = bf16[4,4,96,512]{3,2,1,0:T(8,128)(2,1)} all-to-all(bf16[4,4,96,512]{3,2,1,0:T(8,128)(2,1)} %branch_1_fun.13), channel_id=1, replica_groups=mesh['z'=4,'p'=4,'c'=2] {'p'}, dimensions={0} | all-to-all | bytes 3145728 | tf_op jit(solution)/shard_map/cond/branch_1_fun/all_to_all | solution.py:460
  247.5 9.2 %shard_map.374 = (f32[2048,512]{1,0:T(8,128)}, f32[512,2048]{1,0:T(8,128)}, f32[512,1536]{1,0:T(8,128)}, f32[512,512]{1,0:T(8,128)}, f32[768,512]{1,0:T(8,128)},...) custom-call(s32[1]{0:T(128)} %bitcast.11.core, ...), custom_call_target="tpu_custom_call" | custom-call | tf_op jit(solution)/shard_map/pallas_call | solution.py:773
  (110 shorter events, 29.7 us)
Async XLA Ops:
  7.2 16.9 %copy-start = (f32[16,49]{1,0:T(8,128)S(1)}, f32[16,49]{1,0:T(8,128)}, u32[]{:S(2)}) copy-start(f32[16,49]{1,0:T(8,128)} %param.36) | copy-start | bytes 9412
  7.2 21.1 %copy-start.21 = (s32[16,1]{1,0:T(8,128)S(1)}, s32[16,1]{1,0:T(8,128)}, u32[]{:S(2)}) copy-start(s32[16,1]{1,0:T(8,128)} %constant.129) | copy-start | bytes 196
  7.2 27.9 %all-to-all-start.3 = ((bf16[32,16,768]{2,1,0:T(8,128)(2,1)}), bf16[32,16,768]{2,1,0:T(8,128)(2,1)S(1)}, u32[]{:S(2)}, u32[]{:S(2)}) async-start(bf16[32,16,768]{2,1,0:T(8,128)(2,1)} %bitcast.42), calls=%async_computation.3 | async-start | bytes 1572864 | tf_op jit(solution)/shard_map/all_to_all | solution.py:460
  14.5 233.0 %all-reduce.4.cloned.1.call-start = ((), (), s32[]{:S(2)}) async-start(), calls=%async_computation.4 | async-start | bytes 8388608 | tf_op jit(solution)/shard_map/psum | solution.py:649
  17.2 11.0 %collective-permute-start.12 = (bf16[32,512]{1,0:T(8,128)(2,1)S(1)}, bf16[32,512]{1,0:T(8,128)(2,1)S(1)}, u32[]{:S(2)}, u32[]{:S(2)}) collective-permute-start(bf16[32,512]{1,0:T(8,128)(2,1)S(1)} %pad_maximum_fusion), channel_id=1, source_target_pairs={{0,31},{1,0},{2,1},{3,2},{4,3},{5,4},{6,5},{7,6},{8,7},{9,8},{10,9... | collective-permute-start | bytes 98312 | tf_op jit(solution)/shard_map/ppermute | solution.py:556
  35.4 8.1 %collective-permute-start.11 = (bf16[16,768]{1,0:T(8,128)(2,1)S(1)}, bf16[16,768]{1,0:T(8,128)(2,1)S(1)}, u32[]{:S(2)}, u32[]{:S(2)}) collective-permute-start(bf16[16,768]{1,0:T(8,128)(2,1)S(1)} %convolution_convert_fusion.1), channel_id=1, source_target_pairs={{0,31},{1,0},{2,1},{3,2},{4,3},{5,4},{6,5},{7,6},{8,7},{9,8},{10,9... | collective-permute-start | bytes 73736 | tf_op jit(solution)/shard_map/ppermute | solution.py:601
  43.5 47.5 %copy-start.6 = (bf16[128,768]{1,0:T(8,128)(2,1)}, bf16[128,768]{1,0:T(8,128)(2,1)S(1)}, u32[]{:S(2)}) copy-start(bf16[128,768]{1,0:T(8,128)(2,1)S(1)} %pad.4.rim) | copy-start | bytes 589828
  132.4 3.6 %collective-permute-start = (bf16[1024,512]{1,0:T(8,128)(2,1)}, bf16[1024,512]{1,0:T(8,128)(2,1)S(1)}, u32[]{:S(2)}, u32[]{:S(2)}) collective-permute-start(bf16[1024,512]{1,0:T(8,128)(2,1)} %get-tuple-element.73), channel_id=1, source_target_pairs={{0,1},{1,0},{2,3},{3,2},{4,5},{5,4},{6,7},{7,6},{8,9},{9,8},{10,11... | collective-permute-start | bytes 3145736 | tf_op jit(solution)/shard_map/cond/branch_1_fun/ppermute | solution.py:456
  132.4 3.6 %collective-permute-start.1 = (bf16[512,512]{1,0:T(8,128)(2,1)}, bf16[512,512]{1,0:T(8,128)(2,1)S(1)}, u32[]{:S(2)}, u32[]{:S(2)}) collective-permute-start(bf16[512,512]{1,0:T(8,128)(2,1)} %get-tuple-element.75), channel_id=1, source_target_pairs={{0,1},{1,0},{2,3},{3,2},{4,5},{5,4},{6,7},{7,6},{8,9},{9,8},{10,11... | collective-permute-start | bytes 1572872 | tf_op jit(solution)/shard_map/cond/branch_1_fun/ppermute | solution.py:456
  141.1 25.4 %all-to-all-start = ((bf16[4,384,512]{2,1,0:T(8,128)(2,1)}), bf16[4,384,512]{2,1,0:T(8,128)(2,1)}, u32[]{:S(2)}, u32[]{:S(2)}) async-start(bf16[4,384,512]{2,1,0:T(8,128)(2,1)} %branch_1_fun.8.after), calls=%async_computation | async-start | bytes 3145728 | tf_op jit(solution)/shard_map/cond/branch_1_fun/all_to_all | solution.py:460
  146.2 22.8 %collective-permute-start.3 = (bf16[16,512]{1,0:T(8,128)(2,1)S(1)}, bf16[16,512]{1,0:T(8,128)(2,1)S(1)}, u32[]{:S(2)}, u32[]{:S(2)}) collective-permute-start(bf16[16,512]{1,0:T(8,128)(2,1)S(1)} %slice.14), channel_id=1, source_target_pairs={{0,1},{1,2},{2,3},{3,4},{4,5},{5,6},{6,7},{7,8},{8,9},{9,10},{10,1... | collective-permute-start | bytes 49160 | tf_op jit(solution)/shard_map/cond/branch_1_fun/ppermute | solution.py:713
  156.1 12.9 %collective-permute-start.2 = (bf16[16,512]{1,0:T(8,128)(2,1)}, bf16[16,512]{1,0:T(8,128)(2,1)S(1)}, u32[]{:S(2)}, u32[]{:S(2)}) collective-permute-start(bf16[16,512]{1,0:T(8,128)(2,1)} %get-tuple-element.77.refs_1_), channel_id=1, source_target_pairs={{0,1},{1,2},{2,3},{3,4},{4,5},{5,6},{6,7},{7,8},{8,9},{9,10},{10,1... | collective-permute-start | bytes 49160 | tf_op jit(solution)/shard_map/cond/branch_1_fun/ppermute | solution.py:731
  171.8 42.7 %all-to-all-start.1 = ((bf16[32,16,512]{2,1,0:T(8,128)(2,1)}), bf16[32,16,512]{2,1,0:T(8,128)(2,1)S(1)}, u32[]{:S(2)}, u32[]{:S(2)}) async-start(bf16[32,16,512]{2,1,0:T(8,128)(2,1)} %bitcast.39), calls=%async_computation.1 | async-start | bytes 1048576 | tf_op jit(solution)/shard_map/cond/branch_1_fun/all_to_all | solution.py:460
  174.5 13.1 %collective-permute-start.4 = (bf16[96,512]{1,0:T(8,128)(2,1)S(1)}, bf16[96,512]{1,0:T(8,128)(2,1)S(1)}, u32[]{:S(2)}, u32[]{:S(2)}) collective-permute-start(bf16[96,512]{1,0:T(8,128)(2,1)S(1)} %copy-done.27), channel_id=1, source_target_pairs={{0,8},{8,0},{16,24},{24,16},{1,9},{9,1},{17,25},{25,17},{2,10},{10... | collective-permute-start | bytes 294920 | tf_op jit(solution)/shard_map/cond/branch_1_fun/ppermute | solution.py:465
  176.2 22.9 %collective-permute-start.5 = (bf16[96,512]{1,0:T(8,128)(2,1)S(1)}, bf16[96,512]{1,0:T(8,128)(2,1)S(1)}, u32[]{:S(2)}, u32[]{:S(2)}) collective-permute-start(bf16[96,512]{1,0:T(8,128)(2,1)S(1)} %copy-done.26), channel_id=1, source_target_pairs={{0,16},{8,24},{16,0},{24,8},{1,17},{9,25},{17,1},{25,9},{2,18},{10... | collective-permute-start | bytes 294920 | tf_op jit(solution)/shard_map/cond/branch_1_fun/ppermute | solution.py:465
  178.7 20.4 %collective-permute-start.6 = (bf16[96,512]{1,0:T(8,128)(2,1)S(1)}, bf16[96,512]{1,0:T(8,128)(2,1)S(1)}, u32[]{:S(2)}, u32[]{:S(2)}) collective-permute-start(bf16[96,512]{1,0:T(8,128)(2,1)S(1)} %copy-done.25), channel_id=1, source_target_pairs={{0,24},{8,16},{16,8},{24,0},{1,25},{9,17},{17,9},{25,1},{2,26},{10... | collective-permute-start | bytes 294920 | tf_op jit(solution)/shard_map/cond/branch_1_fun/ppermute | solution.py:465
  187.6 11.5 %copy-start.15 = (bf16[96,512]{1,0:T(8,128)(2,1)}, bf16[96,512]{1,0:T(8,128)(2,1)S(1)}, u32[]{:S(2)}) copy-start(bf16[96,512]{1,0:T(8,128)(2,1)S(1)} %collective-permute-done.4.refs_1_) | copy-start | bytes 294916 | tf_op jit(solution)/shard_map/cond
  202.1 7.5 %collective-permute-start.9 = (bf16[96,512]{1,0:T(8,128)(2,1)}, bf16[96,512]{1,0:T(8,128)(2,1)S(1)}, u32[]{:S(2)}, u32[]{:S(2)}) collective-permute-start(bf16[96,512]{1,0:T(8,128)(2,1)} %branch_1_fun.12.refs_0_), channel_id=1, source_target_pairs={{0,24},{8,16},{16,8},{24,0},{1,25},{9,17},{17,9},{25,1},{2,26},{10... | collective-permute-start | bytes 294920 | tf_op jit(solution)/shard_map/cond/branch_1_fun/ppermute | solution.py:465
  202.9 11.6 %collective-permute-start.8 = (bf16[96,512]{1,0:T(8,128)(2,1)}, bf16[96,512]{1,0:T(8,128)(2,1)S(1)}, u32[]{:S(2)}, u32[]{:S(2)}) collective-permute-start(bf16[96,512]{1,0:T(8,128)(2,1)} %branch_1_fun.12.refs_0_), channel_id=1, source_target_pairs={{0,16},{8,24},{16,0},{24,8},{1,17},{9,25},{17,1},{25,9},{2,18},{10... | collective-permute-start | bytes 294920 | tf_op jit(solution)/shard_map/cond/branch_1_fun/ppermute | solution.py:465
  206.8 7.7 %collective-permute-start.7 = (bf16[96,512]{1,0:T(8,128)(2,1)}, bf16[96,512]{1,0:T(8,128)(2,1)S(1)}, u32[]{:S(2)}, u32[]{:S(2)}) collective-permute-start(bf16[96,512]{1,0:T(8,128)(2,1)} %branch_1_fun.12.refs_0_), channel_id=1, source_target_pairs={{0,8},{8,0},{16,24},{24,16},{1,9},{9,1},{17,25},{25,17},{2,10},{10... | collective-permute-start | bytes 294920 | tf_op jit(solution)/shard_map/cond/branch_1_fun/ppermute | solution.py:465
  217.7 26.0 %copy-start.19 = (bf16[16,512]{1,0:T(8,128)(2,1)S(1)}, bf16[16,512]{1,0:T(8,128)(2,1)}, u32[]{:S(2)}) copy-start(bf16[16,512]{1,0:T(8,128)(2,1)} %copy-done.18) | copy-start | bytes 49156 | tf_op jit(solution)/shard_map/cond
  217.7 26.6 %copy-start.5 = (bf16[32,16,512]{2,1,0:T(8,128)(2,1)S(1)}, bf16[32,16,512]{2,1,0:T(8,128)(2,1)}, u32[]{:S(2)}) copy-start(bf16[32,16,512]{2,1,0:T(8,128)(2,1)} %copy-done.4) | copy-start | bytes 1572868 | tf_op jit(solution)/shard_map/cond
  217.7 26.6 %copy-start.8 = (bf16[768,512]{1,0:T(8,128)(2,1)S(1)}, bf16[768,512]{1,0:T(8,128)(2,1)}, u32[]{:S(2)}) copy-start(bf16[768,512]{1,0:T(8,128)(2,1)} %get-tuple-element.82) | copy-start | bytes 2359300 | tf_op jit(solution)/shard_map/cond
  243.7 3.8 %collective-permute-start.10 = (bf16[4,384,512]{2,1,0:T(8,128)(2,1)}, bf16[4,384,512]{2,1,0:T(8,128)(2,1)}, u32[]{:S(2)}, u32[]{:S(2)}) collective-permute-start(bf16[4,384,512]{2,1,0:T(8,128)(2,1)} %bitcast.10), channel_id=1, source_target_pairs={{0,1},{1,0},{2,3},{3,2},{4,5},{5,4},{6,7},{7,6},{8,9},{9,8},{10,11... | collective-permute-start | bytes 4718600 | tf_op jit(solution)/shard_map/cond/branch_1_fun/ppermute | solution.py:456
  (21 other events, 97.8 us)
Sparse Core Ops, SparseCore 0:
  91.1 150.1 all-reduce.3

commit v6 on v5

--- a/solution.py
+++ b/solution.py
@@ -375,7 +375,7 @@
             out[cell, at] = share
 
 
-def unpack_kernel(split, core, down, up, mine, other, down_o, up_o, qkv_o, out_o, embed_o, *small_o):
+def unpack_kernel(split, core, down, up, mine, other, rel_hot, down_o, up_o, qkv_o, out_o, embed_o, *small_o):
     step = pl.program_id(0)
     down_o[...] = down[...].astype(f32)
     up_o[...] = up[...].astype(f32)
@@ -401,7 +401,15 @@
         up_bias_o, rel_o = small_o[6:]
         for i in range(up_bias_o.shape[0] // width):
             up_bias_o[i * width : (i + 1) * width] = rows[left + 6 + i]
-        rel_o[...] = rows[left + 16 : left + 16 + SPOTS, 0 : HEADS * SPOTS]
+        sums = rows[left + 16 : left + 16 + SPOTS, 0 : HEADS * SPOTS]
+        head = lax.broadcasted_iota(jnp.int32, (HEADS, HEADS * SPOTS), 0)
+        own = head == lax.broadcasted_iota(jnp.int32, (HEADS, HEADS * SPOTS), 1) // SPOTS
+        by_head = jnp.concatenate(
+            [jnp.where(own, sums[j : j + 1], 0.0) for j in range(SPOTS)], axis=1
+        )
+        rel_o[...] = jnp.dot(
+            by_head, rel_hot[...], precision=PRECISE, preferred_element_type=f32
+        )
 
     @pl.when((step == 0) & (core[0] == 0))
     def _():
@@ -762,25 +770,25 @@
         shape((e_in, width), f32),
         *[vector] * 6,
         shape((hidden,), f32),
-        shape((SPOTS, HEADS * SPOTS), f32),
+        shape((HEADS, rels * rels), f32),
     ]
     turns = 4
+    rel_rows = np.repeat(rel_hot.transpose(1, 0, 2)[:, None], HEADS, axis=1).reshape(
+        SPOTS * HEADS * SPOTS, rels * rels
+    )
     wide = [tile(hidden // turns, width), tile(width // turns, hidden)]
     (
         grad_down_weight, grad_up_weight, grad_qkv_weight, grad_out_weight, grad_embed_weight,
         grad_norm2_gain, grad_out_bias, grad_down_bias, grad_norm1_gain, grad_mask_token,
-        grad_embed_bias, grad_up_bias, rel_sums,
+        grad_embed_bias, grad_up_bias, grad_rel,
     ) = pl.pallas_call(
         partial(unpack_kernel, 2 * width // cells),
         grid=(turns,),
-        in_specs=[SMEM, *wide, held(mine.shape), held(other.shape)],
+        in_specs=[SMEM, *wide, held(mine.shape), held(other.shape), held(rel_rows.shape)],
         out_specs=wide + [whole(o.shape) for o in unpacked],
         out_shape=[shape((hidden, width), f32), shape((width, hidden), f32), *unpacked],
         compiler_params=params(),
-    )(core, down_sum, up_sum, mine, other)
-    grad_rel = jnp.einsum(
-        "jhi,ijr->hr", rel_sums.reshape(SPOTS, HEADS, SPOTS), rel_hot, precision=PRECISE
-    )
+    )(core, down_sum, up_sum, mine, other, rel_rows)
     return (
         out,
         grad_visible,

time: 266 us -> 266 us (level)
  no operation moved by 1% of the time
where the time goes in v6:
time: 266 us; the launch traced here: 265 us
  Pallas kernels  126 us (47%)
  waiting for transfers between devices  49.9 us (19%)
  starting transfers between devices  34.4 us (13%)
  blocking collectives  25.2 us (9%)
  between operations  14.2 us (5%)
  local copies, waits for them, and re-layouts  10.6 us (4%)
  matrix products  2.86 us (1%)
    pallas_call x1, Pallas kernels, per_device(): pl.pallas_call(first_kernel, grid=grid, in_specs=specs, out_specs=[tile(t...  47.4 us
    pallas_call x1, Pallas kernels, rest(): pl.pallas_call(second_kernel, grid=grid, in_specs=[SMEM, tile(tm, 3 * wid...  40.7 us
    ppermute x6, waiting for transfers between devices, across(): lax.ppermute(x[b], axis, [(i, i ^ b) for i in range(size)])  28.7 us
    all_to_all x1, blocking collectives, exchange(): return lax.all_to_all(x, axis, 0, 0, tiled=True)  25.2 us
    all_to_all x3, waiting for transfers between devices, exchange(): return lax.all_to_all(x, axis, 0, 0, tiled=True)  15.2 us
    all_to_all x3, starting transfers between devices, exchange(): return lax.all_to_all(x, axis, 0, 0, tiled=True)  14.2 us
    pallas_call x5, Pallas kernels, at_once(): pl.pallas_call(kernel, grid=(1,), in_specs=specs, out_specs=out_specs, ou...  13.1 us
    pallas_call x1, Pallas kernels, per_device(): pl.pallas_call(partial(unpack_kernel, 2 * width // cells), grid=(turns,),...  10.9 us
  transfers between devices with their start and end apart: 17, of which 9 were waited for; matrix products, arithmetic and copies ran while one was open for 4% of the time, Pallas kernels for 25%

profile of v6, /device:TPU:0, one launch (start us, length us, event | category | flops | bytes accessed | tf_op | source)
XLA Modules:
  0.0 265.2 jit_solution(14441654177811804530)
XLA Ops:
  7.2 7.3 %all-to-all-start.3 = ((bf16[32,16,768]{2,1,0:T(8,128)(2,1)}), bf16[32,16,768]{2,1,0:T(8,128)(2,1)S(1)}, u32[]{:S(2)}, u32[]{:S(2)}) async-start(bf16[32,16,768]{2,1,0:T(8,128)(2,1)} %bitcast.38), calls=%async_computation.3 | async-start | bytes 1572864 | tf_op jit(solution)/shard_map/all_to_all | solution.py:468
  17.2 5.2 %collective-permute-start.12 = (bf16[32,512]{1,0:T(8,128)(2,1)S(1)}, bf16[32,512]{1,0:T(8,128)(2,1)S(1)}, u32[]{:S(2)}, u32[]{:S(2)}) collective-permute-start(bf16[32,512]{1,0:T(8,128)(2,1)S(1)} %pad_maximum_fusion), channel_id=1, source_target_pairs={{0,31},{1,0},{2,1},{3,2},{4,3},{5,4},{6,5},{7,6},{8,7},{9,8},{10,9... | collective-permute-start | bytes 98312 | tf_op jit(solution)/shard_map/ppermute | solution.py:564
  28.4 6.8 %all-to-all-done.3 = bf16[32,16,768]{2,1,0:T(8,128)(2,1)S(1)} async-done(((bf16[32,16,768]{2,1,0:T(8,128)(2,1)}), bf16[32,16,768]{2,1,0:T(8,128)(2,1)S(1)}, u32[]{:S(2)}, u32[]{:S(2)}) %all-to-all-start.3) | async-done | bytes 786464 | tf_op jit(solution)/shard_map/all_to_all | solution.py:468
  35.4 2.9 %collective-permute-start.11 = (bf16[16,768]{1,0:T(8,128)(2,1)S(1)}, bf16[16,768]{1,0:T(8,128)(2,1)S(1)}, u32[]{:S(2)}, u32[]{:S(2)}) collective-permute-start(bf16[16,768]{1,0:T(8,128)(2,1)S(1)} %convolution_convert_fusion.1), channel_id=1, source_target_pairs={{0,31},{1,0},{2,1},{3,2},{4,3},{5,4},{6,5},{7,6},{8,7},{9,8},{10,9... | collective-permute-start | bytes 73736 | tf_op jit(solution)/shard_map/ppermute | solution.py:609
  39.0 4.5 %shard_map.372 = (bf16[2048,512]{1,0:T(8,128)(2,1)}, f32[512,512]{1,0:T(8,128)}) custom-call(bf16[2048,512]{1,0:T(8,128)(2,1)} %cotangent.1, bf16[16,512]{1,0:T(8,128)(2,1)} %slice.30.next_cot, f32[512,512]{1,0:T(8,128)} %pos_embed.1, f32[256,256]{1,0:T(8,128)} %constant.124.clone.order), custom_call_target="tpu_custom_call" | custom-call | tf_op jit(solution)/shard_map/pallas_call | solution.py:452
  43.6 47.4 %shard_map.373 = (f32[2048,512]{1,0:T(8,128)}, bf16[2048,1536]{1,0:T(8,128)(2,1)}, f32[2048,256]{1,0:T(8,128)}, bf16[2048,512]{1,0:T(8,128)(2,1)}, f32[2048,512]...) custom-call(f32[128]{0:T(128)} %reshape.127.cut, ...), custom_call_target="tpu_custom_call" | custom-call | tf_op jit(solution)/shard_map/pallas_call | solution.py:620
  91.7 155.8 %conditional.1 = (bf16[2048,512]{1,0:T(8,128)(2,1)}, bf16[512,768]{1,0:T(8,128)(2,1)}, bf16[4,384,512]{2,1,0:T(8,128)(2,1)}, bf16[4,384,512]{2,1,0:T(8,128)(2,1)}) conditional(s32[]{:T(128)} %convert_element_type.31, () %tuple.16, (f32[512]{0:T(512)S(1)}, f32[512]{0:T(512)S(1)}, f32[512]{0:T(512)S(1)}, s32[1]{0:T(128)}, bf16[2048,1536]{1,0:T(8,128)(2,1)}, ...), branch_computations={%region_1.2_spmd, %region_2.3_spmd} | conditional | flops 403046400 | bytes 44041204 | solution.py:764
  91.7 40.7 %branch_1_fun.7 = (bf16[640,512]{1,0:T(8,128)(2,1)}, bf16[1024,512]{1,0:T(8,128)(2,1)}, bf16[1024,512]{1,0:T(8,128)(2,1)}, bf16[512,512]{1,0:T(8,128)(2,1)}, bf16[512,512]{1,0:T(8,128)(2,1)}) custom-call(s32[1]{0:T(128)} %get-tuple-element.55.core, bf16[2048,1536]{1,0:T(8,128)(2,1)} %get-tuple-element.56.qkv, f32[2048,256]{1,0:T(8,128)} %get-tuple-element.57.probs, ...), custom_call_target="tpu_custom_call" | custom-call | tf_op jit(solution)/shard_map/cond/branch_1_fun/pallas_call | solution.py:666
  132.9 3.1 %collective-permute-done.1 = bf16[512,512]{1,0:T(8,128)(2,1)S(1)} collective-permute-done((bf16[512,512]{1,0:T(8,128)(2,1)}, bf16[512,512]{1,0:T(8,128)(2,1)S(1)}, u32[]{:S(2)}, u32[]{:S(2)}) %collective-permute-start.1) | collective-permute-done | bytes 524320 | tf_op jit(solution)/shard_map/cond/branch_1_fun/ppermute | solution.py:464
  137.2 4.0 %branch_1_fun.8.after = bf16[4,384,512]{2,1,0:T(8,128)(2,1)} custom-call(bf16[4,256,512]{2,1,0:T(8,128)(2,1)} %bitcast.36, bf16[4,256,512]{2,1,0:T(8,128)(2,1)} %bitcast.37, bf16[4,128,512]{2,1,0:T(8,128)(2,1)} %bitcast.39, bf16[4,128,512]{2,1,0:T(8,128)(2,1)} %bitcast.40), custom_call_target="tpu_custom_call" | custom-call | tf_op jit(solution)/shard_map/cond/branch_1_fun/pallas_call | solution.py:481
  141.1 4.3 %all-to-all-start = ((bf16[4,384,512]{2,1,0:T(8,128)(2,1)}), bf16[4,384,512]{2,1,0:T(8,128)(2,1)}, u32[]{:S(2)}, u32[]{:S(2)}) async-start(bf16[4,384,512]{2,1,0:T(8,128)(2,1)} %branch_1_fun.8.after), calls=%async_computation | async-start | bytes 3145728 | tf_op jit(solution)/shard_map/cond/branch_1_fun/all_to_all | solution.py:468
  146.3 9.8 %branch_1_fun.9 = (bf16[2048,512]{1,0:T(8,128)(2,1)}, bf16[16,512]{1,0:T(8,128)(2,1)}) custom-call(f32[2048,512]{1,0:T(8,128)} %get-tuple-element.50.middle, bf16[2048,2048]{1,0:T(8,128)(2,1)} %get-tuple-element.51.act, bf16[2048,512]{1,0:T(8,128)(2,1)S(1)} %get-tuple-element.52.down, f32[1,512]{1,0:T(1,128)S(1)} %bitcast.46, ...), custom_call_target="tpu_custom_call" | custom-call | tf_op jit(solution)/shard_map/cond/branch_1_fun/pallas_call | solution.py:724
  158.1 8.5 %all-to-all-done.refs_0_ = bf16[4,384,512]{2,1,0:T(8,128)(2,1)} async-done(((bf16[4,384,512]{2,1,0:T(8,128)(2,1)}), bf16[4,384,512]{2,1,0:T(8,128)(2,1)}, u32[]{:S(2)}, u32[]{:S(2)}) %all-to-all-start) | async-done | bytes 1572896 | tf_op jit(solution)/shard_map/cond/branch_1_fun/all_to_all | solution.py:468
  166.5 2.4 branch_1_fun.10
  171.8 2.6 all-to-all-start.1
  176.2 2.5 collective-permute-start.5
  178.9 8.6 %collective-permute-done.4.refs_1_ = bf16[96,512]{1,0:T(8,128)(2,1)S(1)} collective-permute-done((bf16[96,512]{1,0:T(8,128)(2,1)S(1)}, bf16[96,512]{1,0:T(8,128)(2,1)S(1)}, u32[]{:S(2)}, u32[]{:S(2)}) %collective-permute-start.4) | collective-permute-done | bytes 98336 | tf_op jit(solution)/shard_map/cond/branch_1_fun/ppermute | solution.py:473
  187.5 11.6 %collective-permute-done.5.refs_2_ = bf16[96,512]{1,0:T(8,128)(2,1)S(1)} collective-permute-done((bf16[96,512]{1,0:T(8,128)(2,1)S(1)}, bf16[96,512]{1,0:T(8,128)(2,1)S(1)}, u32[]{:S(2)}, u32[]{:S(2)}) %collective-permute-start.5) | collective-permute-done | bytes 98336 | tf_op jit(solution)/shard_map/cond/branch_1_fun/ppermute | solution.py:473
  203.0 3.9 %collective-permute-start.8 = (bf16[96,512]{1,0:T(8,128)(2,1)}, bf16[96,512]{1,0:T(8,128)(2,1)S(1)}, u32[]{:S(2)}, u32[]{:S(2)}) collective-permute-start(bf16[96,512]{1,0:T(8,128)(2,1)} %branch_1_fun.12.refs_0_), channel_id=1, source_target_pairs={{0,16},{8,24},{16,0},{24,8},{1,17},{9,25},{17,1},{25,9},{2,18},{10... | collective-permute-start | bytes 294920 | tf_op jit(solution)/shard_map/cond/branch_1_fun/ppermute | solution.py:473
  206.9 2.4 collective-permute-done.9.refs_3_
  209.3 6.1 %collective-permute-done.8.refs_2_ = bf16[96,512]{1,0:T(8,128)(2,1)S(1)} collective-permute-done((bf16[96,512]{1,0:T(8,128)(2,1)}, bf16[96,512]{1,0:T(8,128)(2,1)S(1)}, u32[]{:S(2)}, u32[]{:S(2)}) %collective-permute-start.8) | collective-permute-done | bytes 98336 | tf_op jit(solution)/shard_map/cond/branch_1_fun/ppermute | solution.py:473
  216.3 2.3 branch_1_fun.13
  218.6 25.2 %all_to_all.27 = bf16[4,4,96,512]{3,2,1,0:T(8,128)(2,1)} all-to-all(bf16[4,4,96,512]{3,2,1,0:T(8,128)(2,1)} %branch_1_fun.13), channel_id=1, replica_groups=mesh['z'=4,'p'=4,'c'=2] {'p'}, dimensions={0} | all-to-all | bytes 3145728 | tf_op jit(solution)/shard_map/cond/branch_1_fun/all_to_all | solution.py:468
  247.5 10.9 %shard_map.374 = (f32[2048,512]{1,0:T(8,128)}, f32[512,2048]{1,0:T(8,128)}, f32[512,1536]{1,0:T(8,128)}, f32[512,512]{1,0:T(8,128)}, f32[768,512]{1,0:T(8,128)},...) custom-call(s32[1]{0:T(128)} %bitcast.11.core, ...), custom_call_target="tpu_custom_call" | custom-call | tf_op jit(solution)/shard_map/pallas_call | solution.py:784
  (106 shorter events, 28.0 us)
Async XLA Ops:
  7.2 16.9 %copy-start = (f32[16,49]{1,0:T(8,128)S(1)}, f32[16,49]{1,0:T(8,128)}, u32[]{:S(2)}) copy-start(f32[16,49]{1,0:T(8,128)} %param.36) | copy-start | bytes 9412
  7.2 21.1 %copy-start.20 = (s32[16,1]{1,0:T(8,128)S(1)}, s32[16,1]{1,0:T(8,128)}, u32[]{:S(2)}) copy-start(s32[16,1]{1,0:T(8,128)} %constant.132) | copy-start | bytes 196
  7.2 27.9 %all-to-all-start.3 = ((bf16[32,16,768]{2,1,0:T(8,128)(2,1)}), bf16[32,16,768]{2,1,0:T(8,128)(2,1)S(1)}, u32[]{:S(2)}, u32[]{:S(2)}) async-start(bf16[32,16,768]{2,1,0:T(8,128)(2,1)} %bitcast.38), calls=%async_computation.3 | async-start | bytes 1572864 | tf_op jit(solution)/shard_map/all_to_all | solution.py:468
  14.5 233.0 %all-reduce.4.cloned.1.call-start = ((), (), s32[]{:S(2)}) async-start(), calls=%async_computation.4 | async-start | bytes 8388608 | tf_op jit(solution)/shard_map/psum | solution.py:657
  17.2 11.0 %collective-permute-start.12 = (bf16[32,512]{1,0:T(8,128)(2,1)S(1)}, bf16[32,512]{1,0:T(8,128)(2,1)S(1)}, u32[]{:S(2)}, u32[]{:S(2)}) collective-permute-start(bf16[32,512]{1,0:T(8,128)(2,1)S(1)} %pad_maximum_fusion), channel_id=1, source_target_pairs={{0,31},{1,0},{2,1},{3,2},{4,3},{5,4},{6,5},{7,6},{8,7},{9,8},{10,9... | collective-permute-start | bytes 98312 | tf_op jit(solution)/shard_map/ppermute | solution.py:564
  35.4 8.1 %collective-permute-start.11 = (bf16[16,768]{1,0:T(8,128)(2,1)S(1)}, bf16[16,768]{1,0:T(8,128)(2,1)S(1)}, u32[]{:S(2)}, u32[]{:S(2)}) collective-permute-start(bf16[16,768]{1,0:T(8,128)(2,1)S(1)} %convolution_convert_fusion.1), channel_id=1, source_target_pairs={{0,31},{1,0},{2,1},{3,2},{4,3},{5,4},{6,5},{7,6},{8,7},{9,8},{10,9... | collective-permute-start | bytes 73736 | tf_op jit(solution)/shard_map/ppermute | solution.py:609
  43.5 47.5 %copy-start.6 = (bf16[128,768]{1,0:T(8,128)(2,1)}, bf16[128,768]{1,0:T(8,128)(2,1)S(1)}, u32[]{:S(2)}) copy-start(bf16[128,768]{1,0:T(8,128)(2,1)S(1)} %pad.4.rim) | copy-start | bytes 589828
  132.4 3.6 %collective-permute-start = (bf16[1024,512]{1,0:T(8,128)(2,1)}, bf16[1024,512]{1,0:T(8,128)(2,1)S(1)}, u32[]{:S(2)}, u32[]{:S(2)}) collective-permute-start(bf16[1024,512]{1,0:T(8,128)(2,1)} %get-tuple-element.73), channel_id=1, source_target_pairs={{0,1},{1,0},{2,3},{3,2},{4,5},{5,4},{6,7},{7,6},{8,9},{9,8},{10,11... | collective-permute-start | bytes 3145736 | tf_op jit(solution)/shard_map/cond/branch_1_fun/ppermute | solution.py:464
  132.4 3.6 %collective-permute-start.1 = (bf16[512,512]{1,0:T(8,128)(2,1)}, bf16[512,512]{1,0:T(8,128)(2,1)S(1)}, u32[]{:S(2)}, u32[]{:S(2)}) collective-permute-start(bf16[512,512]{1,0:T(8,128)(2,1)} %get-tuple-element.75), channel_id=1, source_target_pairs={{0,1},{1,0},{2,3},{3,2},{4,5},{5,4},{6,7},{7,6},{8,9},{9,8},{10,11... | collective-permute-start | bytes 1572872 | tf_op jit(solution)/shard_map/cond/branch_1_fun/ppermute | solution.py:464
  141.1 25.4 %all-to-all-start = ((bf16[4,384,512]{2,1,0:T(8,128)(2,1)}), bf16[4,384,512]{2,1,0:T(8,128)(2,1)}, u32[]{:S(2)}, u32[]{:S(2)}) async-start(bf16[4,384,512]{2,1,0:T(8,128)(2,1)} %branch_1_fun.8.after), calls=%async_computation | async-start | bytes 3145728 | tf_op jit(solution)/shard_map/cond/branch_1_fun/all_to_all | solution.py:468
  146.2 22.8 %collective-permute-start.3 = (bf16[16,512]{1,0:T(8,128)(2,1)S(1)}, bf16[16,512]{1,0:T(8,128)(2,1)S(1)}, u32[]{:S(2)}, u32[]{:S(2)}) collective-permute-start(bf16[16,512]{1,0:T(8,128)(2,1)S(1)} %slice.14), channel_id=1, source_target_pairs={{0,1},{1,2},{2,3},{3,4},{4,5},{5,6},{6,7},{7,8},{8,9},{9,10},{10,1... | collective-permute-start | bytes 49160 | tf_op jit(solution)/shard_map/cond/branch_1_fun/ppermute | solution.py:721
  156.1 12.9 %collective-permute-start.2 = (bf16[16,512]{1,0:T(8,128)(2,1)}, bf16[16,512]{1,0:T(8,128)(2,1)S(1)}, u32[]{:S(2)}, u32[]{:S(2)}) collective-permute-start(bf16[16,512]{1,0:T(8,128)(2,1)} %get-tuple-element.77.refs_1_), channel_id=1, source_target_pairs={{0,1},{1,2},{2,3},{3,4},{4,5},{5,6},{6,7},{7,8},{8,9},{9,10},{10,1... | collective-permute-start | bytes 49160 | tf_op jit(solution)/shard_map/cond/branch_1_fun/ppermute | solution.py:739
  171.8 43.6 %all-to-all-start.1 = ((bf16[32,16,512]{2,1,0:T(8,128)(2,1)}), bf16[32,16,512]{2,1,0:T(8,128)(2,1)S(1)}, u32[]{:S(2)}, u32[]{:S(2)}) async-start(bf16[32,16,512]{2,1,0:T(8,128)(2,1)} %bitcast.35), calls=%async_computation.1 | async-start | bytes 1048576 | tf_op jit(solution)/shard_map/cond/branch_1_fun/all_to_all | solution.py:468
  174.4 13.1 %collective-permute-start.4 = (bf16[96,512]{1,0:T(8,128)(2,1)S(1)}, bf16[96,512]{1,0:T(8,128)(2,1)S(1)}, u32[]{:S(2)}, u32[]{:S(2)}) collective-permute-start(bf16[96,512]{1,0:T(8,128)(2,1)S(1)} %copy-done.26), channel_id=1, source_target_pairs={{0,8},{8,0},{16,24},{24,16},{1,9},{9,1},{17,25},{25,17},{2,10},{10... | collective-permute-start | bytes 294920 | tf_op jit(solution)/shard_map/cond/branch_1_fun/ppermute | solution.py:473
  176.2 22.9 %collective-permute-start.5 = (bf16[96,512]{1,0:T(8,128)(2,1)S(1)}, bf16[96,512]{1,0:T(8,128)(2,1)S(1)}, u32[]{:S(2)}, u32[]{:S(2)}) collective-permute-start(bf16[96,512]{1,0:T(8,128)(2,1)S(1)} %copy-done.25), channel_id=1, source_target_pairs={{0,16},{8,24},{16,0},{24,8},{1,17},{9,25},{17,1},{25,9},{2,18},{10... | collective-permute-start | bytes 294920 | tf_op jit(solution)/shard_map/cond/branch_1_fun/ppermute | solution.py:473
  178.7 20.4 %collective-permute-start.6 = (bf16[96,512]{1,0:T(8,128)(2,1)S(1)}, bf16[96,512]{1,0:T(8,128)(2,1)S(1)}, u32[]{:S(2)}, u32[]{:S(2)}) collective-permute-start(bf16[96,512]{1,0:T(8,128)(2,1)S(1)} %copy-done.24), channel_id=1, source_target_pairs={{0,24},{8,16},{16,8},{24,0},{1,25},{9,17},{17,9},{25,1},{2,26},{10... | collective-permute-start | bytes 294920 | tf_op jit(solution)/shard_map/cond/branch_1_fun/ppermute | solution.py:473
  187.5 11.6 %copy-start.14 = (bf16[96,512]{1,0:T(8,128)(2,1)}, bf16[96,512]{1,0:T(8,128)(2,1)S(1)}, u32[]{:S(2)}) copy-start(bf16[96,512]{1,0:T(8,128)(2,1)S(1)} %collective-permute-done.4.refs_1_) | copy-start | bytes 294916 | tf_op jit(solution)/shard_map/cond
  202.1 7.2 %collective-permute-start.9 = (bf16[96,512]{1,0:T(8,128)(2,1)}, bf16[96,512]{1,0:T(8,128)(2,1)S(1)}, u32[]{:S(2)}, u32[]{:S(2)}) collective-permute-start(bf16[96,512]{1,0:T(8,128)(2,1)} %branch_1_fun.12.refs_0_), channel_id=1, source_target_pairs={{0,24},{8,16},{16,8},{24,0},{1,25},{9,17},{17,9},{25,1},{2,26},{10... | collective-permute-start | bytes 294920 | tf_op jit(solution)/shard_map/cond/branch_1_fun/ppermute | solution.py:473
  203.0 12.4 %collective-permute-start.8 = (bf16[96,512]{1,0:T(8,128)(2,1)}, bf16[96,512]{1,0:T(8,128)(2,1)S(1)}, u32[]{:S(2)}, u32[]{:S(2)}) collective-permute-start(bf16[96,512]{1,0:T(8,128)(2,1)} %branch_1_fun.12.refs_0_), channel_id=1, source_target_pairs={{0,16},{8,24},{16,0},{24,8},{1,17},{9,25},{17,1},{25,9},{2,18},{10... | collective-permute-start | bytes 294920 | tf_op jit(solution)/shard_map/cond/branch_1_fun/ppermute | solution.py:473
  206.9 8.5 %collective-permute-start.7 = (bf16[96,512]{1,0:T(8,128)(2,1)}, bf16[96,512]{1,0:T(8,128)(2,1)S(1)}, u32[]{:S(2)}, u32[]{:S(2)}) collective-permute-start(bf16[96,512]{1,0:T(8,128)(2,1)} %branch_1_fun.12.refs_0_), channel_id=1, source_target_pairs={{0,8},{8,0},{16,24},{24,16},{1,9},{9,1},{17,25},{25,17},{2,10},{10... | collective-permute-start | bytes 294920 | tf_op jit(solution)/shard_map/cond/branch_1_fun/ppermute | solution.py:473
  218.6 25.2 %copy-start.18 = (bf16[16,512]{1,0:T(8,128)(2,1)S(1)}, bf16[16,512]{1,0:T(8,128)(2,1)}, u32[]{:S(2)}) copy-start(bf16[16,512]{1,0:T(8,128)(2,1)} %copy-done.17) | copy-start | bytes 49156 | tf_op jit(solution)/shard_map/cond
  218.6 25.8 %copy-start.5 = (bf16[32,16,512]{2,1,0:T(8,128)(2,1)S(1)}, bf16[32,16,512]{2,1,0:T(8,128)(2,1)}, u32[]{:S(2)}) copy-start(bf16[32,16,512]{2,1,0:T(8,128)(2,1)} %copy-done.4) | copy-start | bytes 1572868 | tf_op jit(solution)/shard_map/cond
  218.6 25.8 %copy-start.8 = (bf16[768,512]{1,0:T(8,128)(2,1)S(1)}, bf16[768,512]{1,0:T(8,128)(2,1)}, u32[]{:S(2)}) copy-start(bf16[768,512]{1,0:T(8,128)(2,1)} %get-tuple-element.82) | copy-start | bytes 2359300 | tf_op jit(solution)/shard_map/cond
  243.8 3.8 %collective-permute-start.10 = (bf16[4,384,512]{2,1,0:T(8,128)(2,1)}, bf16[4,384,512]{2,1,0:T(8,128)(2,1)}, u32[]{:S(2)}, u32[]{:S(2)}) collective-permute-start(bf16[4,384,512]{2,1,0:T(8,128)(2,1)} %bitcast.10), channel_id=1, source_target_pairs={{0,1},{1,0},{2,3},{3,2},{4,5},{5,4},{6,7},{7,6},{8,9},{9,8},{10,11... | collective-permute-start | bytes 4718600 | tf_op jit(solution)/shard_map/cond/branch_1_fun/ppermute | solution.py:464
  (20 other events, 88.7 us)
Sparse Core Ops, SparseCore 0:
  91.1 149.7 all-reduce.3
